TPU v7x, 256 devices: a whole 4x4x8 slice. The times are simulated.
256 devices in a mesh: enc: 32 (over z, x), tp: 8 (over y, core), rep: 1.
Axes of the slice: x: 4, y: 4, z: 8, core: 2. Of those that a mesh axis runs over, the one named last changes fastest.
Arguments:
- patches: bfloat16 [128, 64, 5120], P(('rep', 'enc')), may hold values from -6 to 6
- slot_page: int32 [128], P('rep'), may hold values from -1 to 63, as said below
- page_start: int32 [64], P('rep'), may hold values from 0 to 8128, as said below
- patch_gain: float32 [1280], replicated, may hold values from 0.25 to 1.75
- patch_bias: float32 [1280], replicated, may hold values from -3 to 3
- merge_in: bfloat16 [5120, 5120], P(None, 'tp'), may hold values from -0.078125 to 0.078125
- merge_out: bfloat16 [5120, 8192], P('tp', 'enc'), may hold values from -0.078125 to 0.078125
- text: bfloat16 [8192, 8192], P(('rep', 'enc'), 'tp'), may hold values from -6 to 6
- norm_gain: float32 [8192], P('tp'), may hold values from 0.25 to 1.75
- kv_weight: bfloat16 [8192, 2048], P('tp', 'enc'), may hold values from -0.0625 to 0.0625
Outputs:
- keys_out: bfloat16 [8192, 1024], P(('rep', 'enc'), 'tp')
- values_out: bfloat16 [8192, 1024], P(('rep', 'enc'), 'tp')
Inputs may be any that keep to these rules, and one draw needn't show every extreme that they name: `slot_page`: every page 0 to 63 is held in exactly one slot; slots i * 4 to (i + 1) * 4 - 1 form device i of enc, and the most live pages of one device is exactly 4. `page_start`: page k lies whole inside the block of 256 tokens number k // 2; pages do not intersect.
All inputs are finite; a program needn't handle non-finite values.
Results may differ from a plain program's by a relative error of at most 0.024.
Values may be sent and summed in bfloat16 or wider, within the bound.
No kernel may reach another device: no remote copies, remote signals or barrier semaphores. Data moves between devices by JAX's collectives and lax.ppermute only.
A program may use at most 128 MiB of HBM per device.

v0:
```python
import jax
import jax.numpy as jnp
from jax import lax
from jax.sharding import PartitionSpec as P

D = 8192
HEAD = 128


EPS = 1e-06
THETA = 1000000.0


def patch_norm(flat_rows, patch_gain, patch_bias):
    shaped = flat_rows.astype(jnp.float32).reshape(flat_rows.shape[0], -1, patch_gain.shape[0])
    center = jnp.mean(shaped, axis=-1, keepdims=True)
    spread = jnp.mean(jnp.square(shaped - center), axis=-1, keepdims=True)
    normed = (shaped - center) * lax.rsqrt(spread + EPS) * patch_gain + patch_bias
    return normed.reshape(flat_rows.shape).astype(jnp.bfloat16)


def rotate_keys(key_heads, positions):
    half_size = key_heads.shape[-1] // 2
    frequency = THETA ** (-jnp.arange(half_size, dtype=jnp.float32) * 2.0 / key_heads.shape[-1])
    angles = positions[:, None, None] * frequency
    lower_half = key_heads[..., :half_size]
    upper_half = key_heads[..., half_size:]
    return jnp.concatenate(
        [
            lower_half * jnp.cos(angles) - upper_half * jnp.sin(angles),
            upper_half * jnp.cos(angles) + lower_half * jnp.sin(angles),
        ],
        axis=-1,
    )


def body(
    patches,
    slot_page,
    page_start,
    patch_gain,
    patch_bias,
    merge_in,
    merge_out,
    text,
    norm_gain,
    kv_weight,
):
    enc_count = lax.axis_size("enc")
    enc_index = lax.axis_index("enc")
    slot_count = patches.shape[0]
    page_rows = patches.shape[1]
    feature = patches.shape[2]
    span_rows = text.shape[0]
    column_share = text.shape[1]
    per_shard = page_start.shape[0] // enc_count
    owned_ids = enc_index * per_shard + jnp.arange(per_shard, dtype=jnp.int32)
    normed_rows = patch_norm(
        patches.reshape(slot_count * page_rows, feature), patch_gain, patch_bias
    )
    hidden = jax.nn.gelu(
        jnp.dot(normed_rows, merge_in, preferred_element_type=jnp.float32), approximate=False
    ).astype(jnp.bfloat16)
    partial_terms = jnp.dot(
        hidden,
        lax.all_gather(merge_out, "enc", axis=1, tiled=True),
        preferred_element_type=jnp.float32,
    )
    merged = lax.psum_scatter(
        partial_terms.astype(jnp.bfloat16), "tp", scatter_dimension=1, tiled=True
    )
    merged = merged.reshape(slot_count, page_rows * column_share)
    picker = (slot_page[None, :] == owned_ids[:, None]).astype(jnp.bfloat16)
    collected = jnp.dot(
        picker,
        lax.all_gather(merged, "enc", axis=0, tiled=True),
        preferred_element_type=jnp.float32,
    )
    visual = collected.astype(jnp.bfloat16).reshape(per_shard * page_rows, column_share)
    starts = (
        lax.dynamic_slice_in_dim(page_start, enc_index * per_shard, per_shard)
        - enc_index * span_rows
    )
    column = jnp.arange(per_shard * page_rows, dtype=jnp.int32)
    owner_page = (column // page_rows)[:, None] == jnp.arange(per_shard, dtype=jnp.int32)[None, :]
    target_row = jnp.sum(jnp.where(owner_page, starts[None, :], 0), axis=1) + column % page_rows
    placing = jnp.arange(span_rows, dtype=jnp.int32)[:, None] == target_row[None, :]
    covered = jnp.any(placing, axis=1)
    inserted = jnp.dot(
        placing.astype(jnp.bfloat16), visual, preferred_element_type=jnp.float32
    ).astype(jnp.bfloat16)
    assembled = jnp.where(covered[:, None], inserted, text)
    square_part = jnp.sum(jnp.square(assembled.astype(jnp.float32)), axis=1)
    mean_square = lax.psum(square_part, "tp") / D
    normed = (
        assembled.astype(jnp.float32) * lax.rsqrt(mean_square + EPS)[:, None] * norm_gain
    ).astype(jnp.bfloat16)
    kv_terms = jnp.dot(
        normed,
        lax.all_gather(kv_weight, "enc", axis=1, tiled=True),
        preferred_element_type=jnp.float32,
    )
    kv_local = (
        lax.psum_scatter(kv_terms.astype(jnp.bfloat16), "tp", scatter_dimension=1, tiled=True)
        .astype(jnp.float32)
        .reshape(span_rows, -1, 2, HEAD)
    )
    positions = (enc_index * span_rows + jnp.arange(span_rows, dtype=jnp.int32)).astype(jnp.float32)
    rotated = rotate_keys(kv_local[:, :, 0], positions)
    keys_out = rotated.reshape(span_rows, -1).astype(jnp.bfloat16)
    values_out = kv_local[:, :, 1].reshape(span_rows, -1).astype(jnp.bfloat16)
    return (keys_out, values_out)


def solution(mesh):
    return jax.shard_map(
        body,
        mesh=mesh,
        in_specs=(
            P(("rep", "enc"), None, None),
            P("rep"),
            P("rep"),
            P(),
            P(),
            P(None, "tp"),
            P("tp", "enc"),
            P(("rep", "enc"), "tp"),
            P("tp"),
            P("tp", "enc"),
        ),
        out_specs=(P(("rep", "enc"), "tp"), P(("rep", "enc"), "tp")),
        check_vma=False,
    )
```

profile of v0, /device:TPU:1, one launch (start us, length us, event | category | flops | bytes accessed | tf_op | source)
XLA Modules:
  0.0 450.8 jit_solution(16423397433892386626)
XLA Ops:
  7.2 0.7 all-gather.5.cloned.1.call-update
  7.9 6.3 %reshape.185 = f32[256,4,1280]{2,1,0:T(4,128)} reshape(bf16[4,64,5120]{2,1,0:T(8,128)(2,1)} %param.10) | data formatting | bytes 7864320 | tf_op jit(solution)/shard_map/convert_element_type | solution.py:15
  14.3 3.3 reduce_sum.37
  17.6 4.0 multiply_reduce_fusion
  21.6 0.7 mul.105
  22.3 3.3 copy.22
  25.6 0.7 sub.35
  26.4 3.2 copy.21
  29.7 6.9 %fusion.3 = bf16[256,5120]{1,0:T(8,128)(2,1)} fusion(f32[256,5120]{1,0:T(8,128)} %bitcast.30, f32[256,5120]{1,0:T(8,128)} %bitcast.31, f32[5120]{0:T(1024)S(1)} %add.92, f32[5120]{0:T(1024)S(1)} %mul.109, bf16[4,64,5120]{2,1,0:T(8,128)(2,1)S(1)} %copy-done), kind=kLoop, calls=%fused_computation.6 | loop fusion | flops 7864320 | bytes 15769600 | tf_op jit(solution)/shard_map/convert_element_type | solution.py:19
  36.6 90.5 %all-gather.5.cloned.1.call-done = bf16[640,8192]{1,0:T(8,128)(2,1)} async-done(((bf16[640,256]{1,0:T(8,128)(2,1)}), bf16[640,8192]{1,0:T(8,128)(2,1)}) %all-gather.5.cloned.1.call-update) | async-done | bytes 10485776 | tf_op jit(solution)/shard_map/all_gather | solution.py:66
  127.1 16.9 %convolution_convert_fusion.1 = bf16[256,8192]{1,0:T(8,128)(2,1)} fusion(bf16[640,8192]{1,0:T(8,128)(2,1)} %all-gather.5.cloned.1.call-done, bf16[256,5120]{1,0:T(8,128)(2,1)} %fusion.3, bf16[5120,640]{1,0:T(8,128)(2,1)} %param.15), kind=kOutput, calls=%fused_computation.1 | convolution fusion | flops 4374822912 | bytes 23855104 | tf_op jit(solution)/shard_map/dot_general | solution.py:64
  144.0 37.0 %reduce-scatter.3.cloned.1.call-done = bf16[256,1024]{1,0:T(8,128)(2,1)} async-done(((bf16[256,8192]{1,0:T(8,128)(2,1)}), bf16[256,1024]{1,0:T(8,128)(2,1)}) %reduce-scatter.3.cloned.1.call-update) | async-done | bytes 524304 | tf_op jit(solution)/shard_map/reduce_scatter | solution.py:69
  181.0 2.2 reshape.187
  183.3 0.5 all-gather.7.cloned.1.call-update
  184.3 141.3 %all-gather.9.cloned.1.call-done = bf16[32,4,65536]{2,1,0:T(4,128)(2,1)} async-done(((bf16[1,4,65536]{2,1,0:T(4,128)(2,1)}), bf16[32,4,65536]{2,1,0:T(4,128)(2,1)}) %all-gather.9.cloned.1.call-update) | async-done | bytes 16777232 | tf_op jit(solution)/shard_map/all_gather | solution.py:76
  325.5 18.8 %reshape.188 = bf16[128,65536]{1,0:T(8,128)(2,1)} reshape(bf16[32,4,65536]{2,1,0:T(4,128)(2,1)} %all-gather.9.cloned.1.call-done) | data formatting | bytes 33554432
  344.4 8.2 %convolution_convert_fusion = bf16[2,65536]{1,0:T(2,128)(2,1)S(1)} fusion(bf16[128,65536]{1,0:T(8,128)(2,1)} %reshape.188, s32[128]{0:T(128)S(1)} %copy-done.3, s32[2]{0:T(128)S(1)} %iota_add_fusion), kind=kOutput, calls=%fused_computation | convolution fusion | flops 33685760 | bytes 17039880 | tf_op jit(solution)/shard_map/dot_general | solution.py:74
  353.2 12.8 %psum.7 = f32[256]{0:T(256)S(1)} all-reduce(f32[256]{0:T(256)S(1)} %get-tuple-element.8), channel_id=1, replica_groups=mesh['enc'=32,'tp'=8,'rep'=1] {'tp'}, use_global_device_ids=true, to_apply=%region_6.7 | all-reduce | flops 256 | bytes 2048 | tf_op jit(solution)/shard_map/psum | solution.py:94
  366.0 38.6 %all-gather.7.cloned.1.call-done = bf16[1024,2048]{0,1:T(8,128)(2,1)} async-done(((bf16[1024,64]{0,1:T(8,128)(2,1)}), bf16[1024,2048]{0,1:T(8,128)(2,1)}) %all-gather.7.cloned.1.call-update) | async-done | bytes 4194320 | tf_op jit(solution)/shard_map/all_gather | solution.py:100
  404.6 4.5 convolution_convert_fusion.2
  409.2 32.2 %reduce-scatter.5.cloned.1.call-done = bf16[256,256]{1,0:T(8,128)(2,1)} async-done(((bf16[256,2048]{1,0:T(8,128)(2,1)}), bf16[256,256]{1,0:T(8,128)(2,1)}) %reduce-scatter.5.cloned.1.call-update) | async-done | bytes 131088 | tf_op jit(solution)/shard_map/reduce_scatter | solution.py:104
  441.4 1.0 copy.18
  442.8 0.7 copy.19
  443.5 0.7 copy.20
  (42 shorter events, 1.6 us)
Async XLA Ops:
  7.2 119.9 %all-gather.5.cloned.1.call-start = ((), (), s32[]{:S(2)}) async-start(), calls=%async_computation.2 | async-start | bytes 10813440 | tf_op jit(solution)/shard_map/all_gather | solution.py:66
  7.9 173.2 %reduce-scatter.3.cloned.1.call-start = ((), (), s32[]{:S(2)}) async-start(), calls=%async_computation.3 | async-start | bytes 4718592 | tf_op jit(solution)/shard_map/reduce_scatter | solution.py:69
  26.4 3.2 copy-start.1
  26.4 3.2 copy-start.2
  26.4 3.2 copy-start
  144.0 40.0 %copy-start.4 = (s32[64]{0:T(128)S(1)}, s32[64]{0:T(128)}, u32[]{:S(2)}) copy-start(s32[64]{0:T(128)} %param.12) | copy-start | bytes 772
  144.0 181.6 %all-gather.9.cloned.1.call-start = ((), (), s32[]{:S(2)}) async-start(), calls=%async_computation.6 | async-start | bytes 17301504 | tf_op jit(solution)/shard_map/all_gather | solution.py:76
  183.3 221.3 %all-gather.7.cloned.1.call-start = ((), (), s32[]{:S(2)}) async-start(), calls=%async_computation.4 | async-start | bytes 4325376 | tf_op jit(solution)/shard_map/all_gather | solution.py:100
  183.9 257.5 %reduce-scatter.5.cloned.1.call-start = ((), (), s32[]{:S(2)}) async-start(), calls=%async_computation.5 | async-start | bytes 1179648 | tf_op jit(solution)/shard_map/reduce_scatter | solution.py:104
  184.2 160.1 %copy-start.3 = (s32[128]{0:T(128)S(1)}, s32[128]{0:T(128)}, u32[]{:S(2)}) copy-start(s32[128]{0:T(128)} %param.11) | copy-start | bytes 1540
  344.3 8.4 %copy-start.5 = (bf16[256,1024]{1,0:T(8,128)(2,1)S(1)}, bf16[256,1024]{1,0:T(8,128)(2,1)}, u32[]{:S(2)}) copy-start(bf16[256,1024]{1,0:T(8,128)(2,1)} %param.17) | copy-start | bytes 1572868
  344.4 60.3 %copy-start.6 = (f32[1024]{0:T(1024)S(1)}, f32[1024]{0:T(1024)}, u32[]{:S(2)}) copy-start(f32[1024]{0:T(1024)} %param.18) | copy-start | bytes 12292
Sparse Core Ops, SparseCore 0:
  10.5 116.5 all-gather.4
  144.1 36.8 reduce-scatter.2
  183.6 141.8 all-gather.8
  328.0 76.6 all-gather.6
  409.3 32.0 reduce-scatter.4
where the time goes:
time: 453 us; the launch traced here: 451 us
  waiting for transfers between devices  341 us (75%)
  local copies, waits for them, and re-layouts  38.1 us (8%)
  matrix products  30 us (7%)
  other arithmetic  14.9 us (3%)
  between operations  14 us (3%)
  blocking collectives  12.8 us (3%)
    all_gather x1, waiting for transfers between devices, body(): lax.all_gather(merged, 'enc', axis=0, tiled=True)  141 us
    all_gather x1, waiting for transfers between devices, body(): lax.all_gather(merge_out, 'enc', axis=1, tiled=True)  90.5 us
    all_gather x1, waiting for transfers between devices, body(): lax.all_gather(kv_weight, 'enc', axis=1, tiled=True)  38.6 us
    reduce_scatter x1, waiting for transfers between devices, body(): lax.psum_scatter(partial_terms.astype(jnp.bfloat16), 'tp', scatter_dimens...  37 us
    reduce_scatter x1, waiting for transfers between devices, body(): lax.psum_scatter(kv_terms.astype(jnp.bfloat16), 'tp', scatter_dimension=1...  32.2 us
    unnamed x20, local copies, waits for them, and re-layouts  29 us
    dot_general x1, matrix products, body(): jnp.dot(hidden, lax.all_gather(merge_out, 'enc', axis=1, tiled=True), pre...  16.9 us
    psum x1, blocking collectives, body(): mean_square = lax.psum(square_part, 'tp') / D  12.8 us
  transfers between devices with their start and end apart: 5, of which 5 were waited for; matrix products, arithmetic and copies ran while one was open for 13% of the time, Pallas kernels for 0%

commit v1 on v0

v1 whole, which is shorter than its diff:
```python
import functools

import jax
import jax.numpy as jnp
from jax import lax
from jax.experimental import pallas as pl
from jax.experimental.pallas import tpu as pltpu
from jax.sharding import PartitionSpec as P

EPS = 1e-06
THETA = 1000000.0
NZ, NX, NY, NC = 8, 4, 4, 2
VMEM_LIMIT = 40 * 1024 * 1024
BF = jnp.bfloat16
F32 = jnp.float32

GROUPS_Z = [[z * NX + x for z in range(NZ)] for x in range(NX)]


def shift_x(d):
    return [(z * NX + x, z * NX + (x + d) % NX) for z in range(NZ) for x in range(NX)]


def shift_y(d):
    return [(y * NC + c, (y + d) % NY * NC + c) for y in range(NY) for c in range(NC)]


SWAP_CORE = [(t, t ^ 1) for t in range(NY * NC)]


def hidden_kernel(slots, patch_ref, gain_ref, bias_ref, weight_ref, out_ref, acc_ref):
    step = pl.program_id(0)
    part = patch_ref[...].astype(F32)
    center = jnp.mean(part, axis=-1, keepdims=True)
    part = part - center
    spread = jnp.mean(part * part, axis=-1, keepdims=True)
    normed = part * lax.rsqrt(spread + EPS) * gain_ref[...] + bias_ref[...]
    term = jnp.dot(normed.astype(BF), weight_ref[...], preferred_element_type=F32)

    @pl.when(step == 0)
    def _():
        acc_ref[...] = term

    @pl.when(step > 0)
    def _():
        acc_ref[...] += term

    @pl.when(step == pl.num_programs(0) - 1)
    def _():
        total = acc_ref[...]
        total = 0.5 * total * (1.0 + lax.erf(total * 0.7071067811865476))
        rows = total.shape[0] // slots
        chunk = rows // NZ
        pieces = [
            total[slot * rows + z * chunk : slot * rows + (z + 1) * chunk]
            for z in range(NZ)
            for slot in range(slots)
        ]
        out_ref[...] = jnp.concatenate(pieces, axis=0).astype(BF)


def hidden_rows(patches, patch_gain, patch_bias, merge_in):
    slots, rows, feature = patches.shape
    width = patch_gain.shape[0]
    flat = patches.reshape(slots * rows, feature)
    out_width = merge_in.shape[1]
    return pl.pallas_call(
        functools.partial(hidden_kernel, slots),
        grid=(feature // width,),
        in_specs=[
            pl.BlockSpec((slots * rows, width), lambda i: (0, i)),
            pl.BlockSpec((1, width), lambda i: (0, 0)),
            pl.BlockSpec((1, width), lambda i: (0, 0)),
            pl.BlockSpec((width, out_width), lambda i: (i, 0)),
        ],
        out_specs=pl.BlockSpec((slots * rows, out_width), lambda i: (0, 0)),
        out_shape=jax.ShapeDtypeStruct((slots * rows, out_width), BF),
        scratch_shapes=[pltpu.VMEM((slots * rows, out_width), F32)],
        compiler_params=pltpu.CompilerParams(vmem_limit_bytes=VMEM_LIMIT),
        cost_estimate=pl.CostEstimate(
            flops=2 * slots * rows * feature * out_width,
            bytes_accessed=2 * feature * (out_width + slots * rows),
            transcendentals=0,
        ),
    )(flat, patch_gain[None], patch_bias[None], merge_in)


def send_kernel(order_ref, target_ref, a, b, c, d, weight_ref, live_ref, out_ref):
    step = pl.program_id(0)

    @pl.when(step == 0)
    def _():
        target = target_ref[...]
        total = None
        for index, piece in enumerate((a, b, c, d)):
            rows = piece.shape[0]
            place = lax.broadcasted_iota(jnp.int32, (target.shape[0], rows), 1) + index * rows
            pick = jnp.where(place == target, 1.0, 0.0).astype(BF)
            term = jnp.dot(pick, piece[...], preferred_element_type=F32)
            total = term if total is None else total + term
        live_ref[...] = total.astype(BF)

    out_ref[0] = jnp.dot(live_ref[...], weight_ref[0], preferred_element_type=F32).astype(BF)


def send_parts(order, target, pieces, weights):
    rows, depth = target.shape[0], pieces[0].shape[1]
    width = weights.shape[2]
    whole = pl.BlockSpec(pieces[0].shape, lambda i, order: (0, 0))
    return pl.pallas_call(
        send_kernel,
        grid_spec=pltpu.PrefetchScalarGridSpec(
            num_scalar_prefetch=1,
            grid=(NY,),
            in_specs=[pl.BlockSpec((rows, 1), lambda i, order: (0, 0))]
            + [whole] * 4
            + [pl.BlockSpec((1, depth, width), lambda i, order: (order[i], 0, 0))],
            out_specs=[
                pl.BlockSpec((rows, depth), lambda i, order: (0, 0)),
                pl.BlockSpec((1, rows, width), lambda i, order: (i, 0, 0)),
            ],
        ),
        out_shape=[
            jax.ShapeDtypeStruct((rows, depth), BF),
            jax.ShapeDtypeStruct((NY, rows, width), BF),
        ],
        compiler_params=pltpu.CompilerParams(vmem_limit_bytes=VMEM_LIMIT),
        cost_estimate=pl.CostEstimate(
            flops=2 * rows * depth * (width * NY + 2 * rows),
            bytes_accessed=2 * (depth * width * NY + rows * width * NY),
            transcendentals=0,
        ),
    )(order, target, *pieces, weights)


def keep_kernel(order_ref, live_ref, weight_ref, got_ref, *out_refs):
    step = pl.program_id(0)
    own = jnp.dot(live_ref[...], weight_ref[0], preferred_element_type=F32).astype(BF)
    total = (own.astype(F32) + got_ref[0].astype(F32)).astype(BF)
    for index, out_ref in enumerate(out_refs):

        @pl.when(step == index)
        def _(out_ref=out_ref):
            out_ref[...] = total


def keep_parts(order, live, weights, got):
    rows, depth = live.shape
    width = weights.shape[2]
    return pl.pallas_call(
        keep_kernel,
        grid_spec=pltpu.PrefetchScalarGridSpec(
            num_scalar_prefetch=1,
            grid=(NY,),
            in_specs=[
                pl.BlockSpec((rows, depth), lambda i, order: (0, 0)),
                pl.BlockSpec((1, depth, width), lambda i, order: (order[i], 0, 0)),
                pl.BlockSpec((1, rows, width), lambda i, order: (i, 0, 0)),
            ],
            out_specs=[pl.BlockSpec((rows, width), lambda i, order: (0, 0))] * NY,
        ),
        out_shape=[jax.ShapeDtypeStruct((rows, width), BF)] * NY,
        compiler_params=pltpu.CompilerParams(vmem_limit_bytes=VMEM_LIMIT),
        cost_estimate=pl.CostEstimate(
            flops=2 * rows * depth * width * NY,
            bytes_accessed=2 * (depth * width * NY + 2 * rows * width * NY),
            transcendentals=0,
        ),
    )(order, live, weights, got)


def project_kernel(target_ref, moved_ref, text_ref, weight_ref, out_ref, rows_ref, squares_ref):
    step = pl.program_id(0)
    span = text_ref.shape[0]

    @pl.when(step == 0)
    def _():
        target = target_ref[...]
        place = lax.broadcasted_iota(jnp.int32, (span, target.shape[1]), 0) == target
        pick = jnp.where(place, 1.0, 0.0)
        covered = jnp.sum(pick, axis=1, keepdims=True) > 0.5
        pick = pick.astype(BF)
        width = moved_ref.shape[2]
        ones = jnp.ones((16, width), BF)
        contract = (((1,), (1,)), ((), ()))
        squares = jnp.zeros((16, span), F32)
        for x in range(NX):
            stacked = jnp.concatenate([moved_ref[z * NX + x] for z in range(NZ)], axis=0)
            put = jnp.dot(pick, stacked, preferred_element_type=F32)
            columns = slice(x * width, (x + 1) * width)
            mixed = jnp.where(covered, put, text_ref[:, columns].astype(F32))
            rows_ref[:, columns] = mixed.astype(BF)
            square = mixed * mixed
            high = square.astype(BF)
            low = (square - high.astype(F32)).astype(BF)
            for term in (high, low):
                squares += lax.dot_general(ones, term, contract, preferred_element_type=F32)
        high = squares.astype(BF).astype(F32)
        line = lax.broadcasted_iota(jnp.int32, squares.shape, 0)
        squares_ref[...] = jnp.where(
            line == 0, high, jnp.where(line == 1, squares - high, 0.0)
        ).astype(BF)

    out_ref[0, :span] = jnp.dot(
        rows_ref[...], weight_ref[0], preferred_element_type=F32
    ).astype(BF)
    out_ref[0, span:] = squares_ref[...]


def project(target, moved, text, weights):
    span, features = text.shape
    heads, _, width = weights.shape
    return pl.pallas_call(
        project_kernel,
        grid=(heads,),
        in_specs=[
            pl.BlockSpec(target.shape, lambda i: (0, 0)),
            pl.BlockSpec(moved.shape, lambda i: (0, 0, 0)),
            pl.BlockSpec(text.shape, lambda i: (0, 0)),
            pl.BlockSpec((1, features, width), lambda i: (i, 0, 0)),
        ],
        out_specs=pl.BlockSpec((1, span + 16, width), lambda i: (i, 0, 0)),
        out_shape=jax.ShapeDtypeStruct((heads, span + 16, width), BF),
        scratch_shapes=[pltpu.VMEM((span, features), BF), pltpu.VMEM((16, span), BF)],
        compiler_params=pltpu.CompilerParams(vmem_limit_bytes=VMEM_LIMIT),
        cost_estimate=pl.CostEstimate(
            flops=2 * span * features * (width * heads + 2 * span),
            bytes_accessed=2 * heads * width * (features + span),
            transcendentals=0,
        ),
    )(target, moved, text, weights)


def finish_kernel(features, parts_ref, cos_ref, sin_ref, keys_ref, values_ref):
    span = keys_ref.shape[0]
    head = keys_ref.shape[1]
    total = parts_ref[0].astype(F32)
    for index in range(1, parts_ref.shape[0]):
        total = total + parts_ref[index].astype(F32)
    squares = total[span : span + 1] + total[span + 1 : span + 2]
    diagonal = lax.broadcasted_iota(jnp.int32, (span, span), 0) == lax.broadcasted_iota(
        jnp.int32, (span, span), 1
    )
    squares = jnp.sum(jnp.where(diagonal, squares, 0.0), axis=1, keepdims=True)
    scale = lax.rsqrt(squares / features + EPS)
    key = total[:span, :head] * scale
    turned = pltpu.roll(key, head // 2, 1)
    keys_ref[...] = (key * cos_ref[...] + turned * sin_ref[...]).astype(BF)
    values_ref[...] = (total[:span, head:] * scale).astype(BF)


def finish(features, parts, cos, sin):
    span, head = cos.shape
    return pl.pallas_call(
        functools.partial(finish_kernel, features),
        out_shape=[jax.ShapeDtypeStruct((span, head), BF)] * 2,
        compiler_params=pltpu.CompilerParams(vmem_limit_bytes=VMEM_LIMIT),
    )(parts, cos, sin)


def rotary(positions, head):
    half = head // 2
    frequency = THETA ** (-jnp.arange(half, dtype=F32) * 2.0 / head)
    angles = positions[:, None] * frequency
    cos, sin = jnp.cos(angles), jnp.sin(angles)
    return jnp.concatenate([cos, cos], axis=1), jnp.concatenate([-sin, sin], axis=1)


def body(
    patches,
    slot_page,
    page_start,
    patch_gain,
    patch_bias,
    merge_in,
    merge_out,
    text,
    norm_gain,
    kv_weight,
):
    enc_index, tp_index = lax.axis_index("enc"), lax.axis_index("tp")
    x_index = enc_index % NX
    y_index, core = tp_index // NC, tp_index % NC
    slots, page_rows, _ = patches.shape
    pages = page_start.shape[0]
    span, features = text.shape
    chunk = page_rows // NZ
    half = features // 2

    weights = lax.all_gather(merge_out, "enc", axis_index_groups=GROUPS_Z)

    scaled = (kv_weight.astype(F32) * norm_gain[:, None]).astype(BF)
    packed = jnp.concatenate([scaled[:half], scaled[half:]], axis=1)
    quarter = kv_weight.shape[1]
    by_shift = [packed] + [lax.ppermute(packed, "enc", shift_x(d)) for d in range(1, NX)]
    by_x = jnp.stack(by_shift)[(x_index - jnp.arange(NX)) % NX]
    head_weight = by_x.reshape(NX, half, 2, quarter).transpose(2, 1, 0, 3)
    head_weight = head_weight.reshape(features, NX * quarter)
    kv_all = lax.all_gather(head_weight, "enc", axis_index_groups=GROUPS_Z)

    hidden = hidden_rows(patches, patch_gain, patch_bias, merge_in)
    dealt = lax.all_to_all(hidden, "enc", 0, 0, axis_index_groups=GROUPS_Z, tiled=True)
    pieces = [dealt] + [lax.ppermute(dealt, "enc", shift_x(d)) for d in range(1, NX)]

    page_ids = jnp.arange(pages, dtype=jnp.int32)
    slot_ids = jnp.arange(slot_page.shape[0], dtype=jnp.int32)
    slot_of = jnp.sum(
        jnp.where(slot_page[None, :] == page_ids[:, None], slot_ids[None, :], 0), axis=1
    )
    holder = slot_of // slots
    place = (x_index - holder % NX) % NX * NZ + holder // NX
    place = (place * slots + slot_of % slots) * chunk
    target = (place[:, None] + jnp.arange(chunk, dtype=jnp.int32)[None, :]).reshape(-1, 1)

    shifted = (y_index + jnp.arange(NY, dtype=jnp.int32)) % NY * NC
    live, away = send_parts(shifted + (1 - core), target, pieces, weights)
    got = lax.ppermute(away, "tp", SWAP_CORE)
    parts = keep_parts(shifted + core, live, weights, got)
    total = parts[0].astype(F32)
    for d in range(1, NY):
        total = total + lax.ppermute(parts[d], "tp", shift_y(d)).astype(F32)
    merged = total.astype(BF)

    moved = lax.all_to_all(merged, "enc", 0, 0, tiled=True)
    per_block = pages // (NZ * NX)
    moved = moved.reshape(NZ * NX, per_block * chunk, merged.shape[1])
    starts = lax.dynamic_slice_in_dim(page_start, enc_index * per_block, per_block)
    starts = starts - enc_index * span
    rows = (
        jnp.arange(NZ, dtype=jnp.int32)[:, None, None] * chunk
        + starts[None, :, None]
        + jnp.arange(chunk, dtype=jnp.int32)[None, None, :]
    ).reshape(1, -1)
    kv_parts = project(rows, moved, text, kv_all)

    sent = kv_parts.reshape(-1, kv_parts.shape[2])
    gathered = lax.all_to_all(sent, "tp", 0, 0, tiled=True).reshape(kv_parts.shape)
    positions = (enc_index * span + jnp.arange(span, dtype=jnp.int32)).astype(F32)
    cos, sin = rotary(positions, kv_parts.shape[2] // 2)
    return tuple(finish(features * NY * NC, gathered, cos, sin))


def solution(mesh):
    return jax.shard_map(
        body,
        mesh=mesh,
        in_specs=(
            P(("rep", "enc"), None, None),
            P("rep"),
            P("rep"),
            P(),
            P(),
            P(None, "tp"),
            P("tp", "enc"),
            P(("rep", "enc"), "tp"),
            P("tp"),
            P("tp", "enc"),
        ),
        out_specs=(P(("rep", "enc"), "tp"), P(("rep", "enc"), "tp")),
        check_vma=False,
    )
```

time: 453 us -> 160 us (0.35)
  waiting for transfers between devices: 341 us -> 77.8 us
  starting transfers between devices: 0.2 us -> 34.2 us
  matrix products: 30 us -> 0 us
  local copies, waits for them, and re-layouts: 38.1 us -> 13.2 us
  Pallas kernels: 0 us -> 16.7 us
  blocking collectives: 12.8 us -> 0 us
  other arithmetic: 14.9 us -> 3.04 us
    all_gather x3 -> x2, waiting for transfers between devices: 270 us -> 2.08 us  [the longest x1 2.08 us: body(): kv_all = lax.all_gather(head_weight, 'enc', axis_index_groups=GROUPS_Z)]
    reduce_scatter x2 -> x0, waiting for transfers between devices: 69.2 us -> none  [the longest x1 37 us: body(): lax.psum_scatter(partial_terms.astype(jnp.bfloat16), 'tp', scatter_dimens...]
    all_to_all x0 -> x3, waiting for transfers between devices: none -> 44.9 us  [the longest x1 15.7 us: body(): lax.all_to_all(hidden, 'enc', 0, 0, axis_index_groups=GROUPS_Z, tiled=True)]
    ppermute x0 -> x10, waiting for transfers between devices: none -> 30.2 us  [the longest x3 13 us: body(): lax.ppermute(dealt, 'enc', shift_x(d))]
    dot_general x4 -> x0, matrix products: 30 us -> none  [the longest x1 16.9 us: body(): jnp.dot(hidden, lax.all_gather(merge_out, 'enc', axis=1, tiled=True), pre...]
    unnamed x20, local copies, waits for them, and re-layouts: 29 us -> 6.82 us
    all_to_all x0 -> x3, starting transfers between devices: none -> 17.3 us  [the longest x1 8.26 us: body(): lax.all_to_all(hidden, 'enc', 0, 0, axis_index_groups=GROUPS_Z, tiled=True)]
    ppermute x0 -> x10, starting transfers between devices: none -> 16.9 us  [the longest x3 5.72 us: body(): lax.ppermute(packed, 'enc', shift_x(d))]
  transfers between devices with their start and end apart: 5 -> 15, of which waited for: 5 -> 11; matrix products, arithmetic and copies ran while one was open for 13% -> 6% of each run, Pallas kernels for 0% -> 7%
where the time goes in v1:
time: 160 us; the launch traced here: 159 us
  waiting for transfers between devices  77.8 us (49%)
  starting transfers between devices  34.2 us (21%)
  Pallas kernels  16.7 us (10%)
  between operations  14.3 us (9%)
  local copies, waits for them, and re-layouts  13.2 us (8%)
  other arithmetic  3.04 us (2%)
    all_to_all x1, waiting for transfers between devices, body(): lax.all_to_all(hidden, 'enc', 0, 0, axis_index_groups=GROUPS_Z, tiled=True)  15.7 us
    all_to_all x1, waiting for transfers between devices, body(): lax.all_to_all(sent, 'tp', 0, 0, tiled=True).reshape(kv_parts.shape)  15.1 us
    all_to_all x1, waiting for transfers between devices, body(): moved = lax.all_to_all(merged, 'enc', 0, 0, tiled=True)  14.1 us
    ppermute x3, waiting for transfers between devices, body(): lax.ppermute(dealt, 'enc', shift_x(d))  13 us
    ppermute x3, waiting for transfers between devices, body(): total = total + lax.ppermute(parts[d], 'tp', shift_y(d)).astype(F32)  10.4 us
    all_to_all x1, starting transfers between devices, body(): lax.all_to_all(hidden, 'enc', 0, 0, axis_index_groups=GROUPS_Z, tiled=True)  8.26 us
    unnamed x20, local copies, waits for them, and re-layouts  6.82 us
    ppermute x3, starting transfers between devices, body(): lax.ppermute(packed, 'enc', shift_x(d))  5.72 us
  transfers between devices with their start and end apart: 15, of which 11 were waited for; matrix products, arithmetic and copies ran while one was open for 6% of the time, Pallas kernels for 7%

profile of v1, /device:TPU:1, one launch (start us, length us, event | category | flops | bytes accessed | tf_op | source)
XLA Modules:
  0.0 159.2 jit_solution(10322939404222122021)
XLA Ops:
  8.9 2.1 %collective-permute-start.7 = (bf16[512,128]{0,1:T(8,128)(2,1)S(1)}, bf16[512,128]{0,1:T(8,128)(2,1)S(1)}, u32[]{:S(2)}, u32[]{:S(2)}) collective-permute-start(bf16[512,128]{0,1:T(8,128)(2,1)S(1)} %get-tuple-element.15), channel_id=1, source_target_pairs={{0,8},{8,16},{16,24},{24,0},{32,40},{40,48},{48,56},{56,32},{64,72... | collective-permute-start | bytes 393224 | tf_op jit(solution)/shard_map/ppermute | solution.py:295
  11.0 2.5 %collective-permute-start.8 = (bf16[512,128]{0,1:T(8,128)(2,1)S(1)}, bf16[512,128]{0,1:T(8,128)(2,1)S(1)}, u32[]{:S(2)}, u32[]{:S(2)}) collective-permute-start(bf16[512,128]{0,1:T(8,128)(2,1)S(1)} %get-tuple-element.15), channel_id=1, source_target_pairs={{0,16},{8,24},{16,0},{24,8},{32,48},{40,56},{48,32},{56,40},{64,80... | collective-permute-start | bytes 393224 | tf_op jit(solution)/shard_map/ppermute | solution.py:295
  14.7 4.5 %collective-permute-done.8 = bf16[512,128]{0,1:T(8,128)(2,1)S(1)} collective-permute-done((bf16[512,128]{0,1:T(8,128)(2,1)S(1)}, bf16[512,128]{0,1:T(8,128)(2,1)S(1)}, u32[]{:S(2)}, u32[]{:S(2)}) %collective-permute-start.8) | collective-permute-done | bytes 131104 | tf_op jit(solution)/shard_map/ppermute | solution.py:295
  23.4 2.0 %copy.21 = bf16[1,1024,256]{2,1,0:T(8,128)(2,1)} copy(bf16[1,1024,256]{1,2,0:T(8,128)(2,1)} %all_gather_reshape.3) | data formatting | bytes 1048576 | tf_op jit(solution)/shard_map/all_gather;reshape | solution.py:299
  25.5 2.9 %copy-done = bf16[5120,640]{1,0:T(8,128)(2,1)S(1)} copy-done((bf16[5120,640]{1,0:T(8,128)(2,1)S(1)}, bf16[5120,640]{1,0:T(8,128)(2,1)}, u32[]{:S(2)}) %copy-start) | copy-done | bytes 6553624
  28.4 5.4 %shard_map.113 = bf16[256,640]{1,0:T(8,128)(2,1)} custom-call(bf16[256,5120]{1,0:T(8,128)(2,1)S(1)} %bitcast.20, f32[1,1280]{1,0:T(1,128)S(1)} %broadcast_in_dim.18.gain_ref, f32[1,1280]{1,0:T(1,128)S(1)} %broadcast_in_dim.19.bias_ref, bf16[5120,640]{1,0:T(8,128)(2,1)S(1)} %copy-done), custom_call_target="tpu_custom_call" | custom-call | flops 1677721600 | bytes 9175040 | tf_op jit(solution)/shard_map/pallas_call | solution.py:67
  33.8 8.3 %all-to-all-start = ((bf16[8,32,640]{2,1,0:T(8,128)(2,1)}), bf16[8,32,640]{2,1,0:T(8,128)(2,1)S(1)}, u32[]{:S(2)}, u32[]{:S(2)}) async-start(bf16[8,32,640]{2,1,0:T(8,128)(2,1)} %bitcast.1), calls=%async_computation | async-start | bytes 655360 | tf_op jit(solution)/shard_map/all_to_all | solution.py:302
  42.2 15.7 %all-to-all-done = bf16[8,32,640]{2,1,0:T(8,128)(2,1)S(1)} async-done(((bf16[8,32,640]{2,1,0:T(8,128)(2,1)}), bf16[8,32,640]{2,1,0:T(8,128)(2,1)S(1)}, u32[]{:S(2)}, u32[]{:S(2)}) %all-to-all-start) | async-done | bytes 327712 | tf_op jit(solution)/shard_map/all_to_all | solution.py:302
  59.1 2.9 %collective-permute-start.1 = (bf16[256,640]{1,0:T(8,128)(2,1)S(1)}, bf16[256,640]{1,0:T(8,128)(2,1)S(1)}, u32[]{:S(2)}, u32[]{:S(2)}) collective-permute-start(bf16[256,640]{1,0:T(8,128)(2,1)S(1)} %bitcast.22), channel_id=1, source_target_pairs={{0,16},{8,24},{16,0},{24,8},{32,48},{40,56},{48,32},{56,40},{64,80... | collective-permute-start | bytes 983048 | tf_op jit(solution)/shard_map/ppermute | solution.py:303
  62.3 3.9 %collective-permute-done.b = bf16[256,640]{1,0:T(8,128)(2,1)S(1)} collective-permute-done((bf16[256,640]{1,0:T(8,128)(2,1)S(1)}, bf16[256,640]{1,0:T(8,128)(2,1)S(1)}, u32[]{:S(2)}, u32[]{:S(2)}) %collective-permute-start) | collective-permute-done | bytes 327712 | tf_op jit(solution)/shard_map/ppermute | solution.py:303
  66.1 8.7 %collective-permute-done.1.c = bf16[256,640]{1,0:T(8,128)(2,1)S(1)} collective-permute-done((bf16[256,640]{1,0:T(8,128)(2,1)S(1)}, bf16[256,640]{1,0:T(8,128)(2,1)S(1)}, u32[]{:S(2)}, u32[]{:S(2)}) %collective-permute-start.1) | collective-permute-done | bytes 327712 | tf_op jit(solution)/shard_map/ppermute | solution.py:303
  77.0 3.1 %shard_map.114 = (bf16[512,640]{1,0:T(8,128)(2,1)S(1)}, bf16[4,512,256]{2,1,0:T(8,128)(2,1)S(1)}) custom-call(s32[4]{0:T(128)S(1)} %broadcast_add_fusion.1.order_ref, s32[512,1]{1,0:T(8,128)S(1)} %add.222.target_ref, bf16[256,640]{1,0:T(8,128)(2,1)S(1)} %bitcast.24, bf16[256,640]{1,0:T(8,128)(2,1)S(1)} %collective-permute-done.b, ...), custom_call_target="tpu_custom_call" | custom-call | flops 1342177280 | bytes 2359296 | tf_op jit(solution)/shard_map/pallas_call | solution.py:110
  80.1 2.6 %collective-permute-start.3 = (bf16[4,512,256]{2,1,0:T(8,128)(2,1)S(1)}, bf16[4,512,256]{2,1,0:T(8,128)(2,1)S(1)}, u32[]{:S(2)}, u32[]{:S(2)}) collective-permute-start(bf16[4,512,256]{2,1,0:T(8,128)(2,1)S(1)} %get-tuple-element.9), channel_id=1, source_target_pairs={{0,1},{1,0},{2,3},{3,2},{4,5},{5,4},{6,7},{7,6},{8,9},{9,8},{10,11... | collective-permute-start | bytes 3145736 | tf_op jit(solution)/shard_map/ppermute | solution.py:317
  82.7 2.3 %collective-permute-done.3.got_ref = bf16[4,512,256]{2,1,0:T(8,128)(2,1)S(1)} collective-permute-done((bf16[4,512,256]{2,1,0:T(8,128)(2,1)S(1)}, bf16[4,512,256]{2,1,0:T(8,128)(2,1)S(1)}, u32[]{:S(2)}, u32[]{:S(2)}) %collective-permute-start.3) | collective-permute-done | bytes 1048608 | tf_op jit(solution)/shard_map/ppermute | solution.py:317
  84.9 2.2 %shard_map.115 = (bf16[512,256]{1,0:T(8,128)(2,1)S(1)}, bf16[512,256]{1,0:T(8,128)(2,1)S(1)}, bf16[512,256]{1,0:T(8,128)(2,1)S(1)}, bf16[512,256]{1,0:T(8,128)(2,1)S(1)}) custom-call(s32[4]{0:T(128)S(1)} %broadcast_add_fusion.2.order_ref, bf16[512,640]{1,0:T(8,128)(2,1)S(1)} %get-tuple-element.8.live_ref, bf16[8,640,256]{2,1,0:T(8,128)(2,1)S(1)} %bitcast.19, ...), custom_call_target="tpu_custom_call" | custom-call | flops 671088640 | bytes 3407872 | tf_op jit(solution)/shard_map/pallas_call | solution.py:150
  91.7 4.4 %collective-permute-done.4 = bf16[512,256]{1,0:T(8,128)(2,1)S(1)} collective-permute-done((bf16[512,256]{1,0:T(8,128)(2,1)S(1)}, bf16[512,256]{1,0:T(8,128)(2,1)S(1)}, u32[]{:S(2)}, u32[]{:S(2)}) %collective-permute-start.4) | collective-permute-done | bytes 262176 | tf_op jit(solution)/shard_map/ppermute | solution.py:321
  96.1 6.0 %collective-permute-done.5 = bf16[512,256]{1,0:T(8,128)(2,1)S(1)} collective-permute-done((bf16[512,256]{1,0:T(8,128)(2,1)S(1)}, bf16[512,256]{1,0:T(8,128)(2,1)S(1)}, u32[]{:S(2)}, u32[]{:S(2)}) %collective-permute-start.5) | collective-permute-done | bytes 262176 | tf_op jit(solution)/shard_map/ppermute | solution.py:321
  102.9 3.9 %all-to-all-start.1 = ((bf16[32,16,256]{2,1,0:T(8,128)(2,1)}), bf16[32,16,256]{2,1,0:T(8,128)(2,1)S(1)}, u32[]{:S(2)}, u32[]{:S(2)}) async-start(bf16[32,16,256]{2,1,0:T(8,128)(2,1)} %bitcast.4), calls=%async_computation.1 | async-start | bytes 524288 | tf_op jit(solution)/shard_map/all_to_all | solution.py:324
  107.2 14.1 %all-to-all-done.1.moved_ref = bf16[32,16,256]{2,1,0:T(8,128)(2,1)S(1)} async-done(((bf16[32,16,256]{2,1,0:T(8,128)(2,1)}), bf16[32,16,256]{2,1,0:T(8,128)(2,1)S(1)}, u32[]{:S(2)}, u32[]{:S(2)}) %all-to-all-start.1) | async-done | bytes 262176 | tf_op jit(solution)/shard_map/all_to_all | solution.py:324
  121.3 2.1 %all-gather.4.cloned.1.call-done.weight_ref = bf16[8,1024,256]{2,1,0:T(8,128)(2,1)} async-done(((bf16[1,1024,256]{2,1,0:T(8,128)(2,1)}), bf16[8,1024,256]{2,1,0:T(8,128)(2,1)}) %all-gather.4.cloned.1.call-update) | async-done | bytes 4194320 | tf_op jit(solution)/shard_map/all_gather | solution.py:299
  123.4 2.2 %copy-done.1 = bf16[8,1024,256]{2,1,0:T(8,128)(2,1)S(1)} copy-done((bf16[8,1024,256]{2,1,0:T(8,128)(2,1)S(1)}, bf16[8,1024,256]{2,1,0:T(8,128)(2,1)}, u32[]{:S(2)}) %copy-start.1) | copy-done | bytes 4194328
  125.6 5.0 %shard_map.116 = bf16[8,272,256]{2,1,0:T(8,128)(2,1)} custom-call(s32[1,128]{1,0:T(1,128)S(1)} %add.196.target_ref, bf16[32,16,256]{2,1,0:T(8,128)(2,1)S(1)} %all-to-all-done.1.moved_ref, bf16[256,1024]{1,0:T(8,128)(2,1)S(1)} %copy-done.5, bf16[8,1024,256]{2,1,0:T(8,128)(2,1)S(1)} %copy-done.1), custom_call_target="tpu_custom_call" | custom-call | flops 1342177280 | bytes 5242880 | tf_op jit(solution)/shard_map/pallas_call | solution.py:213
  130.6 5.1 %all-to-all-start.2 = ((bf16[8,272,256]{2,1,0:T(8,128)(2,1)}), bf16[8,272,256]{2,1,0:T(8,128)(2,1)S(1)}, u32[]{:S(2)}, u32[]{:S(2)}) async-start(bf16[8,272,256]{2,1,0:T(8,128)(2,1)} %shard_map.116), calls=%async_computation.2 | async-start | bytes 2228224 | tf_op jit(solution)/shard_map/all_to_all | solution.py:337
  136.4 15.1 %all-to-all-done.2.parts_ref = bf16[8,272,256]{2,1,0:T(8,128)(2,1)S(1)} async-done(((bf16[8,272,256]{2,1,0:T(8,128)(2,1)}), bf16[8,272,256]{2,1,0:T(8,128)(2,1)S(1)}, u32[]{:S(2)}, u32[]{:S(2)}) %all-to-all-start.2) | async-done | bytes 1114144 | tf_op jit(solution)/shard_map/all_to_all | solution.py:337
  (61 shorter events, 18.0 us)
Async XLA Ops:
  7.2 68.0 %all-gather.6.cloned.1.call-start = ((), (), s32[]{:S(2)}) async-start(), calls=%async_computation.4 | async-start | bytes 2949120 | tf_op jit(solution)/shard_map/all_gather | solution.py:290
  7.9 115.5 %all-gather.4.cloned.1.call-start = ((), (), s32[]{:S(2)}) async-start(), calls=%async_computation.3 | async-start | bytes 4718592 | tf_op jit(solution)/shard_map/all_gather | solution.py:299
  8.9 5.8 %collective-permute-start.7 = (bf16[512,128]{0,1:T(8,128)(2,1)S(1)}, bf16[512,128]{0,1:T(8,128)(2,1)S(1)}, u32[]{:S(2)}, u32[]{:S(2)}) collective-permute-start(bf16[512,128]{0,1:T(8,128)(2,1)S(1)} %get-tuple-element.15), channel_id=1, source_target_pairs={{0,8},{8,16},{16,24},{24,0},{32,40},{40,48},{48,56},{56,32},{64,72... | collective-permute-start | bytes 393224 | tf_op jit(solution)/shard_map/ppermute | solution.py:295
  11.0 8.2 %collective-permute-start.8 = (bf16[512,128]{0,1:T(8,128)(2,1)S(1)}, bf16[512,128]{0,1:T(8,128)(2,1)S(1)}, u32[]{:S(2)}, u32[]{:S(2)}) collective-permute-start(bf16[512,128]{0,1:T(8,128)(2,1)S(1)} %get-tuple-element.15), channel_id=1, source_target_pairs={{0,16},{8,24},{16,0},{24,8},{32,48},{40,56},{48,32},{56,40},{64,80... | collective-permute-start | bytes 393224 | tf_op jit(solution)/shard_map/ppermute | solution.py:295
  13.5 5.7 %collective-permute-start.9 = (bf16[512,128]{0,1:T(8,128)(2,1)S(1)}, bf16[512,128]{0,1:T(8,128)(2,1)S(1)}, u32[]{:S(2)}, u32[]{:S(2)}) collective-permute-start(bf16[512,128]{0,1:T(8,128)(2,1)S(1)} %get-tuple-element.15), channel_id=1, source_target_pairs={{0,24},{8,0},{16,8},{24,16},{32,56},{40,32},{48,40},{56,48},{64,88... | collective-permute-start | bytes 393224 | tf_op jit(solution)/shard_map/ppermute | solution.py:295
  19.3 6.2 %copy-start.6 = (f32[1280]{0:T(1024)S(1)}, f32[1280]{0:T(1024)}, u32[]{:S(2)}) copy-start(f32[1280]{0:T(1024)} %param.13) | copy-start | bytes 15364
  19.3 6.2 %copy-start.7 = (f32[1280]{0:T(1024)S(1)}, f32[1280]{0:T(1024)}, u32[]{:S(2)}) copy-start(f32[1280]{0:T(1024)} %param.14) | copy-start | bytes 15364
  19.3 6.2 %copy-start.4 = (bf16[4,64,5120]{2,1,0:T(8,128)(2,1)S(1)}, bf16[4,64,5120]{2,1,0:T(8,128)(2,1)}, u32[]{:S(2)}) copy-start(bf16[4,64,5120]{2,1,0:T(8,128)(2,1)} %param.10) | copy-start | bytes 7864324
  25.5 2.9 %copy-start = (bf16[5120,640]{1,0:T(8,128)(2,1)S(1)}, bf16[5120,640]{1,0:T(8,128)(2,1)}, u32[]{:S(2)}) copy-start(bf16[5120,640]{1,0:T(8,128)(2,1)} %weight_ref.1) | copy-start | bytes 19660804
  28.4 13.7 %copy-start.9 = (s32[128]{0:T(128)S(1)}, s32[128]{0:T(128)}, u32[]{:S(2)}) copy-start(s32[128]{0:T(128)} %param.11) | copy-start | bytes 1540
  33.8 24.1 %all-to-all-start = ((bf16[8,32,640]{2,1,0:T(8,128)(2,1)}), bf16[8,32,640]{2,1,0:T(8,128)(2,1)S(1)}, u32[]{:S(2)}, u32[]{:S(2)}) async-start(bf16[8,32,640]{2,1,0:T(8,128)(2,1)} %bitcast.1), calls=%async_computation | async-start | bytes 655360 | tf_op jit(solution)/shard_map/all_to_all | solution.py:302
  57.9 8.2 %collective-permute-start = (bf16[256,640]{1,0:T(8,128)(2,1)S(1)}, bf16[256,640]{1,0:T(8,128)(2,1)S(1)}, u32[]{:S(2)}, u32[]{:S(2)}) collective-permute-start(bf16[256,640]{1,0:T(8,128)(2,1)S(1)} %bitcast.21), channel_id=1, source_target_pairs={{0,8},{8,16},{16,24},{24,0},{32,40},{40,48},{48,56},{56,32},{64,72... | collective-permute-start | bytes 983048 | tf_op jit(solution)/shard_map/ppermute | solution.py:303
  59.1 15.7 %collective-permute-start.1 = (bf16[256,640]{1,0:T(8,128)(2,1)S(1)}, bf16[256,640]{1,0:T(8,128)(2,1)S(1)}, u32[]{:S(2)}, u32[]{:S(2)}) collective-permute-start(bf16[256,640]{1,0:T(8,128)(2,1)S(1)} %bitcast.22), channel_id=1, source_target_pairs={{0,16},{8,24},{16,0},{24,8},{32,48},{40,56},{48,32},{56,40},{64,80... | collective-permute-start | bytes 983048 | tf_op jit(solution)/shard_map/ppermute | solution.py:303
  62.0 13.2 %collective-permute-start.2 = (bf16[256,640]{1,0:T(8,128)(2,1)S(1)}, bf16[256,640]{1,0:T(8,128)(2,1)S(1)}, u32[]{:S(2)}, u32[]{:S(2)}) collective-permute-start(bf16[256,640]{1,0:T(8,128)(2,1)S(1)} %bitcast.23), channel_id=1, source_target_pairs={{0,24},{8,0},{16,8},{24,16},{32,56},{40,32},{48,40},{56,48},{64,88... | collective-permute-start | bytes 983048 | tf_op jit(solution)/shard_map/ppermute | solution.py:303
  77.0 8.0 %copy-start.3 = (bf16[5120,256]{1,0:T(8,128)(2,1)S(1)}, bf16[5120,256]{1,0:T(8,128)(2,1)}, u32[]{:S(2)}) copy-start(bf16[5120,256]{1,0:T(8,128)(2,1)} %all-gather.6.cloned.1.call-done) | copy-start | bytes 7864324
  80.1 4.9 %collective-permute-start.3 = (bf16[4,512,256]{2,1,0:T(8,128)(2,1)S(1)}, bf16[4,512,256]{2,1,0:T(8,128)(2,1)S(1)}, u32[]{:S(2)}, u32[]{:S(2)}) collective-permute-start(bf16[4,512,256]{2,1,0:T(8,128)(2,1)S(1)} %get-tuple-element.9), channel_id=1, source_target_pairs={{0,1},{1,0},{2,3},{3,2},{4,5},{5,4},{6,7},{7,6},{8,9},{9,8},{10,11... | collective-permute-start | bytes 3145736 | tf_op jit(solution)/shard_map/ppermute | solution.py:317
  84.9 21.9 %copy-start.8 = (s32[64]{0:T(128)S(1)}, s32[64]{0:T(128)}, u32[]{:S(2)}) copy-start(s32[64]{0:T(128)} %param.12) | copy-start | bytes 772
  84.9 38.4 %copy-start.5 = (bf16[256,1024]{1,0:T(8,128)(2,1)S(1)}, bf16[256,1024]{1,0:T(8,128)(2,1)}, u32[]{:S(2)}) copy-start(bf16[256,1024]{1,0:T(8,128)(2,1)} %text_ref.1) | copy-start | bytes 1572868
  87.2 8.9 %collective-permute-start.4 = (bf16[512,256]{1,0:T(8,128)(2,1)S(1)}, bf16[512,256]{1,0:T(8,128)(2,1)S(1)}, u32[]{:S(2)}, u32[]{:S(2)}) collective-permute-start(bf16[512,256]{1,0:T(8,128)(2,1)S(1)} %get-tuple-element.11), channel_id=1, source_target_pairs={{0,2},{1,3},{2,4},{3,5},{4,6},{5,7},{6,0},{7,1},{8,10},{9,11},{10,... | collective-permute-start | bytes 786440 | tf_op jit(solution)/shard_map/ppermute | solution.py:321
  88.4 13.7 %collective-permute-start.5 = (bf16[512,256]{1,0:T(8,128)(2,1)S(1)}, bf16[512,256]{1,0:T(8,128)(2,1)S(1)}, u32[]{:S(2)}, u32[]{:S(2)}) collective-permute-start(bf16[512,256]{1,0:T(8,128)(2,1)S(1)} %get-tuple-element.12), channel_id=1, source_target_pairs={{0,4},{1,5},{2,6},{3,7},{4,0},{5,1},{6,2},{7,3},{8,12},{9,13},{10,... | collective-permute-start | bytes 786440 | tf_op jit(solution)/shard_map/ppermute | solution.py:321
  90.4 11.7 %collective-permute-start.6 = (bf16[512,256]{1,0:T(8,128)(2,1)S(1)}, bf16[512,256]{1,0:T(8,128)(2,1)S(1)}, u32[]{:S(2)}, u32[]{:S(2)}) collective-permute-start(bf16[512,256]{1,0:T(8,128)(2,1)S(1)} %get-tuple-element.13), channel_id=1, source_target_pairs={{0,6},{1,7},{2,0},{3,1},{4,2},{5,3},{6,4},{7,5},{8,14},{9,15},{10,... | collective-permute-start | bytes 786440 | tf_op jit(solution)/shard_map/ppermute | solution.py:321
  102.9 18.3 %all-to-all-start.1 = ((bf16[32,16,256]{2,1,0:T(8,128)(2,1)}), bf16[32,16,256]{2,1,0:T(8,128)(2,1)S(1)}, u32[]{:S(2)}, u32[]{:S(2)}) async-start(bf16[32,16,256]{2,1,0:T(8,128)(2,1)} %bitcast.4), calls=%async_computation.1 | async-start | bytes 524288 | tf_op jit(solution)/shard_map/all_to_all | solution.py:324
  123.4 2.2 %copy-start.1 = (bf16[8,1024,256]{2,1,0:T(8,128)(2,1)S(1)}, bf16[8,1024,256]{2,1,0:T(8,128)(2,1)}, u32[]{:S(2)}) copy-start(bf16[8,1024,256]{2,1,0:T(8,128)(2,1)} %all-gather.4.cloned.1.call-done.weight_ref) | copy-start | bytes 12582916
  130.6 20.9 %all-to-all-start.2 = ((bf16[8,272,256]{2,1,0:T(8,128)(2,1)}), bf16[8,272,256]{2,1,0:T(8,128)(2,1)S(1)}, u32[]{:S(2)}, u32[]{:S(2)}) async-start(bf16[8,272,256]{2,1,0:T(8,128)(2,1)} %shard_map.116), calls=%async_computation.2 | async-start | bytes 2228224 | tf_op jit(solution)/shard_map/all_to_all | solution.py:337
  (1 other events, 1.7 us)
Sparse Core Ops, SparseCore 0:
  9.8 50.4 all-gather.5
  62.1 61.2 all-gather.3

commit v2 on v1

v2 whole, which is shorter than its diff:
```python
import functools

import jax
import jax.numpy as jnp
from jax import lax
from jax.experimental import pallas as pl
from jax.experimental.pallas import tpu as pltpu
from jax.sharding import PartitionSpec as P

EPS = 1e-06
THETA = 1000000.0
NZ, NX, NY, NC = 8, 4, 4, 2
TAILS = 2
VMEM_LIMIT = 24 * 1024 * 1024
BF = jnp.bfloat16
F32 = jnp.float32

GROUPS_Z = [[z * NX + x for z in range(NZ)] for x in range(NX)]


def shift_x(d):
    return [(z * NX + x, z * NX + (x + d) % NX) for z in range(NZ) for x in range(NX)]


def shift_y(d):
    return [(y * NC + c, (y + d) % NY * NC + c) for y in range(NY) for c in range(NC)]


SWAP_CORE = [(t, t ^ 1) for t in range(NY * NC)]


IN_VMEM = pl.BlockSpec(memory_space=pltpu.VMEM)
IN_SMEM = pl.BlockSpec(memory_space=pltpu.SMEM)
IN_HBM = pl.BlockSpec(memory_space=pltpu.HBM)


def in_hbm(array):
    return pltpu.with_memory_space_constraint(array, pltpu.HBM)


def hidden_kernel(
    slots, patch_ref, gain_ref, bias_ref, weight_ref, out_ref, patch_buf, weight_buf, sems
):
    width = weight_buf.shape[1]
    copies = []
    for i in range(weight_buf.shape[0]):
        part = pl.ds(i * width, width)
        pair = (
            pltpu.make_async_copy(patch_ref.at[:, part], patch_buf.at[i], sems.at[0, i]),
            pltpu.make_async_copy(weight_ref.at[part], weight_buf.at[i], sems.at[1, i]),
        )
        for copy in pair:
            copy.start()
        copies.append(pair)
    gain, bias = gain_ref[...][None, :], bias_ref[...][None, :]
    total = None
    for i, pair in enumerate(copies):
        pair[0].wait()
        part = patch_buf[i].astype(F32)
        center = jnp.mean(part, axis=-1, keepdims=True)
        part = part - center
        spread = jnp.mean(part * part, axis=-1, keepdims=True)
        normed = (part * lax.rsqrt(spread + EPS) * gain + bias).astype(BF)
        pair[1].wait()
        term = jnp.dot(normed, weight_buf[i], preferred_element_type=F32)
        total = term if total is None else total + term
    total = 0.5 * total * (1.0 + lax.erf(total * 0.7071067811865476))
    rows = total.shape[0] // slots
    chunk = rows // NZ
    pieces = [
        total[slot * rows + z * chunk : slot * rows + (z + 1) * chunk]
        for z in range(NZ)
        for slot in range(slots)
    ]
    out_ref[...] = jnp.concatenate(pieces, axis=0).astype(BF)


def hidden_rows(patches, patch_gain, patch_bias, merge_in):
    slots, rows, feature = patches.shape
    width = patch_gain.shape[0]
    groups = feature // width
    flat = patches.reshape(slots * rows, feature)
    out_width = merge_in.shape[1]
    return pl.pallas_call(
        functools.partial(hidden_kernel, slots),
        in_specs=[
            pl.BlockSpec(memory_space=pltpu.HBM),
            pl.BlockSpec(memory_space=pltpu.VMEM),
            pl.BlockSpec(memory_space=pltpu.VMEM),
            pl.BlockSpec(memory_space=pltpu.HBM),
        ],
        out_specs=pl.BlockSpec(memory_space=pltpu.VMEM),
        out_shape=jax.ShapeDtypeStruct((slots * rows, out_width), BF),
        scratch_shapes=[
            pltpu.VMEM((groups, slots * rows, width), BF),
            pltpu.VMEM((groups, width, out_width), BF),
            pltpu.SemaphoreType.DMA((2, groups)),
        ],
        compiler_params=pltpu.CompilerParams(vmem_limit_bytes=VMEM_LIMIT),
        cost_estimate=pl.CostEstimate(
            flops=2 * slots * rows * feature * out_width,
            bytes_accessed=2 * feature * (out_width + slots * rows),
            transcendentals=0,
        ),
    )(in_hbm(flat), patch_gain, patch_bias, in_hbm(merge_in))


def fetch(order_ref, weight_ref, buf, sems):
    copies = [
        pltpu.make_async_copy(
            weight_ref.at[order_ref[i], : buf.shape[1]], buf.at[i], sems.at[i]
        )
        for i in range(buf.shape[0])
    ]
    for copy in copies:
        copy.start()
    return copies


def send_kernel(order_ref, target_ref, a, b, c, d, weight_ref, live_ref, out_ref, buf, sems):
    copies = fetch(order_ref, weight_ref, buf, sems)
    target = target_ref[...]
    total = None
    for index, piece in enumerate((a, b, c, d)):
        rows = piece.shape[0]
        place = lax.broadcasted_iota(jnp.int32, (target.shape[0], rows), 1) + index * rows
        pick = jnp.where(place == target, 1.0, 0.0).astype(BF)
        term = jnp.dot(pick, piece[...], preferred_element_type=F32)
        total = term if total is None else total + term
    live_ref[...] = total.astype(BF)
    for i, copy in enumerate(copies):
        copy.wait()
        out_ref[i] = jnp.dot(live_ref[...], buf[i], preferred_element_type=F32).astype(BF)


def send_parts(order, target, pieces, weights):
    rows, depth = target.shape[0], pieces[0].shape[1]
    width = weights.shape[2]
    return pl.pallas_call(
        send_kernel,
        in_specs=[IN_SMEM, IN_VMEM] + [IN_VMEM] * 4 + [IN_HBM],
        out_specs=[IN_VMEM, IN_VMEM],
        out_shape=[
            jax.ShapeDtypeStruct((rows, depth), BF),
            jax.ShapeDtypeStruct((NY, rows, width), BF),
        ],
        scratch_shapes=[pltpu.VMEM((NY, depth, width), BF), pltpu.SemaphoreType.DMA((NY,))],
        compiler_params=pltpu.CompilerParams(vmem_limit_bytes=VMEM_LIMIT),
        cost_estimate=pl.CostEstimate(
            flops=2 * rows * depth * (width * NY + 2 * rows),
            bytes_accessed=2 * (depth * width * NY + rows * width * NY),
            transcendentals=0,
        ),
    )(order, target, *pieces, in_hbm(weights))


def keep_kernel(order_ref, live_ref, weight_ref, got_ref, a, b, c, d, buf, sems):
    copies = fetch(order_ref, weight_ref, buf, sems)
    for i, out_ref in enumerate((a, b, c, d)):
        copies[i].wait()
        own = jnp.dot(live_ref[...], buf[i], preferred_element_type=F32).astype(BF)
        out_ref[...] = (own.astype(F32) + got_ref[i].astype(F32)).astype(BF)


def keep_parts(order, live, weights, got):
    rows, depth = live.shape
    width = weights.shape[2]
    return pl.pallas_call(
        keep_kernel,
        in_specs=[IN_SMEM, IN_VMEM, IN_HBM, IN_VMEM],
        out_specs=[IN_VMEM] * NY,
        out_shape=[jax.ShapeDtypeStruct((rows, width), BF)] * NY,
        scratch_shapes=[pltpu.VMEM((NY, depth, width), BF), pltpu.SemaphoreType.DMA((NY,))],
        compiler_params=pltpu.CompilerParams(vmem_limit_bytes=VMEM_LIMIT),
        cost_estimate=pl.CostEstimate(
            flops=2 * rows * depth * width * NY,
            bytes_accessed=2 * (depth * width * NY + 2 * rows * width * NY),
            transcendentals=0,
        ),
    )(order, live, in_hbm(weights), got)


def put_head(i, order_ref, rows_ref, first_ref, rest_refs, out_ref, more=None):
    head = order_ref[i]
    rows = first_ref.shape[1] // NX
    lines = []
    for d in range(NX):
        line = [first_ref[i, d * rows : (d + 1) * rows]]
        line += [ref[head] for ref in rest_refs[d * TAILS : (d + 1) * TAILS]]
        lines.append(jnp.concatenate(line, axis=1))
    part = jnp.dot(
        jnp.concatenate(lines, axis=0), rows_ref[...], preferred_element_type=F32
    ).astype(BF)
    for d in range(NX):
        place = pl.ds(pl.multiple_of(order_ref[NY + d] * rows, rows), rows)
        piece = part[d * rows : (d + 1) * rows]
        if more is not None:
            piece = (piece.astype(F32) + more[i, place].astype(F32)).astype(BF)
        out_ref[place] = piece


def two_lines(squares):
    squares = jnp.broadcast_to(squares, (16, squares.shape[1]))
    high = squares.astype(BF).astype(F32)
    line = lax.broadcasted_iota(jnp.int32, squares.shape, 0)
    return jnp.where(line == 0, high, jnp.where(line == 1, squares - high, 0.0)).astype(BF)


def project_send_kernel(order_ref, target_ref, moved_ref, text_ref, first_ref, *refs):
    rest_refs, (rows_ref, squares_ref, out_ref, buf, sems) = refs[:-5], refs[-5:]
    copies = fetch(order_ref, first_ref, buf, sems)
    span = text_ref.shape[0]
    target = target_ref[...]
    place = lax.broadcasted_iota(jnp.int32, (span, target.shape[1]), 0) == target
    pick = jnp.where(place, 1.0, 0.0)
    covered = jnp.sum(pick, axis=1, keepdims=True) > 0.5
    pick = pick.astype(BF)
    width = moved_ref.shape[2]
    squares = jnp.zeros((1, span), F32)
    for x in range(NX):
        stacked = jnp.concatenate([moved_ref[z * NX + x] for z in range(NZ)], axis=0)
        put = jnp.dot(pick, stacked, preferred_element_type=F32)
        columns = slice(x * width, (x + 1) * width)
        mixed = jnp.where(covered, put, text_ref[:, columns].astype(F32)).T
        rows_ref[columns] = mixed.astype(BF)
        squares += jnp.sum(mixed * mixed, axis=0, keepdims=True)
    squares_ref[...] = two_lines(squares)
    for i, copy in enumerate(copies):
        copy.wait()
        put_head(i, order_ref, rows_ref, buf, rest_refs, out_ref.at[i])
        out_ref[i, buf.shape[1] :] = squares_ref[...]


def project_send(order, target, moved, text, first, rest):
    span, features = text.shape
    width = first.shape[1]
    return pl.pallas_call(
        project_send_kernel,
        in_specs=[IN_SMEM] + [IN_VMEM] * 3 + [IN_HBM] + [IN_VMEM] * len(rest),
        out_specs=[IN_VMEM] * 3,
        out_shape=[
            jax.ShapeDtypeStruct((features, span), BF),
            jax.ShapeDtypeStruct((16, span), BF),
            jax.ShapeDtypeStruct((NY, width + 16, span), BF),
        ],
        scratch_shapes=[
            pltpu.VMEM((NY, width, first.shape[2]), BF),
            pltpu.SemaphoreType.DMA((NY,)),
        ],
        compiler_params=pltpu.CompilerParams(vmem_limit_bytes=VMEM_LIMIT),
        cost_estimate=pl.CostEstimate(
            flops=2 * span * features * (width * NY + 2 * span),
            bytes_accessed=2 * NY * width * (features + span),
            transcendentals=0,
        ),
    )(order, target, moved, text, in_hbm(first), *rest)


def project_keep_kernel(order_ref, rows_ref, squares_ref, got_ref, first_ref, *refs):
    rest_refs, out_refs, (buf, sems) = refs[: -NY - 2], refs[-NY - 2 : -2], refs[-2:]
    copies = fetch(order_ref, first_ref, buf, sems)
    width = first_ref.shape[1]
    for i, out_ref in enumerate(out_refs):
        copies[i].wait()
        put_head(i, order_ref, rows_ref, buf, rest_refs, out_ref, got_ref)
        squares = squares_ref[...].astype(F32) + got_ref[i, width:].astype(F32)
        out_ref[width:] = two_lines(squares[0:1] + squares[1:2])


def project_keep(order, rows, squares, first, rest, got):
    features, span = rows.shape
    width = first.shape[1]
    return pl.pallas_call(
        project_keep_kernel,
        in_specs=[IN_SMEM] + [IN_VMEM] * 3 + [IN_HBM] + [IN_VMEM] * len(rest),
        out_specs=[IN_VMEM] * NY,
        out_shape=[jax.ShapeDtypeStruct((width + 16, span), BF)] * NY,
        scratch_shapes=[
            pltpu.VMEM((NY, width, first.shape[2]), BF),
            pltpu.SemaphoreType.DMA((NY,)),
        ],
        compiler_params=pltpu.CompilerParams(vmem_limit_bytes=VMEM_LIMIT),
        cost_estimate=pl.CostEstimate(
            flops=2 * span * features * width * NY,
            bytes_accessed=2 * NY * width * (features + 2 * span),
            transcendentals=0,
        ),
    )(order, rows, squares, got, in_hbm(first), *rest)


def finish_kernel(features, a, b, c, d, cos_ref, sin_ref, keys_ref, values_ref):
    head = keys_ref.shape[1]
    half = head // 2
    total = a[...].astype(F32)
    for part in (b, c, d):
        total = total + part[...].astype(F32)
    squares = total[2 * head : 2 * head + 1] + total[2 * head + 1 : 2 * head + 2]
    scale = lax.rsqrt(squares / features + EPS)
    lower, upper = total[:half] * scale, total[half:head] * scale
    cos, sin = cos_ref[...], sin_ref[...]
    turned = jnp.concatenate([lower * cos - upper * sin, upper * cos + lower * sin], axis=0)
    keys_ref[...] = turned.T.astype(BF)
    values_ref[...] = (total[head : 2 * head] * scale).T.astype(BF)


def finish(features, parts, cos, sin):
    half, span = cos.shape
    return pl.pallas_call(
        functools.partial(finish_kernel, features),
        out_shape=[jax.ShapeDtypeStruct((span, 2 * half), BF)] * 2,
        compiler_params=pltpu.CompilerParams(vmem_limit_bytes=VMEM_LIMIT),
    )(*parts, cos, sin)


def rotary(positions, head):
    half = head // 2
    frequency = THETA ** (-jnp.arange(half, dtype=F32) * 2.0 / head)
    angles = frequency[:, None] * positions[None, :]
    return jnp.cos(angles), jnp.sin(angles)


def body(
    patches,
    slot_page,
    page_start,
    patch_gain,
    patch_bias,
    merge_in,
    merge_out,
    text,
    norm_gain,
    kv_weight,
):
    enc_index, tp_index = lax.axis_index("enc"), lax.axis_index("tp")
    z_index, x_index = enc_index // NX, enc_index % NX
    y_index, core = tp_index // NC, tp_index % NC
    slots, page_rows, _ = patches.shape
    pages = page_start.shape[0]
    span, features = text.shape
    chunk = page_rows // NZ

    scaled = (kv_weight.T.astype(F32) * norm_gain[None, :]).astype(BF)
    depth, wide = merge_out.shape
    quarter = scaled.shape[0]
    first = features - TAILS * wide
    tail = [scaled[:, first + i * wide : first + (i + 1) * wide] for i in range(TAILS)]
    weights = lax.all_gather(
        jnp.concatenate([merge_out, *tail], axis=0), "enc", axis_index_groups=GROUPS_Z
    )
    scaled = scaled[:, :first]

    hidden = hidden_rows(patches, patch_gain, patch_bias, merge_in)
    dealt = lax.all_to_all(hidden, "enc", 0, 0, axis_index_groups=GROUPS_Z, tiled=True)
    pieces = [dealt] + [lax.ppermute(dealt, "enc", shift_x(d)) for d in range(1, NX)]

    scaled, hidden = lax.optimization_barrier((scaled, hidden))
    by_x = [scaled] + [lax.ppermute(scaled, "enc", shift_x(-d)) for d in range(1, NX)]
    kv_first = lax.all_gather(jnp.concatenate(by_x), "enc", axis_index_groups=GROUPS_Z)

    page_ids = jnp.arange(pages, dtype=jnp.int32)
    slot_ids = jnp.arange(slot_page.shape[0], dtype=jnp.int32)
    slot_of = jnp.sum(
        jnp.where(slot_page[None, :] == page_ids[:, None], slot_ids[None, :], 0), axis=1
    )
    holder = slot_of // slots
    place = (x_index - holder % NX) % NX * NZ + holder // NX
    place = (place * slots + slot_of % slots) * chunk
    target = (place[:, None] + jnp.arange(chunk, dtype=jnp.int32)[None, :]).reshape(-1, 1)

    shifted = (y_index + jnp.arange(NY, dtype=jnp.int32)) % NY * NC
    live, away = send_parts(shifted + (1 - core), target, pieces, weights)
    got = lax.ppermute(away, "tp", SWAP_CORE)
    parts = keep_parts(shifted + core, live, weights, got)
    rest, *parts = lax.optimization_barrier((weights[:, depth:], *parts))
    others = [lax.ppermute(parts[d], "tp", shift_y(d)) for d in range(1, NY)]
    after, before = (lax.ppermute(rest, "enc", shift_x(d)) for d in (-1, 1))
    *others, after, before = lax.optimization_barrier((*others, after, before))
    total = parts[0].astype(F32)
    for other in others:
        total = total + other.astype(F32)
    merged = total.astype(BF)
    across = [
        lax.ppermute(after[:, :quarter], "enc", shift_x(-1)),
        lax.ppermute(before[:, quarter:], "enc", shift_x(1)),
    ]
    kv_rest = [
        rest[:, :quarter],
        rest[:, quarter:],
        after[:, :quarter],
        after[:, quarter:],
        *across,
        before[:, :quarter],
        before[:, quarter:],
    ]

    moved = lax.all_to_all(merged, "enc", 0, 0, tiled=True)
    per_block = pages // (NZ * NX)
    moved = moved.reshape(NZ * NX, per_block * chunk, merged.shape[1])
    starts = lax.dynamic_slice_in_dim(page_start, enc_index * per_block, per_block)
    starts = starts - enc_index * span
    rows = (
        jnp.arange(NZ, dtype=jnp.int32)[:, None, None] * chunk
        + starts[None, :, None]
        + jnp.arange(chunk, dtype=jnp.int32)[None, None, :]
    ).reshape(1, -1)
    order = jnp.concatenate([shifted, (jnp.arange(NX, dtype=jnp.int32) + x_index) % NX])
    turn = jnp.arange(2 * NY, dtype=jnp.int32) < NY
    own_heads = order + jnp.where(turn, core, 0)
    other_heads = order + jnp.where(turn, 1 - core, 0)
    mixed, squares, away = project_send(other_heads, rows, moved, text, kv_first, kv_rest)
    got = lax.ppermute(away, "tp", SWAP_CORE)
    sums = project_keep(own_heads, mixed, squares, kv_first, kv_rest, got)
    sums = [sums[0]] + [lax.ppermute(sums[d], "tp", shift_y(d)) for d in range(1, NY)]

    positions = (enc_index * span + jnp.arange(span, dtype=jnp.int32)).astype(F32)
    cos, sin = rotary(positions, kv_first.shape[1] // 2)
    return tuple(finish(features * NY * NC, sums, cos, sin))


def solution(mesh):
    return jax.shard_map(
        body,
        mesh=mesh,
        in_specs=(
            P(("rep", "enc"), None, None),
            P("rep"),
            P("rep"),
            P(),
            P(),
            P(None, "tp"),
            P("tp", "enc"),
            P(("rep", "enc"), "tp"),
            P("tp"),
            P("tp", "enc"),
        ),
        out_specs=(P(("rep", "enc"), "tp"), P(("rep", "enc"), "tp")),
        check_vma=False,
    )
```

time: 160 us -> 144 us (0.900)
  waiting for transfers between devices: 77.8 us -> 56 us
  local copies, waits for them, and re-layouts: 13.2 us -> 3.87 us
  starting transfers between devices: 34.2 us -> 42.5 us
  Pallas kernels: 16.7 us -> 21.9 us
  other arithmetic: 3.04 us -> 5.15 us
    all_to_all x1 -> x0, waiting for transfers between devices: 15.1 us -> none  [body(): lax.all_to_all(sent, 'tp', 0, 0, tiled=True).reshape(kv_parts.shape)]
    all_to_all x1, waiting for transfers between devices: 14.1 us -> 1.45 us  [body(): moved = lax.all_to_all(merged, 'enc', 0, 0, tiled=True)]
    ppermute x6 -> x13, starting transfers between devices: 10.2 us -> 21.6 us  [the longest x3 6.34 us: body(): lax.ppermute(scaled, 'enc', shift_x(-d))]
    ppermute x6 -> x13, waiting for transfers between devices: 15 us -> 22.6 us  [the longest x3 10.2 us: body(): others = [lax.ppermute(parts[d], 'tp', shift_y(d)) for d in range(1, NY)]]
    unnamed x20 -> x12, local copies, waits for them, and re-layouts: 6.82 us -> 1.41 us
    pallas_call x4 -> x5, Pallas kernels: 15.8 us -> 21.1 us  [the longest x1 6.62 us: hidden_rows(): pl.pallas_call(functools.partial(hidden_kernel, slots), in_specs=[pl.Bloc...]
    all_to_all x1 -> x0, starting transfers between devices: 5.09 us -> none  [body(): lax.all_to_all(sent, 'tp', 0, 0, tiled=True).reshape(kv_parts.shape)]
    ppermute x1 -> x2, starting transfers between devices: 2.57 us -> 6.11 us  [body(): got = lax.ppermute(away, 'tp', SWAP_CORE)]
  transfers between devices with their start and end apart: 15 -> 22, of which waited for: 11 -> 12; matrix products, arithmetic and copies ran while one was open for 6% -> 3% of each run, Pallas kernels for 7% -> 10%
where the time goes in v2:
time: 144 us
  waiting for transfers between devices  56 us (39%)
  starting transfers between devices  42.5 us (30%)
  Pallas kernels  21.9 us (15%)
  between operations  14.3 us (10%)
  other arithmetic  5.15 us (4%)
  local copies, waits for them, and re-layouts  3.87 us (3%)
    all_to_all x1, waiting for transfers between devices, body(): lax.all_to_all(hidden, 'enc', 0, 0, axis_index_groups=GROUPS_Z, tiled=True)  15.4 us
    ppermute x3, waiting for transfers between devices, body(): lax.ppermute(dealt, 'enc', shift_x(d))  13.9 us
    ppermute x3, waiting for transfers between devices, body(): others = [lax.ppermute(parts[d], 'tp', shift_y(d)) for d in range(1, NY)]  10.2 us
    all_to_all x1, starting transfers between devices, body(): lax.all_to_all(hidden, 'enc', 0, 0, axis_index_groups=GROUPS_Z, tiled=True)  8.19 us
    pallas_call x1, Pallas kernels, hidden_rows(): pl.pallas_call(functools.partial(hidden_kernel, slots), in_specs=[pl.Bloc...  6.62 us
    ppermute x3, starting transfers between devices, body(): lax.ppermute(scaled, 'enc', shift_x(-d))  6.34 us
    ppermute x1, waiting for transfers between devices, body(): lax.ppermute(before[:, quarter:], 'enc', shift_x(1))  6.28 us
    ppermute x2, starting transfers between devices, body(): got = lax.ppermute(away, 'tp', SWAP_CORE)  6.11 us
  transfers between devices with their start and end apart: 22, of which 12 were waited for; matrix products, arithmetic and copies ran while one was open for 3% of the time, Pallas kernels for 10%

profile of v2, /device:TPU:1, one launch (start us, length us, event | category | flops | bytes accessed | tf_op | source)
XLA Modules:
  0.0 143.8 jit_solution(10447201929307503150)
XLA Ops:
  11.3 6.6 %shard_map.113 = bf16[256,640]{1,0:T(8,128)(2,1)} custom-call(bf16[256,5120]{1,0:T(8,128)(2,1)} %bitcast.17, f32[1280]{0:T(1024)S(1)} %copy-done.1, f32[1280]{0:T(1024)S(1)} %copy-done.2, bf16[5120,640]{1,0:T(8,128)(2,1)} %weight_ref.1), custom_call_target="tpu_custom_call" | custom-call | flops 1677721600 | bytes 9175040 | tf_op jit(solution)/shard_map/pallas_call | solution.py:84
  18.0 3.7 %collective-permute-start.10 = (bf16[64,512]{1,0:T(8,128)(2,1)S(1)}, bf16[64,512]{1,0:T(8,128)(2,1)S(1)}, u32[]{:S(2)}, u32[]{:S(2)}) collective-permute-start(bf16[64,512]{1,0:T(8,128)(2,1)S(1)} %slice.45), channel_id=1, source_target_pairs={{0,16},{8,24},{16,0},{24,8},{32,48},{40,56},{48,32},{56,40},{64,80... | collective-permute-start | bytes 196616 | tf_op jit(solution)/shard_map/ppermute | solution.py:357
  21.9 2.4 %collective-permute-start.9 = (bf16[64,512]{1,0:T(8,128)(2,1)S(1)}, bf16[64,512]{1,0:T(8,128)(2,1)S(1)}, u32[]{:S(2)}, u32[]{:S(2)}) collective-permute-start(bf16[64,512]{1,0:T(8,128)(2,1)S(1)} %slice.45), channel_id=1, source_target_pairs={{0,24},{8,0},{16,8},{24,16},{32,56},{40,32},{48,40},{56,48},{64,88... | collective-permute-start | bytes 196616 | tf_op jit(solution)/shard_map/ppermute | solution.py:357
  24.3 8.2 %all-to-all-start = ((bf16[8,32,640]{2,1,0:T(8,128)(2,1)}), bf16[8,32,640]{2,1,0:T(8,128)(2,1)S(1)}, u32[]{:S(2)}, u32[]{:S(2)}) async-start(bf16[8,32,640]{2,1,0:T(8,128)(2,1)} %bitcast.3), calls=%async_computation | async-start | bytes 655360 | tf_op jit(solution)/shard_map/all_to_all | solution.py:353
  33.5 15.4 %all-to-all-done = bf16[8,32,640]{2,1,0:T(8,128)(2,1)S(1)} async-done(((bf16[8,32,640]{2,1,0:T(8,128)(2,1)}), bf16[8,32,640]{2,1,0:T(8,128)(2,1)S(1)}, u32[]{:S(2)}, u32[]{:S(2)}) %all-to-all-start) | async-done | bytes 327712 | tf_op jit(solution)/shard_map/all_to_all | solution.py:353
  51.9 6.8 %collective-permute-done.b = bf16[256,640]{1,0:T(8,128)(2,1)S(1)} collective-permute-done((bf16[256,640]{1,0:T(8,128)(2,1)S(1)}, bf16[256,640]{1,0:T(8,128)(2,1)S(1)}, u32[]{:S(2)}, u32[]{:S(2)}) %collective-permute-start) | collective-permute-done | bytes 327712 | tf_op jit(solution)/shard_map/ppermute | solution.py:354
  58.7 4.3 %collective-permute-done.1.c = bf16[256,640]{1,0:T(8,128)(2,1)S(1)} collective-permute-done((bf16[256,640]{1,0:T(8,128)(2,1)S(1)}, bf16[256,640]{1,0:T(8,128)(2,1)S(1)}, u32[]{:S(2)}, u32[]{:S(2)}) %collective-permute-start.1) | collective-permute-done | bytes 327712 | tf_op jit(solution)/shard_map/ppermute | solution.py:354
  63.0 2.7 %collective-permute-done.2.d = bf16[256,640]{1,0:T(8,128)(2,1)S(1)} collective-permute-done((bf16[256,640]{1,0:T(8,128)(2,1)S(1)}, bf16[256,640]{1,0:T(8,128)(2,1)S(1)}, u32[]{:S(2)}, u32[]{:S(2)}) %collective-permute-start.2) | collective-permute-done | bytes 327712 | tf_op jit(solution)/shard_map/ppermute | solution.py:354
  65.7 4.2 %shard_map.114 = (bf16[512,640]{1,0:T(8,128)(2,1)S(1)}, bf16[4,512,256]{2,1,0:T(8,128)(2,1)S(1)}) custom-call(s32[4]{0:T(128)S(1)} %broadcast_add_fusion.1.order_ref, s32[512,1]{1,0:T(8,128)S(1)} %add.220.target_ref, bf16[256,640]{1,0:T(8,128)(2,1)S(1)} %bitcast.11, bf16[256,640]{1,0:T(8,128)(2,1)S(1)} %collective-permute-done.b, ...), custom_call_target="tpu_custom_call" | custom-call | flops 1342177280 | bytes 2359296 | tf_op jit(solution)/shard_map/pallas_call | solution.py:139
  70.0 2.5 %collective-permute-start.3 = (bf16[4,512,256]{2,1,0:T(8,128)(2,1)S(1)}, bf16[4,512,256]{2,1,0:T(8,128)(2,1)S(1)}, u32[]{:S(2)}, u32[]{:S(2)}) collective-permute-start(bf16[4,512,256]{2,1,0:T(8,128)(2,1)S(1)} %get-tuple-element.27), channel_id=1, source_target_pairs={{0,1},{1,0},{2,3},{3,2},{4,5},{5,4},{6,7},{7,6},{8,9},{9,8},{10,11... | collective-permute-start | bytes 3145736 | tf_op jit(solution)/shard_map/ppermute | solution.py:372
  74.7 3.8 %shard_map.115 = (bf16[512,256]{1,0:T(8,128)(2,1)S(1)}, bf16[512,256]{1,0:T(8,128)(2,1)S(1)}, bf16[512,256]{1,0:T(8,128)(2,1)S(1)}, bf16[512,256]{1,0:T(8,128)(2,1)S(1)}) custom-call(s32[4]{0:T(128)S(1)} %broadcast_add_fusion.2.order_ref, bf16[512,640]{1,0:T(8,128)(2,1)S(1)} %get-tuple-element.26.live_ref, bf16[8,768,256]{2,1,0:T(8,128)(2,1)} %bitcast.16, ...), custom_call_target="tpu_custom_call" | custom-call | flops 671088640 | bytes 3407872 | tf_op jit(solution)/shard_map/pallas_call | solution.py:168
  78.5 2.1 %collective-permute-start.7 = (bf16[8,128,256]{2,1,0:T(8,128)(2,1)S(1)}, bf16[8,128,256]{2,1,0:T(8,128)(2,1)S(1)}, u32[]{:S(2)}, u32[]{:S(2)}) collective-permute-start(bf16[8,128,256]{2,1,0:T(8,128)(2,1)S(1)} %slice.44), channel_id=1, source_target_pairs={{0,24},{8,0},{16,8},{24,16},{32,56},{40,32},{48,40},{56,48},{64,88... | collective-permute-start | bytes 1572872 | tf_op jit(solution)/shard_map/ppermute | solution.py:376
  82.1 2.3 %collective-permute-start.5 = (bf16[512,256]{1,0:T(8,128)(2,1)S(1)}, bf16[512,256]{1,0:T(8,128)(2,1)S(1)}, u32[]{:S(2)}, u32[]{:S(2)}) collective-permute-start(bf16[512,256]{1,0:T(8,128)(2,1)S(1)} %get-tuple-element.34), channel_id=1, source_target_pairs={{0,4},{1,5},{2,6},{3,7},{4,0},{5,1},{6,2},{7,3},{8,12},{9,13},{10,... | collective-permute-start | bytes 786440 | tf_op jit(solution)/shard_map/ppermute | solution.py:375
  85.5 3.6 %collective-permute-done.4 = bf16[512,256]{1,0:T(8,128)(2,1)S(1)} collective-permute-done((bf16[512,256]{1,0:T(8,128)(2,1)S(1)}, bf16[512,256]{1,0:T(8,128)(2,1)S(1)}, u32[]{:S(2)}, u32[]{:S(2)}) %collective-permute-start.4) | collective-permute-done | bytes 262176 | tf_op jit(solution)/shard_map/ppermute | solution.py:375
  89.2 6.6 %collective-permute-done.5 = bf16[512,256]{1,0:T(8,128)(2,1)S(1)} collective-permute-done((bf16[512,256]{1,0:T(8,128)(2,1)S(1)}, bf16[512,256]{1,0:T(8,128)(2,1)S(1)}, u32[]{:S(2)}, u32[]{:S(2)}) %collective-permute-start.5) | collective-permute-done | bytes 262176 | tf_op jit(solution)/shard_map/ppermute | solution.py:375
  95.8 2.4 %collective-permute-start.12 = (bf16[8,64,256]{2,1,0:T(8,128)(2,1)S(1)}, bf16[8,64,256]{2,1,0:T(8,128)(2,1)S(1)}, u32[]{:S(2)}, u32[]{:S(2)}) collective-permute-start(bf16[8,64,256]{2,1,0:T(8,128)(2,1)S(1)} %get-tuple-element.53.refs_2_), channel_id=1, source_target_pairs={{0,24},{8,0},{16,8},{24,16},{32,56},{40,32},{48,40},{56,48},{64,88... | collective-permute-start | bytes 786440 | tf_op jit(solution)/shard_map/ppermute | solution.py:383
  99.1 3.9 %all-to-all-start.1 = ((bf16[32,16,256]{2,1,0:T(8,128)(2,1)}), bf16[32,16,256]{2,1,0:T(8,128)(2,1)S(1)}, u32[]{:S(2)}, u32[]{:S(2)}) async-start(bf16[32,16,256]{2,1,0:T(8,128)(2,1)} %bitcast.5), calls=%async_computation.1 | async-start | bytes 524288 | tf_op jit(solution)/shard_map/all_to_all | solution.py:396
  105.5 6.3 %collective-permute-done.13.refs_5_ = bf16[8,64,256]{2,1,0:T(8,128)(2,1)S(1)} collective-permute-done((bf16[8,64,256]{2,1,0:T(8,128)(2,1)S(1)}, bf16[8,64,256]{2,1,0:T(8,128)(2,1)S(1)}, u32[]{:S(2)}, u32[]{:S(2)}) %collective-permute-start.13) | collective-permute-done | bytes 262176 | tf_op jit(solution)/shard_map/ppermute | solution.py:384
  113.2 3.2 %shard_map.116 = (bf16[1024,256]{1,0:T(8,128)(2,1)S(1)}, bf16[16,256]{1,0:T(8,128)(2,1)S(1)}, bf16[4,272,256]{2,1,0:T(8,128)(2,1)S(1)}) custom-call(s32[8]{0:T(128)S(1)} %get-tuple-element.60.order_ref, s32[1,128]{1,0:T(1,128)S(1)} %add.201.target_ref, bf16[32,16,256]{2,1,0:T(8,128)(2,1)S(1)} %all-to-all-done.1.moved_ref, bf16[256,1024]{1,0:T(8,128)(2,1)S(1)} %copy-done, ...), custom_call_target="tpu_custom_call" | custom-call | flops 805306368 | bytes 2621440 | tf_op jit(solution)/shard_map/pallas_call | solution.py:237
  116.5 3.6 %collective-permute-start.14 = (bf16[4,272,256]{2,1,0:T(8,128)(2,1)S(1)}, bf16[4,272,256]{2,1,0:T(8,128)(2,1)S(1)}, u32[]{:S(2)}, u32[]{:S(2)}) collective-permute-start(bf16[4,272,256]{2,1,0:T(8,128)(2,1)S(1)} %get-tuple-element.45), channel_id=1, source_target_pairs={{0,1},{1,0},{2,3},{3,2},{4,5},{5,4},{6,7},{7,6},{8,9},{9,8},{10,11... | collective-permute-start | bytes 1671176 | tf_op jit(solution)/shard_map/ppermute | solution.py:411
  121.7 3.2 %shard_map.117 = (bf16[272,256]{1,0:T(8,128)(2,1)S(1)}, bf16[272,256]{1,0:T(8,128)(2,1)S(1)}, bf16[272,256]{1,0:T(8,128)(2,1)S(1)}, bf16[272,256]{1,0:T(8,128)(2,1)S(1)}) custom-call(s32[8]{0:T(128)S(1)} %get-tuple-element.61.order_ref, bf16[1024,256]{1,0:T(8,128)(2,1)S(1)} %get-tuple-element.43.rows_ref, bf16[16,256]{1,0:T(8,128)(2,1)S(1)} %get-tuple-element.44.squares_ref, ...), custom_call_target="tpu_custom_call" | custom-call | flops 536870912 | bytes 3145728 | tf_op jit(solution)/shard_map/pallas_call | solution.py:273
  127.0 2.7 %collective-permute-start.16 = (bf16[272,256]{1,0:T(8,128)(2,1)S(1)}, bf16[272,256]{1,0:T(8,128)(2,1)S(1)}, u32[]{:S(2)}, u32[]{:S(2)}) collective-permute-start(bf16[272,256]{1,0:T(8,128)(2,1)S(1)} %get-tuple-element.48), channel_id=1, source_target_pairs={{0,4},{1,5},{2,6},{3,7},{4,0},{5,1},{6,2},{7,3},{8,12},{9,13},{10,... | collective-permute-start | bytes 417800 | tf_op jit(solution)/shard_map/ppermute | solution.py:413
  130.0 2.2 %collective-permute-done.15.b = bf16[272,256]{1,0:T(8,128)(2,1)S(1)} collective-permute-done((bf16[272,256]{1,0:T(8,128)(2,1)S(1)}, bf16[272,256]{1,0:T(8,128)(2,1)S(1)}, u32[]{:S(2)}, u32[]{:S(2)}) %collective-permute-start.15) | collective-permute-done | bytes 139296 | tf_op jit(solution)/shard_map/ppermute | solution.py:413
  132.3 3.8 %collective-permute-done.16.c = bf16[272,256]{1,0:T(8,128)(2,1)S(1)} collective-permute-done((bf16[272,256]{1,0:T(8,128)(2,1)S(1)}, bf16[272,256]{1,0:T(8,128)(2,1)S(1)}, u32[]{:S(2)}, u32[]{:S(2)}) %collective-permute-start.16) | collective-permute-done | bytes 139296 | tf_op jit(solution)/shard_map/ppermute | solution.py:413
  (66 shorter events, 22.7 us)
Async XLA Ops:
  7.2 58.6 %all-gather.5.cloned.1.call-start = ((), (), s32[]{:S(2)}) async-start(), calls=%async_computation.2 | async-start | bytes 3538944 | tf_op jit(solution)/shard_map/all_gather | solution.py:347
  18.0 14.6 %collective-permute-start.10 = (bf16[64,512]{1,0:T(8,128)(2,1)S(1)}, bf16[64,512]{1,0:T(8,128)(2,1)S(1)}, u32[]{:S(2)}, u32[]{:S(2)}) collective-permute-start(bf16[64,512]{1,0:T(8,128)(2,1)S(1)} %slice.45), channel_id=1, source_target_pairs={{0,16},{8,24},{16,0},{24,8},{32,48},{40,56},{48,32},{56,40},{64,80... | collective-permute-start | bytes 196616 | tf_op jit(solution)/shard_map/ppermute | solution.py:357
  21.6 10.9 %collective-permute-start.11 = (bf16[64,512]{1,0:T(8,128)(2,1)S(1)}, bf16[64,512]{1,0:T(8,128)(2,1)S(1)}, u32[]{:S(2)}, u32[]{:S(2)}) collective-permute-start(bf16[64,512]{1,0:T(8,128)(2,1)S(1)} %slice.45), channel_id=1, source_target_pairs={{0,8},{8,16},{16,24},{24,0},{32,40},{40,48},{48,56},{56,32},{64,72... | collective-permute-start | bytes 196616 | tf_op jit(solution)/shard_map/ppermute | solution.py:357
  21.9 10.6 %collective-permute-start.9 = (bf16[64,512]{1,0:T(8,128)(2,1)S(1)}, bf16[64,512]{1,0:T(8,128)(2,1)S(1)}, u32[]{:S(2)}, u32[]{:S(2)}) collective-permute-start(bf16[64,512]{1,0:T(8,128)(2,1)S(1)} %slice.45), channel_id=1, source_target_pairs={{0,24},{8,0},{16,8},{24,16},{32,56},{40,32},{48,40},{56,48},{64,88... | collective-permute-start | bytes 196616 | tf_op jit(solution)/shard_map/ppermute | solution.py:357
  24.3 24.6 %all-to-all-start = ((bf16[8,32,640]{2,1,0:T(8,128)(2,1)}), bf16[8,32,640]{2,1,0:T(8,128)(2,1)S(1)}, u32[]{:S(2)}, u32[]{:S(2)}) async-start(bf16[8,32,640]{2,1,0:T(8,128)(2,1)} %bitcast.3), calls=%async_computation | async-start | bytes 655360 | tf_op jit(solution)/shard_map/all_to_all | solution.py:353
  32.5 40.0 %copy-start.4 = (s32[64]{0:T(128)S(1)}, s32[64]{0:T(128)}, u32[]{:S(2)}) copy-start(s32[64]{0:T(128)} %param.12) | copy-start | bytes 772
  32.5 73.0 %all-gather.7.cloned.1.call-start = ((), (), s32[]{:S(2)}) async-start(), calls=%async_computation.3 | async-start | bytes 2359296 | tf_op jit(solution)/shard_map/all_gather | solution.py:358
  49.0 9.7 %collective-permute-start = (bf16[256,640]{1,0:T(8,128)(2,1)S(1)}, bf16[256,640]{1,0:T(8,128)(2,1)S(1)}, u32[]{:S(2)}, u32[]{:S(2)}) collective-permute-start(bf16[256,640]{1,0:T(8,128)(2,1)S(1)} %bitcast.8), channel_id=1, source_target_pairs={{0,8},{8,16},{16,24},{24,0},{32,40},{40,48},{48,56},{56,32},{64,72... | collective-permute-start | bytes 983048 | tf_op jit(solution)/shard_map/ppermute | solution.py:354
  49.0 14.0 %collective-permute-start.1 = (bf16[256,640]{1,0:T(8,128)(2,1)S(1)}, bf16[256,640]{1,0:T(8,128)(2,1)S(1)}, u32[]{:S(2)}, u32[]{:S(2)}) collective-permute-start(bf16[256,640]{1,0:T(8,128)(2,1)S(1)} %bitcast.9), channel_id=1, source_target_pairs={{0,16},{8,24},{16,0},{24,8},{32,48},{40,56},{48,32},{56,40},{64,80... | collective-permute-start | bytes 983048 | tf_op jit(solution)/shard_map/ppermute | solution.py:354
  50.2 15.6 %collective-permute-start.2 = (bf16[256,640]{1,0:T(8,128)(2,1)S(1)}, bf16[256,640]{1,0:T(8,128)(2,1)S(1)}, u32[]{:S(2)}, u32[]{:S(2)}) collective-permute-start(bf16[256,640]{1,0:T(8,128)(2,1)S(1)} %bitcast.10), channel_id=1, source_target_pairs={{0,24},{8,0},{16,8},{24,16},{32,56},{40,32},{48,40},{56,48},{64,88... | collective-permute-start | bytes 983048 | tf_op jit(solution)/shard_map/ppermute | solution.py:354
  70.0 4.8 %collective-permute-start.3 = (bf16[4,512,256]{2,1,0:T(8,128)(2,1)S(1)}, bf16[4,512,256]{2,1,0:T(8,128)(2,1)S(1)}, u32[]{:S(2)}, u32[]{:S(2)}) collective-permute-start(bf16[4,512,256]{2,1,0:T(8,128)(2,1)S(1)} %get-tuple-element.27), channel_id=1, source_target_pairs={{0,1},{1,0},{2,3},{3,2},{4,5},{5,4},{6,7},{7,6},{8,9},{9,8},{10,11... | collective-permute-start | bytes 3145736 | tf_op jit(solution)/shard_map/ppermute | solution.py:372
  78.5 34.7 %copy-start = (bf16[256,1024]{1,0:T(8,128)(2,1)S(1)}, bf16[256,1024]{1,0:T(8,128)(2,1)}, u32[]{:S(2)}) copy-start(bf16[256,1024]{1,0:T(8,128)(2,1)} %text_ref.1) | copy-start | bytes 1572868
  78.5 17.2 %collective-permute-start.7 = (bf16[8,128,256]{2,1,0:T(8,128)(2,1)S(1)}, bf16[8,128,256]{2,1,0:T(8,128)(2,1)S(1)}, u32[]{:S(2)}, u32[]{:S(2)}) collective-permute-start(bf16[8,128,256]{2,1,0:T(8,128)(2,1)S(1)} %slice.44), channel_id=1, source_target_pairs={{0,24},{8,0},{16,8},{24,16},{32,56},{40,32},{48,40},{56,48},{64,88... | collective-permute-start | bytes 1572872 | tf_op jit(solution)/shard_map/ppermute | solution.py:376
  80.7 15.1 %collective-permute-start.8 = (bf16[8,128,256]{2,1,0:T(8,128)(2,1)S(1)}, bf16[8,128,256]{2,1,0:T(8,128)(2,1)S(1)}, u32[]{:S(2)}, u32[]{:S(2)}) collective-permute-start(bf16[8,128,256]{2,1,0:T(8,128)(2,1)S(1)} %slice.44), channel_id=1, source_target_pairs={{0,8},{8,16},{16,24},{24,0},{32,40},{40,48},{48,56},{56,32},{64,72... | collective-permute-start | bytes 1572872 | tf_op jit(solution)/shard_map/ppermute | solution.py:376
  80.8 8.4 %collective-permute-start.4 = (bf16[512,256]{1,0:T(8,128)(2,1)S(1)}, bf16[512,256]{1,0:T(8,128)(2,1)S(1)}, u32[]{:S(2)}, u32[]{:S(2)}) collective-permute-start(bf16[512,256]{1,0:T(8,128)(2,1)S(1)} %get-tuple-element.33), channel_id=1, source_target_pairs={{0,2},{1,3},{2,4},{3,5},{4,6},{5,7},{6,0},{7,1},{8,10},{9,11},{10,... | collective-permute-start | bytes 786440 | tf_op jit(solution)/shard_map/ppermute | solution.py:375
  82.1 13.7 %collective-permute-start.5 = (bf16[512,256]{1,0:T(8,128)(2,1)S(1)}, bf16[512,256]{1,0:T(8,128)(2,1)S(1)}, u32[]{:S(2)}, u32[]{:S(2)}) collective-permute-start(bf16[512,256]{1,0:T(8,128)(2,1)S(1)} %get-tuple-element.34), channel_id=1, source_target_pairs={{0,4},{1,5},{2,6},{3,7},{4,0},{5,1},{6,2},{7,3},{8,12},{9,13},{10,... | collective-permute-start | bytes 786440 | tf_op jit(solution)/shard_map/ppermute | solution.py:375
  84.4 11.4 %collective-permute-start.6 = (bf16[512,256]{1,0:T(8,128)(2,1)S(1)}, bf16[512,256]{1,0:T(8,128)(2,1)S(1)}, u32[]{:S(2)}, u32[]{:S(2)}) collective-permute-start(bf16[512,256]{1,0:T(8,128)(2,1)S(1)} %get-tuple-element.35), channel_id=1, source_target_pairs={{0,6},{1,7},{2,0},{3,1},{4,2},{5,3},{6,4},{7,5},{8,14},{9,15},{10,... | collective-permute-start | bytes 786440 | tf_op jit(solution)/shard_map/ppermute | solution.py:375
  95.8 9.7 %collective-permute-start.12 = (bf16[8,64,256]{2,1,0:T(8,128)(2,1)S(1)}, bf16[8,64,256]{2,1,0:T(8,128)(2,1)S(1)}, u32[]{:S(2)}, u32[]{:S(2)}) collective-permute-start(bf16[8,64,256]{2,1,0:T(8,128)(2,1)S(1)} %get-tuple-element.53.refs_2_), channel_id=1, source_target_pairs={{0,24},{8,0},{16,8},{24,16},{32,56},{40,32},{48,40},{56,48},{64,88... | collective-permute-start | bytes 786440 | tf_op jit(solution)/shard_map/ppermute | solution.py:383
  99.1 14.1 %all-to-all-start.1 = ((bf16[32,16,256]{2,1,0:T(8,128)(2,1)}), bf16[32,16,256]{2,1,0:T(8,128)(2,1)S(1)}, u32[]{:S(2)}, u32[]{:S(2)}) async-start(bf16[32,16,256]{2,1,0:T(8,128)(2,1)} %bitcast.5), calls=%async_computation.1 | async-start | bytes 524288 | tf_op jit(solution)/shard_map/all_to_all | solution.py:396
  103.0 8.8 %collective-permute-start.13 = (bf16[8,64,256]{2,1,0:T(8,128)(2,1)S(1)}, bf16[8,64,256]{2,1,0:T(8,128)(2,1)S(1)}, u32[]{:S(2)}, u32[]{:S(2)}) collective-permute-start(bf16[8,64,256]{2,1,0:T(8,128)(2,1)S(1)} %get-tuple-element.51.refs_7_), channel_id=1, source_target_pairs={{0,8},{8,16},{16,24},{24,0},{32,40},{40,48},{48,56},{56,32},{64,72... | collective-permute-start | bytes 786440 | tf_op jit(solution)/shard_map/ppermute | solution.py:384
  116.5 5.2 %collective-permute-start.14 = (bf16[4,272,256]{2,1,0:T(8,128)(2,1)S(1)}, bf16[4,272,256]{2,1,0:T(8,128)(2,1)S(1)}, u32[]{:S(2)}, u32[]{:S(2)}) collective-permute-start(bf16[4,272,256]{2,1,0:T(8,128)(2,1)S(1)} %get-tuple-element.45), channel_id=1, source_target_pairs={{0,1},{1,0},{2,3},{3,2},{4,5},{5,4},{6,7},{7,6},{8,9},{9,8},{10,11... | collective-permute-start | bytes 1671176 | tf_op jit(solution)/shard_map/ppermute | solution.py:411
  124.9 7.4 %collective-permute-start.15 = (bf16[272,256]{1,0:T(8,128)(2,1)S(1)}, bf16[272,256]{1,0:T(8,128)(2,1)S(1)}, u32[]{:S(2)}, u32[]{:S(2)}) collective-permute-start(bf16[272,256]{1,0:T(8,128)(2,1)S(1)} %get-tuple-element.47), channel_id=1, source_target_pairs={{0,2},{1,3},{2,4},{3,5},{4,6},{5,7},{6,0},{7,1},{8,10},{9,11},{10,... | collective-permute-start | bytes 417800 | tf_op jit(solution)/shard_map/ppermute | solution.py:413
  127.0 9.1 %collective-permute-start.16 = (bf16[272,256]{1,0:T(8,128)(2,1)S(1)}, bf16[272,256]{1,0:T(8,128)(2,1)S(1)}, u32[]{:S(2)}, u32[]{:S(2)}) collective-permute-start(bf16[272,256]{1,0:T(8,128)(2,1)S(1)} %get-tuple-element.48), channel_id=1, source_target_pairs={{0,4},{1,5},{2,6},{3,7},{4,0},{5,1},{6,2},{7,3},{8,12},{9,13},{10,... | collective-permute-start | bytes 417800 | tf_op jit(solution)/shard_map/ppermute | solution.py:413
  129.7 6.4 %collective-permute-start.17 = (bf16[272,256]{1,0:T(8,128)(2,1)S(1)}, bf16[272,256]{1,0:T(8,128)(2,1)S(1)}, u32[]{:S(2)}, u32[]{:S(2)}) collective-permute-start(bf16[272,256]{1,0:T(8,128)(2,1)S(1)} %get-tuple-element.49), channel_id=1, source_target_pairs={{0,6},{1,7},{2,0},{3,1},{4,2},{5,3},{6,4},{7,5},{8,14},{9,15},{10,... | collective-permute-start | bytes 417800 | tf_op jit(solution)/shard_map/ppermute | solution.py:413
  (4 other events, 48.9 us)
Sparse Core Ops, SparseCore 0:
  10.1 55.5 all-gather.4
  67.5 36.2 all-gather.6

commit v3 on v2

v3 whole, which is shorter than its diff:
```python
import functools

import jax
import jax.numpy as jnp
from jax import lax
from jax.experimental import pallas as pl
from jax.experimental.pallas import tpu as pltpu
from jax.sharding import PartitionSpec as P

EPS = 1e-06
THETA = 1000000.0
NZ, NX, NY, NC = 8, 4, 4, 2
VMEM_LIMIT = 24 * 1024 * 1024
BF = jnp.bfloat16
F32 = jnp.float32

GROUPS_Z = [[z * NX + x for z in range(NZ)] for x in range(NX)]


def shift_x(d):
    return [(z * NX + x, z * NX + (x + d) % NX) for z in range(NZ) for x in range(NX)]


def shift_z(d):
    return [(z * NX + x, (z + d) % NZ * NX + x) for z in range(NZ) for x in range(NX)]


def shift_y(d):
    return [(y * NC + c, (y + d) % NY * NC + c) for y in range(NY) for c in range(NC)]


SWAP_CORE = [(t, t ^ 1) for t in range(NY * NC)]


IN_VMEM = pl.BlockSpec(memory_space=pltpu.VMEM)
IN_SMEM = pl.BlockSpec(memory_space=pltpu.SMEM)
IN_HBM = pl.BlockSpec(memory_space=pltpu.HBM)


def in_hbm(array):
    return pltpu.with_memory_space_constraint(array, pltpu.HBM)


def hidden_kernel(
    slots,
    patch_ref,
    gain_ref,
    bias_ref,
    weight_ref,
    out_ref,
    patch_buf,
    weight_buf,
    gain_buf,
    bias_buf,
    sems,
):
    width = weight_buf.shape[1]
    groups = weight_buf.shape[0]
    small = (
        pltpu.make_async_copy(gain_ref, gain_buf, sems.at[0, groups]),
        pltpu.make_async_copy(bias_ref, bias_buf, sems.at[1, groups]),
    )
    for copy in small:
        copy.start()
    copies = []
    for i in range(groups):
        part = pl.ds(i * width, width)
        pair = (
            pltpu.make_async_copy(patch_ref.at[:, part], patch_buf.at[i], sems.at[0, i]),
            pltpu.make_async_copy(weight_ref.at[part], weight_buf.at[i], sems.at[1, i]),
        )
        for copy in pair:
            copy.start()
        copies.append(pair)
    for copy in small:
        copy.wait()
    gain, bias = gain_buf[...][None, :], bias_buf[...][None, :]
    total = None
    for i, pair in enumerate(copies):
        pair[0].wait()
        part = patch_buf[i].astype(F32)
        center = jnp.mean(part, axis=-1, keepdims=True)
        part = part - center
        spread = jnp.mean(part * part, axis=-1, keepdims=True)
        normed = (part * lax.rsqrt(spread + EPS) * gain + bias).astype(BF)
        pair[1].wait()
        term = jnp.dot(normed, weight_buf[i], preferred_element_type=F32)
        total = term if total is None else total + term
    total = 0.5 * total * (1.0 + lax.erf(total * 0.7071067811865476))
    rows = total.shape[0] // slots
    chunk = rows // NZ
    pieces = [
        total[slot * rows + z * chunk : slot * rows + (z + 1) * chunk]
        for z in range(NZ)
        for slot in range(slots)
    ]
    out_ref[...] = jnp.concatenate(pieces, axis=0).astype(BF)


def hidden_rows(patches, patch_gain, patch_bias, merge_in):
    slots, rows, feature = patches.shape
    width = patch_gain.shape[0]
    groups = feature // width
    flat = patches.reshape(slots * rows, feature)
    out_width = merge_in.shape[1]
    return pl.pallas_call(
        functools.partial(hidden_kernel, slots),
        in_specs=[IN_HBM] * 4,
        out_specs=IN_VMEM,
        out_shape=jax.ShapeDtypeStruct((slots * rows, out_width), BF),
        scratch_shapes=[
            pltpu.VMEM((groups, slots * rows, width), BF),
            pltpu.VMEM((groups, width, out_width), BF),
            pltpu.VMEM((width,), F32),
            pltpu.VMEM((width,), F32),
            pltpu.SemaphoreType.DMA((2, groups + 1)),
        ],
        compiler_params=pltpu.CompilerParams(vmem_limit_bytes=VMEM_LIMIT),
    )(in_hbm(flat), in_hbm(patch_gain), in_hbm(patch_bias), in_hbm(merge_in))


def live_kernel(target_ref, a, b, c, d, live_ref):
    target = target_ref[...]
    total = None
    for index, piece in enumerate((a, b, c, d)):
        rows = piece.shape[0]
        place = lax.broadcasted_iota(jnp.int32, (target.shape[0], rows), 1) + index * rows
        pick = jnp.where(place == target, 1.0, 0.0).astype(BF)
        term = jnp.dot(pick, piece[...], preferred_element_type=F32)
        total = term if total is None else total + term
    live_ref[...] = total.astype(BF)


def live_rows(target, pieces):
    rows, depth = target.shape[0], pieces[0].shape[1]
    return pl.pallas_call(
        live_kernel,
        out_shape=jax.ShapeDtypeStruct((rows, depth), BF),
        compiler_params=pltpu.CompilerParams(vmem_limit_bytes=VMEM_LIMIT),
    )(target, *pieces)


def fetch_rows(blocks, r, start, rows, target, sems):
    if r == NZ // 2:
        cut = blocks[r].shape[0]
        spans = []
        if start < cut:
            spans.append((blocks[r], start, 0, min(rows, cut - start)))
        if start + rows > cut:
            skip = max(cut - start, 0)
            spans.append((blocks[r + 1], start + skip - cut, skip, rows - skip))
    else:
        spans = [(blocks[r if r < NZ // 2 else r + 1], start, 0, rows)]
    copies = [
        pltpu.make_async_copy(
            ref.at[pl.ds(at, count)], target.at[pl.ds(to, count)], sems.at[index]
        )
        for index, (ref, at, to, count) in enumerate(spans)
    ]
    for copy in copies:
        copy.start()
    return copies


def send_kernel(plan_ref, live_ref, *refs):
    depth = live_ref.shape[1]
    blocks, (out_ref, low_ref, high_ref, buf, sems, kv_sems) = refs[:-6], refs[-6:]
    half = low_ref.shape[1]
    copies = []
    for r in range(NZ):
        copies += fetch_rows(blocks, r, depth, half, low_ref.at[r], kv_sems.at[0, r])
        copies += fetch_rows(blocks, r, depth + half, half, high_ref.at[r], kv_sems.at[1, r])
    for side in range(NC):

        @pl.when(plan_ref[0] == side)
        def _(side=side):
            groups = [
                fetch_rows(blocks, NC * j + side, 0, depth, buf.at[j], sems.at[j])
                for j in range(NY)
            ]
            for j, group in enumerate(groups):
                for copy in group:
                    copy.wait()
                part = jnp.dot(live_ref[...], buf[j], preferred_element_type=F32)
                out_ref[plan_ref[1 + j]] = part.astype(BF)

    for copy in copies:
        copy.wait()


def send_parts(plan, live, blocks):
    rows, depth = live.shape
    total, width = blocks[0].shape
    half = (total - depth) // 2
    return pl.pallas_call(
        send_kernel,
        in_specs=[IN_SMEM, IN_VMEM] + [IN_HBM] * len(blocks),
        out_specs=[IN_VMEM, IN_HBM, IN_HBM],
        out_shape=[jax.ShapeDtypeStruct((NY, rows, width), BF)]
        + [jax.ShapeDtypeStruct((NZ, half, width), BF)] * 2,
        scratch_shapes=[
            pltpu.VMEM((NY, depth, width), BF),
            pltpu.SemaphoreType.DMA((NY, 2)),
            pltpu.SemaphoreType.DMA((2, NZ, 2)),
        ],
        compiler_params=pltpu.CompilerParams(vmem_limit_bytes=VMEM_LIMIT),
    )(plan, live, *[in_hbm(block) for block in blocks])


def keep_kernel(plan_ref, live_ref, got_ref, *refs):
    depth = live_ref.shape[1]
    blocks, out_refs, (buf, sems) = refs[: -NY - 2], refs[-NY - 2 : -2], refs[-2:]
    for side in range(NC):

        @pl.when(plan_ref[0] == side)
        def _(side=side):
            groups = [
                fetch_rows(
                    blocks, NC * j + side, 0, depth, buf.at[plan_ref[1 + j]], sems.at[j]
                )
                for j in range(NY)
            ]
            for group in groups:
                for copy in group:
                    copy.wait()

    for d, out_ref in enumerate(out_refs):
        own = jnp.dot(live_ref[...], buf[d], preferred_element_type=F32).astype(BF)
        out_ref[...] = (own.astype(F32) + got_ref[d].astype(F32)).astype(BF)


def keep_parts(plan, live, got, blocks):
    rows, depth = live.shape
    width = blocks[0].shape[1]
    return pl.pallas_call(
        keep_kernel,
        in_specs=[IN_SMEM, IN_VMEM, IN_VMEM] + [IN_HBM] * len(blocks),
        out_specs=[IN_VMEM] * NY,
        out_shape=[jax.ShapeDtypeStruct((rows, width), BF)] * NY,
        scratch_shapes=[
            pltpu.VMEM((NY, depth, width), BF),
            pltpu.SemaphoreType.DMA((NY, 2)),
        ],
        compiler_params=pltpu.CompilerParams(vmem_limit_bytes=VMEM_LIMIT),
    )(plan, live, got, *[in_hbm(block) for block in blocks])


def put_head(i, order_ref, rows_ref, weight_refs, out_ref, more=None):
    head = order_ref[i]
    rows = weight_refs[0].shape[2] // NX
    lines = []
    for d in range(NX):
        line = [
            ref[head, j * rows : (j + 1) * rows]
            for ref in weight_refs[2 * d : 2 * d + 2]
            for j in range(ref.shape[1] // rows)
        ]
        lines.append(jnp.concatenate(line, axis=1))
    part = jnp.dot(
        jnp.concatenate(lines, axis=0), rows_ref[...], preferred_element_type=F32
    ).astype(BF)
    for d in range(NX):
        place = pl.ds(pl.multiple_of(order_ref[NY + d] * rows, rows), rows)
        piece = part[d * rows : (d + 1) * rows]
        if more is not None:
            piece = (piece.astype(F32) + more[i, place].astype(F32)).astype(BF)
        out_ref[place] = piece


def two_lines(squares):
    squares = jnp.broadcast_to(squares, (16, squares.shape[1]))
    high = squares.astype(BF).astype(F32)
    line = lax.broadcasted_iota(jnp.int32, squares.shape, 0)
    return jnp.where(line == 0, high, jnp.where(line == 1, squares - high, 0.0)).astype(BF)


def project_send_kernel(order_ref, target_ref, moved_ref, text_ref, *refs):
    weight_refs, (rows_ref, squares_ref, out_ref, text_buf, sem) = refs[:-5], refs[-5:]
    text_copy = pltpu.make_async_copy(text_ref, text_buf, sem)
    text_copy.start()
    span = text_ref.shape[0]
    target = target_ref[...]
    place = lax.broadcasted_iota(jnp.int32, (span, target.shape[1]), 0) == target
    pick = jnp.where(place, 1.0, 0.0)
    covered = jnp.sum(pick, axis=1, keepdims=True) > 0.5
    pick = pick.astype(BF)
    width = moved_ref.shape[2]
    squares = jnp.zeros((1, span), F32)
    text_copy.wait()
    for x in range(NX):
        stacked = jnp.concatenate([moved_ref[z * NX + x] for z in range(NZ)], axis=0)
        put = jnp.dot(pick, stacked, preferred_element_type=F32)
        columns = slice(x * width, (x + 1) * width)
        mixed = jnp.where(covered, put, text_buf[:, columns].astype(F32)).T
        rows_ref[columns] = mixed.astype(BF)
        squares += jnp.sum(mixed * mixed, axis=0, keepdims=True)
    squares_ref[...] = two_lines(squares)
    width = weight_refs[0].shape[2]
    for i in range(NY):
        put_head(i, order_ref, rows_ref, weight_refs, out_ref.at[i])
        out_ref[i, width:] = squares_ref[...]


def project_send(order, target, moved, text, weights):
    span, features = text.shape
    width = weights[0].shape[2]
    return pl.pallas_call(
        project_send_kernel,
        in_specs=[IN_SMEM, IN_VMEM, IN_VMEM, IN_HBM] + [IN_VMEM] * len(weights),
        out_specs=[IN_VMEM] * 3,
        out_shape=[
            jax.ShapeDtypeStruct((features, span), BF),
            jax.ShapeDtypeStruct((16, span), BF),
            jax.ShapeDtypeStruct((NY, width + 16, span), BF),
        ],
        scratch_shapes=[pltpu.VMEM((span, features), BF), pltpu.SemaphoreType.DMA(())],
        compiler_params=pltpu.CompilerParams(vmem_limit_bytes=VMEM_LIMIT),
    )(order, target, moved, in_hbm(text), *weights)


def project_keep_kernel(order_ref, rows_ref, squares_ref, got_ref, *refs):
    weight_refs, out_refs = refs[:-NY], refs[-NY:]
    width = weight_refs[0].shape[2]
    for i, out_ref in enumerate(out_refs):
        put_head(i, order_ref, rows_ref, weight_refs, out_ref, got_ref)
        squares = squares_ref[...].astype(F32) + got_ref[i, width:].astype(F32)
        out_ref[width:] = two_lines(squares[0:1] + squares[1:2])


def project_keep(order, rows, squares, got, weights):
    features, span = rows.shape
    width = weights[0].shape[2]
    return pl.pallas_call(
        project_keep_kernel,
        in_specs=[IN_SMEM] + [IN_VMEM] * (3 + len(weights)),
        out_specs=[IN_VMEM] * NY,
        out_shape=[jax.ShapeDtypeStruct((width + 16, span), BF)] * NY,
        compiler_params=pltpu.CompilerParams(vmem_limit_bytes=VMEM_LIMIT),
    )(order, rows, squares, got, *weights)


def finish_kernel(features, a, b, c, d, cos_ref, sin_ref, keys_ref, values_ref):
    head = keys_ref.shape[1]
    half = head // 2
    total = a[...].astype(F32)
    for part in (b, c, d):
        total = total + part[...].astype(F32)
    squares = total[2 * head : 2 * head + 1] + total[2 * head + 1 : 2 * head + 2]
    scale = lax.rsqrt(squares / features + EPS)
    lower, upper = total[:half] * scale, total[half:head] * scale
    cos, sin = cos_ref[...], sin_ref[...]
    turned = jnp.concatenate([lower * cos - upper * sin, upper * cos + lower * sin], axis=0)
    keys_ref[...] = turned.T.astype(BF)
    values_ref[...] = (total[head : 2 * head] * scale).T.astype(BF)


def finish(features, parts, cos, sin):
    half, span = cos.shape
    return pl.pallas_call(
        functools.partial(finish_kernel, features),
        out_shape=[jax.ShapeDtypeStruct((span, 2 * half), BF)] * 2,
        compiler_params=pltpu.CompilerParams(vmem_limit_bytes=VMEM_LIMIT),
    )(*parts, cos, sin)


def rotary(positions, head):
    half = head // 2
    frequency = THETA ** (-jnp.arange(half, dtype=F32) * 2.0 / head)
    angles = frequency[:, None] * positions[None, :]
    return jnp.cos(angles), jnp.sin(angles)


def body(
    patches,
    slot_page,
    page_start,
    patch_gain,
    patch_bias,
    merge_in,
    merge_out,
    text,
    norm_gain,
    kv_weight,
):
    enc_index, tp_index = lax.axis_index("enc"), lax.axis_index("tp")
    z_index, x_index = enc_index // NX, enc_index % NX
    y_index, core = tp_index // NC, tp_index % NC
    slots, page_rows, _ = patches.shape
    pages = page_start.shape[0]
    span, features = text.shape
    chunk = page_rows // NZ

    depth, wide = merge_out.shape
    scaled = (kv_weight.T.astype(F32) * norm_gain[None, :]).astype(BF)
    tails = [scaled[:, i : i + wide] for i in range(0, features, wide)]
    block = jnp.concatenate([merge_out, *tails], axis=0)
    middle = block.shape[0] // 2
    up = [block, lax.ppermute(block, "enc", shift_z(-1))]
    down = [block, lax.ppermute(block, "enc", shift_z(1))]
    hidden = hidden_rows(patches, patch_gain, patch_bias, merge_in)
    hidden, up[1], down[1] = lax.optimization_barrier((hidden, up[1], down[1]))
    for _ in range(NZ // 2 - 2):
        up.append(lax.ppermute(up[-1], "enc", shift_z(-1)))
        down.append(lax.ppermute(down[-1], "enc", shift_z(1)))

    dealt = lax.all_to_all(hidden, "enc", 0, 0, axis_index_groups=GROUPS_Z, tiled=True)
    pieces = [dealt] + [lax.ppermute(dealt, "enc", shift_x(d)) for d in range(1, NX)]
    pieces[1], up[-1], down[-1] = lax.optimization_barrier((pieces[1], up[-1], down[-1]))
    far = [
        lax.ppermute(up[-1][:middle], "enc", shift_z(-1)),
        lax.ppermute(down[-1][middle:], "enc", shift_z(1)),
    ]
    blocks = up + far + down[:0:-1]

    page_ids = jnp.arange(pages, dtype=jnp.int32)
    slot_ids = jnp.arange(slot_page.shape[0], dtype=jnp.int32)
    slot_of = jnp.sum(
        jnp.where(slot_page[None, :] == page_ids[:, None], slot_ids[None, :], 0), axis=1
    )
    holder = slot_of // slots
    place = (x_index - holder % NX) % NX * NZ + holder // NX
    place = (place * slots + slot_of % slots) * chunk
    target = (place[:, None] + jnp.arange(chunk, dtype=jnp.int32)[None, :]).reshape(-1, 1)

    live = live_rows(target, pieces)
    side = (z_index + core) % NC
    steps = jnp.arange(NY, dtype=jnp.int32) * NC

    def plan(side):
        owner = (z_index + steps + side) % NZ // NC
        return jnp.concatenate([side[None], (owner - y_index) % NY])

    away, *kv_own = send_parts(plan(1 - side), live, blocks)
    got = lax.ppermute(away, "tp", SWAP_CORE)
    after = [lax.ppermute(part, "enc", shift_x(-1)) for part in kv_own]
    before = [lax.ppermute(part, "enc", shift_x(1)) for part in kv_own]
    parts = keep_parts(plan(side), live, got, blocks)
    others = [lax.ppermute(parts[d], "tp", shift_y(d)) for d in range(1, NY)]
    opposite = [
        lax.ppermute(after[0], "enc", shift_x(-1)),
        lax.ppermute(before[1], "enc", shift_x(1)),
    ]
    total = parts[0].astype(F32)
    for other in others:
        total = total + other.astype(F32)
    merged = total.astype(BF)
    kv_all = [*kv_own, *after, *opposite, *before]

    moved = lax.all_to_all(merged, "enc", 0, 0, tiled=True)
    per_block = pages // (NZ * NX)
    moved = moved.reshape(NZ * NX, per_block * chunk, merged.shape[1])
    starts = lax.dynamic_slice_in_dim(page_start, enc_index * per_block, per_block)
    starts = starts - enc_index * span
    rows = (
        jnp.arange(NZ, dtype=jnp.int32)[:, None, None] * chunk
        + starts[None, :, None]
        + jnp.arange(chunk, dtype=jnp.int32)[None, None, :]
    ).reshape(1, -1)
    shifted = (y_index + jnp.arange(NY, dtype=jnp.int32)) % NY * NC
    order = jnp.concatenate([shifted - z_index, (jnp.arange(NX, dtype=jnp.int32) + x_index) % NX])
    turn = jnp.arange(2 * NY, dtype=jnp.int32) < NY
    own_heads = jnp.where(turn, (order + core) % NZ, order)
    other_heads = jnp.where(turn, (order + 1 - core) % NZ, order)
    mixed, squares, away = project_send(other_heads, rows, moved, text, kv_all)
    got = lax.ppermute(away, "tp", SWAP_CORE)
    sums = project_keep(own_heads, mixed, squares, got, kv_all)
    sums = [sums[0]] + [lax.ppermute(sums[d], "tp", shift_y(d)) for d in range(1, NY)]

    positions = (enc_index * span + jnp.arange(span, dtype=jnp.int32)).astype(F32)
    cos, sin = rotary(positions, wide // 2)
    return tuple(finish(features * NY * NC, sums, cos, sin))


def solution(mesh):
    return jax.shard_map(
        body,
        mesh=mesh,
        in_specs=(
            P(("rep", "enc"), None, None),
            P("rep"),
            P("rep"),
            P(),
            P(),
            P(None, "tp"),
            P("tp", "enc"),
            P(("rep", "enc"), "tp"),
            P("tp"),
            P("tp", "enc"),
        ),
        out_specs=(P(("rep", "enc"), "tp"), P(("rep", "enc"), "tp")),
        check_vma=False,
    )
```

time: 144 us -> 132 us (0.917)
  between operations: 14.3 us -> 0.86 us
  starting transfers between devices: 42.5 us -> 47.7 us
    ppermute x7 -> x14, waiting for transfers between devices: 6.29 us -> 32.3 us  [the longest x2 8.33 us: body(): up.append(lax.ppermute(up[-1], 'enc', shift_z(-1)))]
    ppermute x3, waiting for transfers between devices: 13.9 us -> 2.07 us  [body(): lax.ppermute(dealt, 'enc', shift_x(d))]
    all_to_all x1, waiting for transfers between devices: 15.4 us -> 3.85 us  [body(): lax.all_to_all(hidden, 'enc', 0, 0, axis_index_groups=GROUPS_Z, tiled=True)]
    all_to_all x1, starting transfers between devices: 8.19 us -> 3.43 us  [body(): lax.all_to_all(hidden, 'enc', 0, 0, axis_index_groups=GROUPS_Z, tiled=True)]
    ppermute x7 -> x14, starting transfers between devices: 12.1 us -> 16.8 us  [the longest x1 6.48 us: body(): up = [block, lax.ppermute(block, 'enc', shift_z(-1))]]
    ppermute x3, waiting for transfers between devices: 10.2 us -> 6.87 us  [body(): others = [lax.ppermute(parts[d], 'tp', shift_y(d)) for d in range(1, NY)]]
    all_to_all x1, starting transfers between devices: 3.87 us -> 6.98 us  [body(): moved = lax.all_to_all(merged, 'enc', 0, 0, tiled=True)]
    concatenate x2, other arithmetic: 2.49 us -> 0.16 us  [plan(): return jnp.concatenate([side[None], (owner - y_index) % NY])]
  transfers between devices with their start and end apart: 22 -> 27, of which waited for: 12 -> 20; matrix products, arithmetic and copies ran while one was open for 3% -> 4% of each run, Pallas kernels for 10% -> 9%
where the time goes in v3:
time: 132 us
  waiting for transfers between devices  54.8 us (42%)
  starting transfers between devices  47.7 us (36%)
  Pallas kernels  21.9 us (17%)
  other arithmetic  3.94 us (3%)
  local copies, waits for them, and re-layouts  2.74 us (2%)
    ppermute x2, waiting for transfers between devices, body(): up.append(lax.ppermute(up[-1], 'enc', shift_z(-1)))  8.33 us
    ppermute x2, starting transfers between devices, body(): got = lax.ppermute(away, 'tp', SWAP_CORE)  7.88 us
    all_to_all x1, starting transfers between devices, body(): moved = lax.all_to_all(merged, 'enc', 0, 0, tiled=True)  6.98 us
    ppermute x3, waiting for transfers between devices, body(): others = [lax.ppermute(parts[d], 'tp', shift_y(d)) for d in range(1, NY)]  6.87 us
    pallas_call x1, Pallas kernels, hidden_rows(): pl.pallas_call(functools.partial(hidden_kernel, slots), in_specs=[IN_HBM]...  6.65 us
    ppermute x1, starting transfers between devices, body(): up = [block, lax.ppermute(block, 'enc', shift_z(-1))]  6.48 us
    ppermute x3, waiting for transfers between devices, body(): lax.ppermute(sums[d], 'tp', shift_y(d))  5.27 us
    ppermute x1, waiting for transfers between devices, body(): lax.ppermute(after[0], 'enc', shift_x(-1))  4.95 us
  transfers between devices with their start and end apart: 27, of which 20 were waited for; matrix products, arithmetic and copies ran while one was open for 4% of the time, Pallas kernels for 9%

profile of v3, /device:TPU:1, one launch (start us, length us, event | category | flops | bytes accessed | tf_op | source)
XLA Modules:
  0.0 131.9 jit_solution(14453904829205922977)
XLA Ops:
  2.6 6.5 %collective-permute-start = (bf16[896,256]{1,0:T(8,128)(2,1)S(1)}, bf16[896,256]{1,0:T(8,128)(2,1)S(1)}, u32[]{:S(2)}, u32[]{:S(2)}) collective-permute-start(bf16[896,256]{1,0:T(8,128)(2,1)S(1)} %slice_dynamic-update-slice_fusion.refs_0_), channel_id=1, source_target_pairs={{0,224},{8,232},{16,240},{24,248},{32,0},{40,8},{48,16},{56,24},{6... | collective-permute-start | bytes 1376264 | tf_op jit(solution)/shard_map/ppermute | solution.py:398
  9.1 6.7 %shard_map.113 = bf16[256,640]{1,0:T(8,128)(2,1)} custom-call(bf16[256,5120]{1,0:T(8,128)(2,1)} %bitcast.12, f32[1280]{0:T(1024)} %gain_ref.1, f32[1280]{0:T(1024)} %bias_ref.1, bf16[5120,640]{1,0:T(8,128)(2,1)} %weight_ref.1), custom_call_target="tpu_custom_call" | custom-call | tf_op jit(solution)/shard_map/pallas_call | solution.py:106
  15.8 2.5 %collective-permute-done.refs_1_ = bf16[896,256]{1,0:T(8,128)(2,1)S(1)} collective-permute-done((bf16[896,256]{1,0:T(8,128)(2,1)S(1)}, bf16[896,256]{1,0:T(8,128)(2,1)S(1)}, u32[]{:S(2)}, u32[]{:S(2)}) %collective-permute-start) | collective-permute-done | bytes 458784 | tf_op jit(solution)/shard_map/ppermute | solution.py:398
  18.3 3.1 %collective-permute-done.1.refs_8_ = bf16[896,256]{1,0:T(8,128)(2,1)S(1)} collective-permute-done((bf16[896,256]{1,0:T(8,128)(2,1)S(1)}, bf16[896,256]{1,0:T(8,128)(2,1)S(1)}, u32[]{:S(2)}, u32[]{:S(2)}) %collective-permute-start.1) | collective-permute-done | bytes 458784 | tf_op jit(solution)/shard_map/ppermute | solution.py:399
  22.9 3.4 %all-to-all-start = ((bf16[8,32,640]{2,1,0:T(8,128)(2,1)}), bf16[8,32,640]{2,1,0:T(8,128)(2,1)S(1)}, u32[]{:S(2)}, u32[]{:S(2)}) async-start(bf16[8,32,640]{2,1,0:T(8,128)(2,1)} %bitcast.3), calls=%async_computation | async-start | bytes 655360 | tf_op jit(solution)/shard_map/all_to_all | solution.py:406
  26.3 5.3 %collective-permute-done.3.refs_2_ = bf16[896,256]{1,0:T(8,128)(2,1)} collective-permute-done((bf16[896,256]{1,0:T(8,128)(2,1)S(1)}, bf16[896,256]{1,0:T(8,128)(2,1)}, u32[]{:S(2)}, u32[]{:S(2)}) %collective-permute-start.3) | collective-permute-done | bytes 458784 | tf_op jit(solution)/shard_map/ppermute | solution.py:403
  34.4 3.8 %all-to-all-done = bf16[8,32,640]{2,1,0:T(8,128)(2,1)S(1)} async-done(((bf16[8,32,640]{2,1,0:T(8,128)(2,1)}), bf16[8,32,640]{2,1,0:T(8,128)(2,1)S(1)}, u32[]{:S(2)}, u32[]{:S(2)}) %all-to-all-start) | async-done | bytes 327712 | tf_op jit(solution)/shard_map/all_to_all | solution.py:406
  39.7 2.5 %collective-permute-start.7 = (bf16[256,640]{1,0:T(8,128)(2,1)S(1)}, bf16[256,640]{1,0:T(8,128)(2,1)S(1)}, u32[]{:S(2)}, u32[]{:S(2)}) collective-permute-start(bf16[256,640]{1,0:T(8,128)(2,1)S(1)} %bitcast.9), channel_id=1, source_target_pairs={{0,16},{8,24},{16,0},{24,8},{32,48},{40,56},{48,32},{56,40},{64,80... | collective-permute-start | bytes 983048 | tf_op jit(solution)/shard_map/ppermute | solution.py:407
  45.4 3.0 %collective-permute-done.4.refs_3_ = bf16[896,256]{1,0:T(8,128)(2,1)S(1)} collective-permute-done((bf16[896,256]{1,0:T(8,128)(2,1)}, bf16[896,256]{1,0:T(8,128)(2,1)S(1)}, u32[]{:S(2)}, u32[]{:S(2)}) %collective-permute-start.4) | collective-permute-done | bytes 458784 | tf_op jit(solution)/shard_map/ppermute | solution.py:403
  55.2 2.6 %collective-permute-done.10.refs_5_ = bf16[448,256]{1,0:T(8,128)(2,1)} collective-permute-done((bf16[448,256]{1,0:T(8,128)(2,1)}, bf16[448,256]{1,0:T(8,128)(2,1)}, u32[]{:S(2)}, u32[]{:S(2)}) %collective-permute-start.10) | collective-permute-done | bytes 229408 | tf_op jit(solution)/shard_map/ppermute | solution.py:411
  57.8 4.6 %shard_map.115 = (bf16[4,512,256]{2,1,0:T(8,128)(2,1)S(1)}, bf16[8,128,256]{2,1,0:T(8,128)(2,1)S(1)}, bf16[8,128,256]{2,1,0:T(8,128)(2,1)S(1)}) custom-call(s32[5]{0:T(128)S(1)} %pad_add_fusion.2.plan_ref, bf16[512,640]{1,0:T(8,128)(2,1)S(1)} %shard_map.114.live_ref, bf16[896,256]{1,0:T(8,128)(2,1)} %copy-done, bf16[896,256]{1,0:T(8,128)(2,1)} %copy-done.3, ...), custom_call_target="tpu_custom_call" | custom-call | tf_op jit(solution)/shard_map/pallas_call | solution.py:195
  62.4 5.5 %collective-permute-start.11 = (bf16[4,512,256]{2,1,0:T(8,128)(2,1)S(1)}, bf16[4,512,256]{2,1,0:T(8,128)(2,1)S(1)}, u32[]{:S(2)}, u32[]{:S(2)}) collective-permute-start(bf16[4,512,256]{2,1,0:T(8,128)(2,1)S(1)} %get-tuple-element.28), channel_id=1, source_target_pairs={{0,1},{1,0},{2,3},{3,2},{4,5},{5,4},{6,7},{7,6},{8,9},{9,8},{10,11... | collective-permute-start | bytes 3145736 | tf_op jit(solution)/shard_map/ppermute | solution.py:434
  70.1 3.7 %shard_map.116 = (bf16[512,256]{1,0:T(8,128)(2,1)S(1)}, bf16[512,256]{1,0:T(8,128)(2,1)}, bf16[512,256]{1,0:T(8,128)(2,1)}, bf16[512,256]{1,0:T(8,128)(2,1)}) custom-call(s32[5]{0:T(128)S(1)} %pad_add_fusion.1.plan_ref, bf16[512,640]{1,0:T(8,128)(2,1)S(1)} %shard_map.114.live_ref, bf16[4,512,256]{2,1,0:T(8,128)(2,1)S(1)} %collective-permute-done.11.got_ref, ...), custom_call_target="tpu_custom_call" | custom-call | tf_op jit(solution)/shard_map/pallas_call | solution.py:235
  73.8 2.8 %collective-permute-start.14 = (bf16[512,256]{1,0:T(8,128)(2,1)}, bf16[512,256]{1,0:T(8,128)(2,1)}, u32[]{:S(2)}, u32[]{:S(2)}) collective-permute-start(bf16[512,256]{1,0:T(8,128)(2,1)} %get-tuple-element.32), channel_id=1, source_target_pairs={{0,6},{1,7},{2,0},{3,1},{4,2},{5,3},{6,4},{7,5},{8,14},{9,15},{10,... | collective-permute-start | bytes 786440 | tf_op jit(solution)/shard_map/ppermute | solution.py:438
  77.8 3.7 %collective-permute-done.15.refs_2_ = bf16[8,128,256]{2,1,0:T(8,128)(2,1)S(1)} collective-permute-done((bf16[8,128,256]{2,1,0:T(8,128)(2,1)S(1)}, bf16[8,128,256]{2,1,0:T(8,128)(2,1)S(1)}, u32[]{:S(2)}, u32[]{:S(2)}) %collective-permute-start.15) | collective-permute-done | bytes 524320 | tf_op jit(solution)/shard_map/ppermute | solution.py:435
  81.5 2.5 %collective-permute-start.16 = (bf16[8,128,256]{2,1,0:T(8,128)(2,1)S(1)}, bf16[8,128,256]{2,1,0:T(8,128)(2,1)S(1)}, u32[]{:S(2)}, u32[]{:S(2)}) collective-permute-start(bf16[8,128,256]{2,1,0:T(8,128)(2,1)S(1)} %get-tuple-element.34.refs_1_), channel_id=1, source_target_pairs={{0,24},{8,0},{16,8},{24,16},{32,56},{40,32},{48,40},{56,48},{64,88... | collective-permute-start | bytes 1572872 | tf_op jit(solution)/shard_map/ppermute | solution.py:435
  84.0 3.8 %collective-permute-done.14 = bf16[512,256]{1,0:T(8,128)(2,1)} collective-permute-done((bf16[512,256]{1,0:T(8,128)(2,1)}, bf16[512,256]{1,0:T(8,128)(2,1)}, u32[]{:S(2)}, u32[]{:S(2)}) %collective-permute-start.14) | collective-permute-done | bytes 262176 | tf_op jit(solution)/shard_map/ppermute | solution.py:438
  89.2 3.1 %collective-permute-done.12 = bf16[512,256]{1,0:T(8,128)(2,1)} collective-permute-done((bf16[512,256]{1,0:T(8,128)(2,1)}, bf16[512,256]{1,0:T(8,128)(2,1)}, u32[]{:S(2)}, u32[]{:S(2)}) %collective-permute-start.12) | collective-permute-done | bytes 262176 | tf_op jit(solution)/shard_map/ppermute | solution.py:438
  94.2 7.0 %all-to-all-start.1 = ((bf16[32,16,256]{2,1,0:T(8,128)(2,1)}), bf16[32,16,256]{2,1,0:T(8,128)(2,1)S(1)}, u32[]{:S(2)}, u32[]{:S(2)}) async-start(bf16[32,16,256]{2,1,0:T(8,128)(2,1)} %bitcast.13), calls=%async_computation.1 | async-start | bytes 524288 | tf_op jit(solution)/shard_map/all_to_all | solution.py:449
  101.6 5.0 %collective-permute-done.17.refs_4_ = bf16[8,128,256]{2,1,0:T(8,128)(2,1)} collective-permute-done((bf16[8,128,256]{2,1,0:T(8,128)(2,1)S(1)}, bf16[8,128,256]{2,1,0:T(8,128)(2,1)}, u32[]{:S(2)}, u32[]{:S(2)}) %collective-permute-start.17) | collective-permute-done | bytes 524320 | tf_op jit(solution)/shard_map/ppermute | solution.py:440
  106.5 3.8 %collective-permute-done.19.refs_5_ = bf16[8,128,256]{2,1,0:T(8,128)(2,1)} collective-permute-done((bf16[8,128,256]{2,1,0:T(8,128)(2,1)S(1)}, bf16[8,128,256]{2,1,0:T(8,128)(2,1)}, u32[]{:S(2)}, u32[]{:S(2)}) %collective-permute-start.19) | collective-permute-done | bytes 524320 | tf_op jit(solution)/shard_map/ppermute | solution.py:441
  112.5 3.3 %shard_map.117 = (bf16[1024,256]{1,0:T(8,128)(2,1)S(1)}, bf16[16,256]{1,0:T(8,128)(2,1)S(1)}, bf16[4,272,256]{2,1,0:T(8,128)(2,1)S(1)}) custom-call(s32[8]{0:T(128)S(1)} %get-tuple-element.44.order_ref, s32[1,128]{1,0:T(1,128)S(1)} %add.248.target_ref, bf16[32,16,256]{2,1,0:T(8,128)(2,1)S(1)} %all-to-all-done.1.moved_ref, bf16[256,1024]{1,0:T(8,128)(2,1)} %text_ref.1, ...), custom_call_target="tpu_custom_call" | custom-call | tf_op jit(solution)/shard_map/pallas_call | solution.py:307
  121.8 2.9 %collective-permute-start.23 = (bf16[272,256]{1,0:T(8,128)(2,1)S(1)}, bf16[272,256]{1,0:T(8,128)(2,1)S(1)}, u32[]{:S(2)}, u32[]{:S(2)}) collective-permute-start(bf16[272,256]{1,0:T(8,128)(2,1)S(1)} %get-tuple-element.40), channel_id=1, source_target_pairs={{0,4},{1,5},{2,6},{3,7},{4,0},{5,1},{6,2},{7,3},{8,12},{9,13},{10,... | collective-permute-start | bytes 417800 | tf_op jit(solution)/shard_map/ppermute | solution.py:467
  127.8 3.3 %collective-permute-done.23.c = bf16[272,256]{1,0:T(8,128)(2,1)S(1)} collective-permute-done((bf16[272,256]{1,0:T(8,128)(2,1)S(1)}, bf16[272,256]{1,0:T(8,128)(2,1)S(1)}, u32[]{:S(2)}, u32[]{:S(2)}) %collective-permute-start.23) | collective-permute-done | bytes 139296 | tf_op jit(solution)/shard_map/ppermute | solution.py:467
  (78 shorter events, 36.9 us)
Async XLA Ops:
  2.6 15.7 %collective-permute-start = (bf16[896,256]{1,0:T(8,128)(2,1)S(1)}, bf16[896,256]{1,0:T(8,128)(2,1)S(1)}, u32[]{:S(2)}, u32[]{:S(2)}) collective-permute-start(bf16[896,256]{1,0:T(8,128)(2,1)S(1)} %slice_dynamic-update-slice_fusion.refs_0_), channel_id=1, source_target_pairs={{0,224},{8,232},{16,240},{24,248},{32,0},{40,8},{48,16},{56,24},{6... | collective-permute-start | bytes 1376264 | tf_op jit(solution)/shard_map/ppermute | solution.py:398
  9.1 12.3 %collective-permute-start.1 = (bf16[896,256]{1,0:T(8,128)(2,1)S(1)}, bf16[896,256]{1,0:T(8,128)(2,1)S(1)}, u32[]{:S(2)}, u32[]{:S(2)}) collective-permute-start(bf16[896,256]{1,0:T(8,128)(2,1)S(1)} %slice_dynamic-update-slice_fusion.refs_0_), channel_id=1, source_target_pairs={{0,32},{8,40},{16,48},{24,56},{32,64},{40,72},{48,80},{56,88},{64,... | collective-permute-start | bytes 1376264 | tf_op jit(solution)/shard_map/ppermute | solution.py:399
  21.4 10.3 %collective-permute-start.3 = (bf16[896,256]{1,0:T(8,128)(2,1)S(1)}, bf16[896,256]{1,0:T(8,128)(2,1)}, u32[]{:S(2)}, u32[]{:S(2)}) collective-permute-start(bf16[896,256]{1,0:T(8,128)(2,1)S(1)} %collective-permute-done.refs_1_), channel_id=1, source_target_pairs={{0,224},{8,232},{16,240},{24,248},{32,0},{40,8},{48,16},{56,24},{6... | collective-permute-start | bytes 1376264 | tf_op jit(solution)/shard_map/ppermute | solution.py:403
  21.8 12.6 %collective-permute-start.5 = (bf16[896,256]{1,0:T(8,128)(2,1)S(1)}, bf16[896,256]{1,0:T(8,128)(2,1)}, u32[]{:S(2)}, u32[]{:S(2)}) collective-permute-start(bf16[896,256]{1,0:T(8,128)(2,1)S(1)} %collective-permute-done.1.refs_8_), channel_id=1, source_target_pairs={{0,32},{8,40},{16,48},{24,56},{32,64},{40,72},{48,80},{56,88},{64,... | collective-permute-start | bytes 1376264 | tf_op jit(solution)/shard_map/ppermute | solution.py:404
  22.9 15.4 %all-to-all-start = ((bf16[8,32,640]{2,1,0:T(8,128)(2,1)}), bf16[8,32,640]{2,1,0:T(8,128)(2,1)S(1)}, u32[]{:S(2)}, u32[]{:S(2)}) async-start(bf16[8,32,640]{2,1,0:T(8,128)(2,1)} %bitcast.3), calls=%async_computation | async-start | bytes 655360 | tf_op jit(solution)/shard_map/all_to_all | solution.py:406
  31.7 16.7 %collective-permute-start.4 = (bf16[896,256]{1,0:T(8,128)(2,1)}, bf16[896,256]{1,0:T(8,128)(2,1)S(1)}, u32[]{:S(2)}, u32[]{:S(2)}) collective-permute-start(bf16[896,256]{1,0:T(8,128)(2,1)} %collective-permute-done.3.refs_2_), channel_id=1, source_target_pairs={{0,224},{8,232},{16,240},{24,248},{32,0},{40,8},{48,16},{56,24},{6... | collective-permute-start | bytes 1376264 | tf_op jit(solution)/shard_map/ppermute | solution.py:403
  34.4 14.7 %collective-permute-start.6 = (bf16[896,256]{1,0:T(8,128)(2,1)}, bf16[896,256]{1,0:T(8,128)(2,1)S(1)}, u32[]{:S(2)}, u32[]{:S(2)}) collective-permute-start(bf16[896,256]{1,0:T(8,128)(2,1)} %collective-permute-done.5.refs_7_), channel_id=1, source_target_pairs={{0,32},{8,40},{16,48},{24,56},{32,64},{40,72},{48,80},{56,88},{64,... | collective-permute-start | bytes 1376264 | tf_op jit(solution)/shard_map/ppermute | solution.py:404
  38.3 7.1 %collective-permute-start.2 = (bf16[256,640]{1,0:T(8,128)(2,1)S(1)}, bf16[256,640]{1,0:T(8,128)(2,1)S(1)}, u32[]{:S(2)}, u32[]{:S(2)}) collective-permute-start(bf16[256,640]{1,0:T(8,128)(2,1)S(1)} %bitcast.8), channel_id=1, source_target_pairs={{0,8},{8,16},{16,24},{24,0},{32,40},{40,48},{48,56},{56,32},{64,72... | collective-permute-start | bytes 983048 | tf_op jit(solution)/shard_map/ppermute | solution.py:407
  39.7 12.7 %collective-permute-start.7 = (bf16[256,640]{1,0:T(8,128)(2,1)S(1)}, bf16[256,640]{1,0:T(8,128)(2,1)S(1)}, u32[]{:S(2)}, u32[]{:S(2)}) collective-permute-start(bf16[256,640]{1,0:T(8,128)(2,1)S(1)} %bitcast.9), channel_id=1, source_target_pairs={{0,16},{8,24},{16,0},{24,8},{32,48},{40,56},{48,32},{56,40},{64,80... | collective-permute-start | bytes 983048 | tf_op jit(solution)/shard_map/ppermute | solution.py:407
  42.2 10.2 %collective-permute-start.8 = (bf16[256,640]{1,0:T(8,128)(2,1)S(1)}, bf16[256,640]{1,0:T(8,128)(2,1)S(1)}, u32[]{:S(2)}, u32[]{:S(2)}) collective-permute-start(bf16[256,640]{1,0:T(8,128)(2,1)S(1)} %bitcast.10), channel_id=1, source_target_pairs={{0,24},{8,0},{16,8},{24,16},{32,56},{40,32},{48,40},{56,48},{64,88... | collective-permute-start | bytes 983048 | tf_op jit(solution)/shard_map/ppermute | solution.py:407
  51.2 6.6 %collective-permute-start.10 = (bf16[448,256]{1,0:T(8,128)(2,1)}, bf16[448,256]{1,0:T(8,128)(2,1)}, u32[]{:S(2)}, u32[]{:S(2)}) collective-permute-start(bf16[448,256]{1,0:T(8,128)(2,1)} %slice.23), channel_id=1, source_target_pairs={{0,32},{8,40},{16,48},{24,56},{32,64},{40,72},{48,80},{56,88},{64,... | collective-permute-start | bytes 688136 | tf_op jit(solution)/shard_map/ppermute | solution.py:411
  62.4 7.8 %collective-permute-start.11 = (bf16[4,512,256]{2,1,0:T(8,128)(2,1)S(1)}, bf16[4,512,256]{2,1,0:T(8,128)(2,1)S(1)}, u32[]{:S(2)}, u32[]{:S(2)}) collective-permute-start(bf16[4,512,256]{2,1,0:T(8,128)(2,1)S(1)} %get-tuple-element.28), channel_id=1, source_target_pairs={{0,1},{1,0},{2,3},{3,2},{4,5},{5,4},{6,7},{7,6},{8,9},{9,8},{10,11... | collective-permute-start | bytes 3145736 | tf_op jit(solution)/shard_map/ppermute | solution.py:434
  67.9 13.6 %collective-permute-start.15 = (bf16[8,128,256]{2,1,0:T(8,128)(2,1)S(1)}, bf16[8,128,256]{2,1,0:T(8,128)(2,1)S(1)}, u32[]{:S(2)}, u32[]{:S(2)}) collective-permute-start(bf16[8,128,256]{2,1,0:T(8,128)(2,1)S(1)} %get-tuple-element.33.refs_0_), channel_id=1, source_target_pairs={{0,24},{8,0},{16,8},{24,16},{32,56},{40,32},{48,40},{56,48},{64,88... | collective-permute-start | bytes 1572872 | tf_op jit(solution)/shard_map/ppermute | solution.py:435
  69.3 14.7 %collective-permute-start.18 = (bf16[8,128,256]{2,1,0:T(8,128)(2,1)S(1)}, bf16[8,128,256]{2,1,0:T(8,128)(2,1)S(1)}, u32[]{:S(2)}, u32[]{:S(2)}) collective-permute-start(bf16[8,128,256]{2,1,0:T(8,128)(2,1)S(1)} %get-tuple-element.34.refs_1_), channel_id=1, source_target_pairs={{0,8},{8,16},{16,24},{24,0},{32,40},{40,48},{48,56},{56,32},{64,72... | collective-permute-start | bytes 1572872 | tf_op jit(solution)/shard_map/ppermute | solution.py:436
  73.8 13.9 %collective-permute-start.14 = (bf16[512,256]{1,0:T(8,128)(2,1)}, bf16[512,256]{1,0:T(8,128)(2,1)}, u32[]{:S(2)}, u32[]{:S(2)}) collective-permute-start(bf16[512,256]{1,0:T(8,128)(2,1)} %get-tuple-element.32), channel_id=1, source_target_pairs={{0,6},{1,7},{2,0},{3,1},{4,2},{5,3},{6,4},{7,5},{8,14},{9,15},{10,... | collective-permute-start | bytes 786440 | tf_op jit(solution)/shard_map/ppermute | solution.py:438
  76.6 11.1 %collective-permute-start.13 = (bf16[512,256]{1,0:T(8,128)(2,1)}, bf16[512,256]{1,0:T(8,128)(2,1)}, u32[]{:S(2)}, u32[]{:S(2)}) collective-permute-start(bf16[512,256]{1,0:T(8,128)(2,1)} %get-tuple-element.31), channel_id=1, source_target_pairs={{0,4},{1,5},{2,6},{3,7},{4,0},{5,1},{6,2},{7,3},{8,12},{9,13},{10,... | collective-permute-start | bytes 786440 | tf_op jit(solution)/shard_map/ppermute | solution.py:438
  77.0 15.3 %collective-permute-start.12 = (bf16[512,256]{1,0:T(8,128)(2,1)}, bf16[512,256]{1,0:T(8,128)(2,1)}, u32[]{:S(2)}, u32[]{:S(2)}) collective-permute-start(bf16[512,256]{1,0:T(8,128)(2,1)} %get-tuple-element.30), channel_id=1, source_target_pairs={{0,2},{1,3},{2,4},{3,5},{4,6},{5,7},{6,0},{7,1},{8,10},{9,11},{10,... | collective-permute-start | bytes 786440 | tf_op jit(solution)/shard_map/ppermute | solution.py:438
  81.5 20.1 %collective-permute-start.16 = (bf16[8,128,256]{2,1,0:T(8,128)(2,1)S(1)}, bf16[8,128,256]{2,1,0:T(8,128)(2,1)S(1)}, u32[]{:S(2)}, u32[]{:S(2)}) collective-permute-start(bf16[8,128,256]{2,1,0:T(8,128)(2,1)S(1)} %get-tuple-element.34.refs_1_), channel_id=1, source_target_pairs={{0,24},{8,0},{16,8},{24,16},{32,56},{40,32},{48,40},{56,48},{64,88... | collective-permute-start | bytes 1572872 | tf_op jit(solution)/shard_map/ppermute | solution.py:435
  84.0 17.6 %collective-permute-start.20 = (bf16[8,128,256]{2,1,0:T(8,128)(2,1)S(1)}, bf16[8,128,256]{2,1,0:T(8,128)(2,1)S(1)}, u32[]{:S(2)}, u32[]{:S(2)}) collective-permute-start(bf16[8,128,256]{2,1,0:T(8,128)(2,1)S(1)} %get-tuple-element.33.refs_0_), channel_id=1, source_target_pairs={{0,8},{8,16},{16,24},{24,0},{32,40},{40,48},{48,56},{56,32},{64,72... | collective-permute-start | bytes 1572872 | tf_op jit(solution)/shard_map/ppermute | solution.py:436
  87.8 18.8 %collective-permute-start.17 = (bf16[8,128,256]{2,1,0:T(8,128)(2,1)S(1)}, bf16[8,128,256]{2,1,0:T(8,128)(2,1)}, u32[]{:S(2)}, u32[]{:S(2)}) collective-permute-start(bf16[8,128,256]{2,1,0:T(8,128)(2,1)S(1)} %collective-permute-done.15.refs_2_), channel_id=1, source_target_pairs={{0,24},{8,0},{16,8},{24,16},{32,56},{40,32},{48,40},{56,48},{64,88... | collective-permute-start | bytes 1572872 | tf_op jit(solution)/shard_map/ppermute | solution.py:440
  87.8 22.6 %collective-permute-start.19 = (bf16[8,128,256]{2,1,0:T(8,128)(2,1)S(1)}, bf16[8,128,256]{2,1,0:T(8,128)(2,1)}, u32[]{:S(2)}, u32[]{:S(2)}) collective-permute-start(bf16[8,128,256]{2,1,0:T(8,128)(2,1)S(1)} %collective-permute-done.18.refs_7_), channel_id=1, source_target_pairs={{0,8},{8,16},{16,24},{24,0},{32,40},{40,48},{48,56},{56,32},{64,72... | collective-permute-start | bytes 1572872 | tf_op jit(solution)/shard_map/ppermute | solution.py:441
  94.2 18.2 %all-to-all-start.1 = ((bf16[32,16,256]{2,1,0:T(8,128)(2,1)}), bf16[32,16,256]{2,1,0:T(8,128)(2,1)S(1)}, u32[]{:S(2)}, u32[]{:S(2)}) async-start(bf16[32,16,256]{2,1,0:T(8,128)(2,1)} %bitcast.13), calls=%async_computation.1 | async-start | bytes 524288 | tf_op jit(solution)/shard_map/all_to_all | solution.py:449
  121.8 9.3 %collective-permute-start.23 = (bf16[272,256]{1,0:T(8,128)(2,1)S(1)}, bf16[272,256]{1,0:T(8,128)(2,1)S(1)}, u32[]{:S(2)}, u32[]{:S(2)}) collective-permute-start(bf16[272,256]{1,0:T(8,128)(2,1)S(1)} %get-tuple-element.40), channel_id=1, source_target_pairs={{0,4},{1,5},{2,6},{3,7},{4,0},{5,1},{6,2},{7,3},{8,12},{9,13},{10,... | collective-permute-start | bytes 417800 | tf_op jit(solution)/shard_map/ppermute | solution.py:467
  124.7 6.4 %collective-permute-start.24 = (bf16[272,256]{1,0:T(8,128)(2,1)S(1)}, bf16[272,256]{1,0:T(8,128)(2,1)S(1)}, u32[]{:S(2)}, u32[]{:S(2)}) collective-permute-start(bf16[272,256]{1,0:T(8,128)(2,1)S(1)} %get-tuple-element.41), channel_id=1, source_target_pairs={{0,6},{1,7},{2,0},{3,1},{4,2},{5,3},{6,4},{7,5},{8,14},{9,15},{10,... | collective-permute-start | bytes 417800 | tf_op jit(solution)/shard_map/ppermute | solution.py:467
  (10 other events, 217.6 us)

commit v4 on v3

--- a/solution.py
+++ b/solution.py
@@ -164,7 +164,10 @@
 
 def send_kernel(plan_ref, live_ref, *refs):
     depth = live_ref.shape[1]
-    blocks, (out_ref, low_ref, high_ref, buf, sems, kv_sems) = refs[:-6], refs[-6:]
+    blocks, (out_ref, low_ref, high_ref, kept_ref, buf, sems, kv_sems, kept_sems) = (
+        refs[:-8],
+        refs[-8:],
+    )
     half = low_ref.shape[1]
     copies = []
     for r in range(NZ):
@@ -178,11 +181,19 @@
                 fetch_rows(blocks, NC * j + side, 0, depth, buf.at[j], sems.at[j])
                 for j in range(NY)
             ]
+            kept = []
+            for j in range(NY):
+                target = kept_ref.at[plan_ref[1 + NY + j]]
+                kept += fetch_rows(
+                    blocks, NC * j + 1 - side, 0, depth, target, kept_sems.at[j]
+                )
             for j, group in enumerate(groups):
                 for copy in group:
                     copy.wait()
                 part = jnp.dot(live_ref[...], buf[j], preferred_element_type=F32)
                 out_ref[plan_ref[1 + j]] = part.astype(BF)
+            for copy in kept:
+                copy.wait()
 
     for copy in copies:
         copy.wait()
@@ -190,59 +201,38 @@
 
 def send_parts(plan, live, blocks):
     rows, depth = live.shape
-    total, width = blocks[0].shape
-    half = (total - depth) // 2
+    width = blocks[0].shape[1]
+    half = (blocks[0].shape[0] - depth) // 2
     return pl.pallas_call(
         send_kernel,
         in_specs=[IN_SMEM, IN_VMEM] + [IN_HBM] * len(blocks),
-        out_specs=[IN_VMEM, IN_HBM, IN_HBM],
+        out_specs=[IN_VMEM, IN_HBM, IN_HBM, IN_VMEM],
         out_shape=[jax.ShapeDtypeStruct((NY, rows, width), BF)]
-        + [jax.ShapeDtypeStruct((NZ, half, width), BF)] * 2,
+        + [jax.ShapeDtypeStruct((NZ, half, width), BF)] * 2
+        + [jax.ShapeDtypeStruct((NY, depth, width), BF)],
         scratch_shapes=[
             pltpu.VMEM((NY, depth, width), BF),
             pltpu.SemaphoreType.DMA((NY, 2)),
             pltpu.SemaphoreType.DMA((2, NZ, 2)),
-        ],
-        compiler_params=pltpu.CompilerParams(vmem_limit_bytes=VMEM_LIMIT),
-    )(plan, live, *[in_hbm(block) for block in blocks])
-
-
-def keep_kernel(plan_ref, live_ref, got_ref, *refs):
-    depth = live_ref.shape[1]
-    blocks, out_refs, (buf, sems) = refs[: -NY - 2], refs[-NY - 2 : -2], refs[-2:]
-    for side in range(NC):
-
-        @pl.when(plan_ref[0] == side)
-        def _(side=side):
-            groups = [
-                fetch_rows(
-                    blocks, NC * j + side, 0, depth, buf.at[plan_ref[1 + j]], sems.at[j]
-                )
-                for j in range(NY)
-            ]
-            for group in groups:
-                for copy in group:
-                    copy.wait()
-
-    for d, out_ref in enumerate(out_refs):
-        own = jnp.dot(live_ref[...], buf[d], preferred_element_type=F32).astype(BF)
-        out_ref[...] = (own.astype(F32) + got_ref[d].astype(F32)).astype(BF)
-
-
-def keep_parts(plan, live, got, blocks):
-    rows, depth = live.shape
-    width = blocks[0].shape[1]
-    return pl.pallas_call(
-        keep_kernel,
-        in_specs=[IN_SMEM, IN_VMEM, IN_VMEM] + [IN_HBM] * len(blocks),
-        out_specs=[IN_VMEM] * NY,
-        out_shape=[jax.ShapeDtypeStruct((rows, width), BF)] * NY,
-        scratch_shapes=[
-            pltpu.VMEM((NY, depth, width), BF),
             pltpu.SemaphoreType.DMA((NY, 2)),
         ],
         compiler_params=pltpu.CompilerParams(vmem_limit_bytes=VMEM_LIMIT),
-    )(plan, live, got, *[in_hbm(block) for block in blocks])
+    )(plan, live, *[in_hbm(block) for block in blocks])
+
+
+def keep_kernel(live_ref, got_ref, weight_ref, *out_refs):
+    for d, out_ref in enumerate(out_refs):
+        own = jnp.dot(live_ref[...], weight_ref[d], preferred_element_type=F32).astype(BF)
+        out_ref[...] = (own.astype(F32) + got_ref[d].astype(F32)).astype(BF)
+
+
+def keep_parts(live, got, weights):
+    rows, width = live.shape[0], weights.shape[2]
+    return pl.pallas_call(
+        keep_kernel,
+        out_shape=[jax.ShapeDtypeStruct((rows, width), BF)] * NY,
+        compiler_params=pltpu.CompilerParams(vmem_limit_bytes=VMEM_LIMIT),
+    )(live, got, weights)
 
 
 def put_head(i, order_ref, rows_ref, weight_refs, out_ref, more=None):
@@ -428,13 +418,14 @@
 
     def plan(side):
         owner = (z_index + steps + side) % NZ // NC
-        return jnp.concatenate([side[None], (owner - y_index) % NY])
-
-    away, *kv_own = send_parts(plan(1 - side), live, blocks)
+        return (owner - y_index) % NY
+
+    plan = jnp.concatenate([1 - side[None], plan(1 - side), plan(side)])
+    away, *kv_own, kept = send_parts(plan, live, blocks)
     got = lax.ppermute(away, "tp", SWAP_CORE)
     after = [lax.ppermute(part, "enc", shift_x(-1)) for part in kv_own]
     before = [lax.ppermute(part, "enc", shift_x(1)) for part in kv_own]
-    parts = keep_parts(plan(side), live, got, blocks)
+    parts = keep_parts(live, got, kept)
     others = [lax.ppermute(parts[d], "tp", shift_y(d)) for d in range(1, NY)]
     opposite = [
         lax.ppermute(after[0], "enc", shift_x(-1)),

time: 132 us -> 132 us (level)
  Pallas kernels: 21.9 us -> 20.2 us
    ppermute x1, waiting for transfers between devices: 4.95 us -> 8.3 us  [body(): lax.ppermute(after[0], 'enc', shift_x(-1))]
    all_to_all x1, waiting for transfers between devices: 2.15 us -> 0.17 us  [body(): moved = lax.all_to_all(merged, 'enc', 0, 0, tiled=True)]
    ppermute x2, waiting for transfers between devices: 3.7 us -> 5.64 us  [body(): after = [lax.ppermute(part, 'enc', shift_x(-1)) for part in kv_own]]
    ppermute x3, waiting for transfers between devices: 6.87 us -> 4.95 us  [body(): others = [lax.ppermute(parts[d], 'tp', shift_y(d)) for d in range(1, NY)]]
    pallas_call x1, Pallas kernels: 3.68 us -> 1.82 us  [keep_parts(): pl.pallas_call(keep_kernel, out_shape=[jax.ShapeDtypeStruct((rows, width)...]
  transfers between devices with their start and end apart: 27 -> 27, of which waited for: 20 -> 20; matrix products, arithmetic and copies ran while one was open for 4% -> 3% of each run, Pallas kernels for 9% -> 7%
where the time goes in v4:
time: 132 us; the launch traced here: 131 us
  waiting for transfers between devices  56 us (42%)
  starting transfers between devices  48.4 us (37%)
  Pallas kernels  20.2 us (15%)
  other arithmetic  3.84 us (3%)
  local copies, waits for them, and re-layouts  2 us (2%)
    ppermute x2, waiting for transfers between devices, body(): up.append(lax.ppermute(up[-1], 'enc', shift_z(-1)))  8.32 us
    ppermute x1, waiting for transfers between devices, body(): lax.ppermute(after[0], 'enc', shift_x(-1))  8.3 us
    ppermute x2, starting transfers between devices, body(): got = lax.ppermute(away, 'tp', SWAP_CORE)  7.71 us
    all_to_all x1, starting transfers between devices, body(): moved = lax.all_to_all(merged, 'enc', 0, 0, tiled=True)  6.87 us
    pallas_call x1, Pallas kernels, hidden_rows(): pl.pallas_call(functools.partial(hidden_kernel, slots), in_specs=[IN_HBM]...  6.66 us
    ppermute x1, starting transfers between devices, body(): up = [block, lax.ppermute(block, 'enc', shift_z(-1))]  6.48 us
    ppermute x2, waiting for transfers between devices, body(): after = [lax.ppermute(part, 'enc', shift_x(-1)) for part in kv_own]  5.64 us
    ppermute x3, waiting for transfers between devices, body(): lax.ppermute(sums[d], 'tp', shift_y(d))  5.14 us
  transfers between devices with their start and end apart: 27, of which 20 were waited for; matrix products, arithmetic and copies ran while one was open for 3% of the time, Pallas kernels for 7%

profile of v4, /device:TPU:1, one launch (start us, length us, event | category | flops | bytes accessed | tf_op | source)
XLA Modules:
  0.0 131.2 jit_solution(8714616172154347480)
XLA Ops:
  2.6 6.5 %collective-permute-start = (bf16[896,256]{1,0:T(8,128)(2,1)S(1)}, bf16[896,256]{1,0:T(8,128)(2,1)S(1)}, u32[]{:S(2)}, u32[]{:S(2)}) collective-permute-start(bf16[896,256]{1,0:T(8,128)(2,1)S(1)} %slice_dynamic-update-slice_fusion.refs_0_), channel_id=1, source_target_pairs={{0,224},{8,232},{16,240},{24,248},{32,0},{40,8},{48,16},{56,24},{6... | collective-permute-start | bytes 1376264 | tf_op jit(solution)/shard_map/ppermute | solution.py:388
  9.1 6.7 %shard_map.113 = bf16[256,640]{1,0:T(8,128)(2,1)} custom-call(bf16[256,5120]{1,0:T(8,128)(2,1)} %bitcast.11, f32[1280]{0:T(1024)} %gain_ref.1, f32[1280]{0:T(1024)} %bias_ref.1, bf16[5120,640]{1,0:T(8,128)(2,1)} %weight_ref.1), custom_call_target="tpu_custom_call" | custom-call | tf_op jit(solution)/shard_map/pallas_call | solution.py:106
  15.8 2.5 %collective-permute-done.refs_1_ = bf16[896,256]{1,0:T(8,128)(2,1)S(1)} collective-permute-done((bf16[896,256]{1,0:T(8,128)(2,1)S(1)}, bf16[896,256]{1,0:T(8,128)(2,1)S(1)}, u32[]{:S(2)}, u32[]{:S(2)}) %collective-permute-start) | collective-permute-done | bytes 458784 | tf_op jit(solution)/shard_map/ppermute | solution.py:388
  18.3 3.1 %collective-permute-done.1.refs_8_ = bf16[896,256]{1,0:T(8,128)(2,1)S(1)} collective-permute-done((bf16[896,256]{1,0:T(8,128)(2,1)S(1)}, bf16[896,256]{1,0:T(8,128)(2,1)S(1)}, u32[]{:S(2)}, u32[]{:S(2)}) %collective-permute-start.1) | collective-permute-done | bytes 458784 | tf_op jit(solution)/shard_map/ppermute | solution.py:389
  22.9 3.4 %all-to-all-start = ((bf16[8,32,640]{2,1,0:T(8,128)(2,1)}), bf16[8,32,640]{2,1,0:T(8,128)(2,1)S(1)}, u32[]{:S(2)}, u32[]{:S(2)}) async-start(bf16[8,32,640]{2,1,0:T(8,128)(2,1)} %bitcast.2), calls=%async_computation | async-start | bytes 655360 | tf_op jit(solution)/shard_map/all_to_all | solution.py:396
  26.3 5.3 %collective-permute-done.3.refs_2_ = bf16[896,256]{1,0:T(8,128)(2,1)S(1)} collective-permute-done((bf16[896,256]{1,0:T(8,128)(2,1)S(1)}, bf16[896,256]{1,0:T(8,128)(2,1)S(1)}, u32[]{:S(2)}, u32[]{:S(2)}) %collective-permute-start.3) | collective-permute-done | bytes 458784 | tf_op jit(solution)/shard_map/ppermute | solution.py:393
  34.4 3.9 %all-to-all-done = bf16[8,32,640]{2,1,0:T(8,128)(2,1)S(1)} async-done(((bf16[8,32,640]{2,1,0:T(8,128)(2,1)}), bf16[8,32,640]{2,1,0:T(8,128)(2,1)S(1)}, u32[]{:S(2)}, u32[]{:S(2)}) %all-to-all-start) | async-done | bytes 327712 | tf_op jit(solution)/shard_map/all_to_all | solution.py:396
  39.7 2.5 %collective-permute-start.7 = (bf16[256,640]{1,0:T(8,128)(2,1)S(1)}, bf16[256,640]{1,0:T(8,128)(2,1)S(1)}, u32[]{:S(2)}, u32[]{:S(2)}) collective-permute-start(bf16[256,640]{1,0:T(8,128)(2,1)S(1)} %bitcast.8), channel_id=1, source_target_pairs={{0,16},{8,24},{16,0},{24,8},{32,48},{40,56},{48,32},{56,40},{64,80... | collective-permute-start | bytes 983048 | tf_op jit(solution)/shard_map/ppermute | solution.py:397
  43.3 2.1 %collective-permute-done.2.b = bf16[256,640]{1,0:T(8,128)(2,1)S(1)} collective-permute-done((bf16[256,640]{1,0:T(8,128)(2,1)S(1)}, bf16[256,640]{1,0:T(8,128)(2,1)S(1)}, u32[]{:S(2)}, u32[]{:S(2)}) %collective-permute-start.2) | collective-permute-done | bytes 327712 | tf_op jit(solution)/shard_map/ppermute | solution.py:397
  45.4 3.0 %collective-permute-done.4.refs_3_ = bf16[896,256]{1,0:T(8,128)(2,1)S(1)} collective-permute-done((bf16[896,256]{1,0:T(8,128)(2,1)S(1)}, bf16[896,256]{1,0:T(8,128)(2,1)S(1)}, u32[]{:S(2)}, u32[]{:S(2)}) %collective-permute-start.4) | collective-permute-done | bytes 458784 | tf_op jit(solution)/shard_map/ppermute | solution.py:393
  54.4 2.8 %collective-permute-done.10.refs_5_ = bf16[448,256]{1,0:T(8,128)(2,1)} collective-permute-done((bf16[448,256]{1,0:T(8,128)(2,1)}, bf16[448,256]{1,0:T(8,128)(2,1)}, u32[]{:S(2)}, u32[]{:S(2)}) %collective-permute-start.10) | collective-permute-done | bytes 229408 | tf_op jit(solution)/shard_map/ppermute | solution.py:401
  57.2 4.6 %shard_map.115 = (bf16[4,512,256]{2,1,0:T(8,128)(2,1)S(1)}, bf16[8,128,256]{2,1,0:T(8,128)(2,1)S(1)}, bf16[8,128,256]{2,1,0:T(8,128)(2,1)S(1)}, bf16[4,640,256]{2,1,0:T(8,128)(2,1)S(1)}) custom-call(s32[9]{0:T(128)S(1)} %pad_add_fusion.1.plan_ref, bf16[512,640]{1,0:T(8,128)(2,1)S(1)} %shard_map.114.live_ref, bf16[896,256]{1,0:T(8,128)(2,1)} %copy-done, ...), custom_call_target="tpu_custom_call" | custom-call | tf_op jit(solution)/shard_map/pallas_call | solution.py:206
  61.8 5.6 %collective-permute-start.11 = (bf16[4,512,256]{2,1,0:T(8,128)(2,1)S(1)}, bf16[4,512,256]{2,1,0:T(8,128)(2,1)S(1)}, u32[]{:S(2)}, u32[]{:S(2)}) collective-permute-start(bf16[4,512,256]{2,1,0:T(8,128)(2,1)S(1)} %get-tuple-element.29), channel_id=1, source_target_pairs={{0,1},{1,0},{2,3},{3,2},{4,5},{5,4},{6,7},{7,6},{8,9},{9,8},{10,11... | collective-permute-start | bytes 3145736 | tf_op jit(solution)/shard_map/ppermute | solution.py:425
  71.5 2.7 %collective-permute-start.14 = (bf16[512,256]{1,0:T(8,128)(2,1)}, bf16[512,256]{1,0:T(8,128)(2,1)}, u32[]{:S(2)}, u32[]{:S(2)}) collective-permute-start(bf16[512,256]{1,0:T(8,128)(2,1)} %get-tuple-element.34), channel_id=1, source_target_pairs={{0,6},{1,7},{2,0},{3,1},{4,2},{5,3},{6,4},{7,5},{8,14},{9,15},{10,... | collective-permute-start | bytes 786440 | tf_op jit(solution)/shard_map/ppermute | solution.py:429
  75.3 5.6 %collective-permute-done.15.refs_2_ = bf16[8,128,256]{2,1,0:T(8,128)(2,1)S(1)} collective-permute-done((bf16[8,128,256]{2,1,0:T(8,128)(2,1)S(1)}, bf16[8,128,256]{2,1,0:T(8,128)(2,1)S(1)}, u32[]{:S(2)}, u32[]{:S(2)}) %collective-permute-start.15) | collective-permute-done | bytes 524320 | tf_op jit(solution)/shard_map/ppermute | solution.py:426
  81.0 2.5 %collective-permute-start.16 = (bf16[8,128,256]{2,1,0:T(8,128)(2,1)S(1)}, bf16[8,128,256]{2,1,0:T(8,128)(2,1)S(1)}, u32[]{:S(2)}, u32[]{:S(2)}) collective-permute-start(bf16[8,128,256]{2,1,0:T(8,128)(2,1)S(1)} %get-tuple-element.36.refs_1_), channel_id=1, source_target_pairs={{0,24},{8,0},{16,8},{24,16},{32,56},{40,32},{48,40},{56,48},{64,88... | collective-permute-start | bytes 1572872 | tf_op jit(solution)/shard_map/ppermute | solution.py:426
  86.8 3.1 %collective-permute-done.12 = bf16[512,256]{1,0:T(8,128)(2,1)} collective-permute-done((bf16[512,256]{1,0:T(8,128)(2,1)}, bf16[512,256]{1,0:T(8,128)(2,1)}, u32[]{:S(2)}, u32[]{:S(2)}) %collective-permute-start.12) | collective-permute-done | bytes 262176 | tf_op jit(solution)/shard_map/ppermute | solution.py:429
  91.8 6.9 %all-to-all-start.1 = ((bf16[32,16,256]{2,1,0:T(8,128)(2,1)}), bf16[32,16,256]{2,1,0:T(8,128)(2,1)S(1)}, u32[]{:S(2)}, u32[]{:S(2)}) async-start(bf16[32,16,256]{2,1,0:T(8,128)(2,1)} %bitcast.12), calls=%async_computation.1 | async-start | bytes 524288 | tf_op jit(solution)/shard_map/all_to_all | solution.py:440
  99.1 8.3 %collective-permute-done.17.refs_4_ = bf16[8,128,256]{2,1,0:T(8,128)(2,1)} collective-permute-done((bf16[8,128,256]{2,1,0:T(8,128)(2,1)S(1)}, bf16[8,128,256]{2,1,0:T(8,128)(2,1)}, u32[]{:S(2)}, u32[]{:S(2)}) %collective-permute-start.17) | collective-permute-done | bytes 524320 | tf_op jit(solution)/shard_map/ppermute | solution.py:431
  107.3 3.5 %collective-permute-done.19.refs_5_ = bf16[8,128,256]{2,1,0:T(8,128)(2,1)} collective-permute-done((bf16[8,128,256]{2,1,0:T(8,128)(2,1)S(1)}, bf16[8,128,256]{2,1,0:T(8,128)(2,1)}, u32[]{:S(2)}, u32[]{:S(2)}) %collective-permute-start.19) | collective-permute-done | bytes 524320 | tf_op jit(solution)/shard_map/ppermute | solution.py:432
  111.0 3.3 %shard_map.117 = (bf16[1024,256]{1,0:T(8,128)(2,1)S(1)}, bf16[16,256]{1,0:T(8,128)(2,1)S(1)}, bf16[4,272,256]{2,1,0:T(8,128)(2,1)S(1)}) custom-call(s32[8]{0:T(128)S(1)} %get-tuple-element.46.order_ref, s32[1,128]{1,0:T(1,128)S(1)} %add.248.target_ref, bf16[32,16,256]{2,1,0:T(8,128)(2,1)S(1)} %all-to-all-done.1.moved_ref, bf16[256,1024]{1,0:T(8,128)(2,1)} %text_ref.1, ...), custom_call_target="tpu_custom_call" | custom-call | tf_op jit(solution)/shard_map/pallas_call | solution.py:297
  114.3 2.1 %collective-permute-start.21 = (bf16[4,272,256]{2,1,0:T(8,128)(2,1)S(1)}, bf16[4,272,256]{2,1,0:T(8,128)(2,1)S(1)}, u32[]{:S(2)}, u32[]{:S(2)}) collective-permute-start(bf16[4,272,256]{2,1,0:T(8,128)(2,1)S(1)} %get-tuple-element.39), channel_id=1, source_target_pairs={{0,1},{1,0},{2,3},{3,2},{4,5},{5,4},{6,7},{7,6},{8,9},{9,8},{10,11... | collective-permute-start | bytes 1671176 | tf_op jit(solution)/shard_map/ppermute | solution.py:456
  121.2 2.7 %collective-permute-start.23 = (bf16[272,256]{1,0:T(8,128)(2,1)S(1)}, bf16[272,256]{1,0:T(8,128)(2,1)S(1)}, u32[]{:S(2)}, u32[]{:S(2)}) collective-permute-start(bf16[272,256]{1,0:T(8,128)(2,1)S(1)} %get-tuple-element.42), channel_id=1, source_target_pairs={{0,4},{1,5},{2,6},{3,7},{4,0},{5,1},{6,2},{7,3},{8,12},{9,13},{10,... | collective-permute-start | bytes 417800 | tf_op jit(solution)/shard_map/ppermute | solution.py:458
  126.3 4.1 %collective-permute-done.23.c = bf16[272,256]{1,0:T(8,128)(2,1)S(1)} collective-permute-done((bf16[272,256]{1,0:T(8,128)(2,1)S(1)}, bf16[272,256]{1,0:T(8,128)(2,1)S(1)}, u32[]{:S(2)}, u32[]{:S(2)}) %collective-permute-start.23) | collective-permute-done | bytes 139296 | tf_op jit(solution)/shard_map/ppermute | solution.py:458
  (78 shorter events, 33.5 us)
Async XLA Ops:
  2.6 15.7 %collective-permute-start = (bf16[896,256]{1,0:T(8,128)(2,1)S(1)}, bf16[896,256]{1,0:T(8,128)(2,1)S(1)}, u32[]{:S(2)}, u32[]{:S(2)}) collective-permute-start(bf16[896,256]{1,0:T(8,128)(2,1)S(1)} %slice_dynamic-update-slice_fusion.refs_0_), channel_id=1, source_target_pairs={{0,224},{8,232},{16,240},{24,248},{32,0},{40,8},{48,16},{56,24},{6... | collective-permute-start | bytes 1376264 | tf_op jit(solution)/shard_map/ppermute | solution.py:388
  9.1 12.3 %collective-permute-start.1 = (bf16[896,256]{1,0:T(8,128)(2,1)S(1)}, bf16[896,256]{1,0:T(8,128)(2,1)S(1)}, u32[]{:S(2)}, u32[]{:S(2)}) collective-permute-start(bf16[896,256]{1,0:T(8,128)(2,1)S(1)} %slice_dynamic-update-slice_fusion.refs_0_), channel_id=1, source_target_pairs={{0,32},{8,40},{16,48},{24,56},{32,64},{40,72},{48,80},{56,88},{64,... | collective-permute-start | bytes 1376264 | tf_op jit(solution)/shard_map/ppermute | solution.py:389
  21.4 10.3 %collective-permute-start.3 = (bf16[896,256]{1,0:T(8,128)(2,1)S(1)}, bf16[896,256]{1,0:T(8,128)(2,1)S(1)}, u32[]{:S(2)}, u32[]{:S(2)}) collective-permute-start(bf16[896,256]{1,0:T(8,128)(2,1)S(1)} %collective-permute-done.refs_1_), channel_id=1, source_target_pairs={{0,224},{8,232},{16,240},{24,248},{32,0},{40,8},{48,16},{56,24},{6... | collective-permute-start | bytes 1376264 | tf_op jit(solution)/shard_map/ppermute | solution.py:393
  21.8 12.6 %collective-permute-start.5 = (bf16[896,256]{1,0:T(8,128)(2,1)S(1)}, bf16[896,256]{1,0:T(8,128)(2,1)}, u32[]{:S(2)}, u32[]{:S(2)}) collective-permute-start(bf16[896,256]{1,0:T(8,128)(2,1)S(1)} %collective-permute-done.1.refs_8_), channel_id=1, source_target_pairs={{0,32},{8,40},{16,48},{24,56},{32,64},{40,72},{48,80},{56,88},{64,... | collective-permute-start | bytes 1376264 | tf_op jit(solution)/shard_map/ppermute | solution.py:394
  22.9 15.4 %all-to-all-start = ((bf16[8,32,640]{2,1,0:T(8,128)(2,1)}), bf16[8,32,640]{2,1,0:T(8,128)(2,1)S(1)}, u32[]{:S(2)}, u32[]{:S(2)}) async-start(bf16[8,32,640]{2,1,0:T(8,128)(2,1)} %bitcast.2), calls=%async_computation | async-start | bytes 655360 | tf_op jit(solution)/shard_map/all_to_all | solution.py:396
  31.7 16.7 %collective-permute-start.4 = (bf16[896,256]{1,0:T(8,128)(2,1)S(1)}, bf16[896,256]{1,0:T(8,128)(2,1)S(1)}, u32[]{:S(2)}, u32[]{:S(2)}) collective-permute-start(bf16[896,256]{1,0:T(8,128)(2,1)S(1)} %collective-permute-done.3.refs_2_), channel_id=1, source_target_pairs={{0,224},{8,232},{16,240},{24,248},{32,0},{40,8},{48,16},{56,24},{6... | collective-permute-start | bytes 1376264 | tf_op jit(solution)/shard_map/ppermute | solution.py:393
  34.4 14.7 %collective-permute-start.6 = (bf16[896,256]{1,0:T(8,128)(2,1)}, bf16[896,256]{1,0:T(8,128)(2,1)S(1)}, u32[]{:S(2)}, u32[]{:S(2)}) collective-permute-start(bf16[896,256]{1,0:T(8,128)(2,1)} %collective-permute-done.5.refs_7_), channel_id=1, source_target_pairs={{0,32},{8,40},{16,48},{24,56},{32,64},{40,72},{48,80},{56,88},{64,... | collective-permute-start | bytes 1376264 | tf_op jit(solution)/shard_map/ppermute | solution.py:394
  38.3 7.1 %collective-permute-start.2 = (bf16[256,640]{1,0:T(8,128)(2,1)S(1)}, bf16[256,640]{1,0:T(8,128)(2,1)S(1)}, u32[]{:S(2)}, u32[]{:S(2)}) collective-permute-start(bf16[256,640]{1,0:T(8,128)(2,1)S(1)} %bitcast.7), channel_id=1, source_target_pairs={{0,8},{8,16},{16,24},{24,0},{32,40},{40,48},{48,56},{56,32},{64,72... | collective-permute-start | bytes 983048 | tf_op jit(solution)/shard_map/ppermute | solution.py:397
  39.7 12.0 %collective-permute-start.7 = (bf16[256,640]{1,0:T(8,128)(2,1)S(1)}, bf16[256,640]{1,0:T(8,128)(2,1)S(1)}, u32[]{:S(2)}, u32[]{:S(2)}) collective-permute-start(bf16[256,640]{1,0:T(8,128)(2,1)S(1)} %bitcast.8), channel_id=1, source_target_pairs={{0,16},{8,24},{16,0},{24,8},{32,48},{40,56},{48,32},{56,40},{64,80... | collective-permute-start | bytes 983048 | tf_op jit(solution)/shard_map/ppermute | solution.py:397
  42.2 9.5 %collective-permute-start.8 = (bf16[256,640]{1,0:T(8,128)(2,1)S(1)}, bf16[256,640]{1,0:T(8,128)(2,1)S(1)}, u32[]{:S(2)}, u32[]{:S(2)}) collective-permute-start(bf16[256,640]{1,0:T(8,128)(2,1)S(1)} %bitcast.9), channel_id=1, source_target_pairs={{0,24},{8,0},{16,8},{24,16},{32,56},{40,32},{48,40},{56,48},{64,88... | collective-permute-start | bytes 983048 | tf_op jit(solution)/shard_map/ppermute | solution.py:397
  50.6 6.6 %collective-permute-start.10 = (bf16[448,256]{1,0:T(8,128)(2,1)}, bf16[448,256]{1,0:T(8,128)(2,1)}, u32[]{:S(2)}, u32[]{:S(2)}) collective-permute-start(bf16[448,256]{1,0:T(8,128)(2,1)} %slice.23), channel_id=1, source_target_pairs={{0,32},{8,40},{16,48},{24,56},{32,64},{40,72},{48,80},{56,88},{64,... | collective-permute-start | bytes 688136 | tf_op jit(solution)/shard_map/ppermute | solution.py:401
  61.8 7.9 %collective-permute-start.11 = (bf16[4,512,256]{2,1,0:T(8,128)(2,1)S(1)}, bf16[4,512,256]{2,1,0:T(8,128)(2,1)S(1)}, u32[]{:S(2)}, u32[]{:S(2)}) collective-permute-start(bf16[4,512,256]{2,1,0:T(8,128)(2,1)S(1)} %get-tuple-element.29), channel_id=1, source_target_pairs={{0,1},{1,0},{2,3},{3,2},{4,5},{5,4},{6,7},{7,6},{8,9},{9,8},{10,11... | collective-permute-start | bytes 3145736 | tf_op jit(solution)/shard_map/ppermute | solution.py:425
  67.4 13.6 %collective-permute-start.15 = (bf16[8,128,256]{2,1,0:T(8,128)(2,1)S(1)}, bf16[8,128,256]{2,1,0:T(8,128)(2,1)S(1)}, u32[]{:S(2)}, u32[]{:S(2)}) collective-permute-start(bf16[8,128,256]{2,1,0:T(8,128)(2,1)S(1)} %get-tuple-element.35.refs_0_), channel_id=1, source_target_pairs={{0,24},{8,0},{16,8},{24,16},{32,56},{40,32},{48,40},{56,48},{64,88... | collective-permute-start | bytes 1572872 | tf_op jit(solution)/shard_map/ppermute | solution.py:426
  68.7 14.8 %collective-permute-start.18 = (bf16[8,128,256]{2,1,0:T(8,128)(2,1)S(1)}, bf16[8,128,256]{2,1,0:T(8,128)(2,1)S(1)}, u32[]{:S(2)}, u32[]{:S(2)}) collective-permute-start(bf16[8,128,256]{2,1,0:T(8,128)(2,1)S(1)} %get-tuple-element.36.refs_1_), channel_id=1, source_target_pairs={{0,8},{8,16},{16,24},{24,0},{32,40},{40,48},{48,56},{56,32},{64,72... | collective-permute-start | bytes 1572872 | tf_op jit(solution)/shard_map/ppermute | solution.py:427
  71.5 13.8 %collective-permute-start.14 = (bf16[512,256]{1,0:T(8,128)(2,1)}, bf16[512,256]{1,0:T(8,128)(2,1)}, u32[]{:S(2)}, u32[]{:S(2)}) collective-permute-start(bf16[512,256]{1,0:T(8,128)(2,1)} %get-tuple-element.34), channel_id=1, source_target_pairs={{0,6},{1,7},{2,0},{3,1},{4,2},{5,3},{6,4},{7,5},{8,14},{9,15},{10,... | collective-permute-start | bytes 786440 | tf_op jit(solution)/shard_map/ppermute | solution.py:429
  74.2 11.9 %collective-permute-start.13 = (bf16[512,256]{1,0:T(8,128)(2,1)}, bf16[512,256]{1,0:T(8,128)(2,1)}, u32[]{:S(2)}, u32[]{:S(2)}) collective-permute-start(bf16[512,256]{1,0:T(8,128)(2,1)} %get-tuple-element.33), channel_id=1, source_target_pairs={{0,4},{1,5},{2,6},{3,7},{4,0},{5,1},{6,2},{7,3},{8,12},{9,13},{10,... | collective-permute-start | bytes 786440 | tf_op jit(solution)/shard_map/ppermute | solution.py:429
  74.6 15.3 %collective-permute-start.12 = (bf16[512,256]{1,0:T(8,128)(2,1)}, bf16[512,256]{1,0:T(8,128)(2,1)}, u32[]{:S(2)}, u32[]{:S(2)}) collective-permute-start(bf16[512,256]{1,0:T(8,128)(2,1)} %get-tuple-element.32), channel_id=1, source_target_pairs={{0,2},{1,3},{2,4},{3,5},{4,6},{5,7},{6,0},{7,1},{8,10},{9,11},{10,... | collective-permute-start | bytes 786440 | tf_op jit(solution)/shard_map/ppermute | solution.py:429
  81.0 18.1 %collective-permute-start.16 = (bf16[8,128,256]{2,1,0:T(8,128)(2,1)S(1)}, bf16[8,128,256]{2,1,0:T(8,128)(2,1)S(1)}, u32[]{:S(2)}, u32[]{:S(2)}) collective-permute-start(bf16[8,128,256]{2,1,0:T(8,128)(2,1)S(1)} %get-tuple-element.36.refs_1_), channel_id=1, source_target_pairs={{0,24},{8,0},{16,8},{24,16},{32,56},{40,32},{48,40},{56,48},{64,88... | collective-permute-start | bytes 1572872 | tf_op jit(solution)/shard_map/ppermute | solution.py:426
  83.4 15.6 %collective-permute-start.20 = (bf16[8,128,256]{2,1,0:T(8,128)(2,1)S(1)}, bf16[8,128,256]{2,1,0:T(8,128)(2,1)S(1)}, u32[]{:S(2)}, u32[]{:S(2)}) collective-permute-start(bf16[8,128,256]{2,1,0:T(8,128)(2,1)S(1)} %get-tuple-element.35.refs_0_), channel_id=1, source_target_pairs={{0,8},{8,16},{16,24},{24,0},{32,40},{40,48},{48,56},{56,32},{64,72... | collective-permute-start | bytes 1572872 | tf_op jit(solution)/shard_map/ppermute | solution.py:427
  85.3 22.0 %collective-permute-start.17 = (bf16[8,128,256]{2,1,0:T(8,128)(2,1)S(1)}, bf16[8,128,256]{2,1,0:T(8,128)(2,1)}, u32[]{:S(2)}, u32[]{:S(2)}) collective-permute-start(bf16[8,128,256]{2,1,0:T(8,128)(2,1)S(1)} %collective-permute-done.15.refs_2_), channel_id=1, source_target_pairs={{0,24},{8,0},{16,8},{24,16},{32,56},{40,32},{48,40},{56,48},{64,88... | collective-permute-start | bytes 1572872 | tf_op jit(solution)/shard_map/ppermute | solution.py:431
  86.1 24.7 %collective-permute-start.19 = (bf16[8,128,256]{2,1,0:T(8,128)(2,1)S(1)}, bf16[8,128,256]{2,1,0:T(8,128)(2,1)}, u32[]{:S(2)}, u32[]{:S(2)}) collective-permute-start(bf16[8,128,256]{2,1,0:T(8,128)(2,1)S(1)} %collective-permute-done.18.refs_7_), channel_id=1, source_target_pairs={{0,8},{8,16},{16,24},{24,0},{32,40},{40,48},{48,56},{56,32},{64,72... | collective-permute-start | bytes 1572872 | tf_op jit(solution)/shard_map/ppermute | solution.py:432
  91.8 19.2 %all-to-all-start.1 = ((bf16[32,16,256]{2,1,0:T(8,128)(2,1)}), bf16[32,16,256]{2,1,0:T(8,128)(2,1)S(1)}, u32[]{:S(2)}, u32[]{:S(2)}) async-start(bf16[32,16,256]{2,1,0:T(8,128)(2,1)} %bitcast.12), calls=%async_computation.1 | async-start | bytes 524288 | tf_op jit(solution)/shard_map/all_to_all | solution.py:440
  121.2 9.1 %collective-permute-start.23 = (bf16[272,256]{1,0:T(8,128)(2,1)S(1)}, bf16[272,256]{1,0:T(8,128)(2,1)S(1)}, u32[]{:S(2)}, u32[]{:S(2)}) collective-permute-start(bf16[272,256]{1,0:T(8,128)(2,1)S(1)} %get-tuple-element.42), channel_id=1, source_target_pairs={{0,4},{1,5},{2,6},{3,7},{4,0},{5,1},{6,2},{7,3},{8,12},{9,13},{10,... | collective-permute-start | bytes 417800 | tf_op jit(solution)/shard_map/ppermute | solution.py:458
  123.9 6.4 %collective-permute-start.24 = (bf16[272,256]{1,0:T(8,128)(2,1)S(1)}, bf16[272,256]{1,0:T(8,128)(2,1)S(1)}, u32[]{:S(2)}, u32[]{:S(2)}) collective-permute-start(bf16[272,256]{1,0:T(8,128)(2,1)S(1)} %get-tuple-element.43), channel_id=1, source_target_pairs={{0,6},{1,7},{2,0},{3,1},{4,2},{5,3},{6,4},{7,5},{8,14},{9,15},{10,... | collective-permute-start | bytes 417800 | tf_op jit(solution)/shard_map/ppermute | solution.py:458
  (11 other events, 156.5 us)

commit v5 on v4

--- a/solution.py
+++ b/solution.py
@@ -235,7 +235,7 @@
     )(live, got, weights)
 
 
-def put_head(i, order_ref, rows_ref, weight_refs, out_ref, more=None):
+def put_head(i, order_ref, rows_ref, weight_refs, out_ref):
     head = order_ref[i]
     rows = weight_refs[0].shape[2] // NX
     lines = []
@@ -251,10 +251,7 @@
     ).astype(BF)
     for d in range(NX):
         place = pl.ds(pl.multiple_of(order_ref[NY + d] * rows, rows), rows)
-        piece = part[d * rows : (d + 1) * rows]
-        if more is not None:
-            piece = (piece.astype(F32) + more[i, place].astype(F32)).astype(BF)
-        out_ref[place] = piece
+        out_ref[place] = part[d * rows : (d + 1) * rows]
 
 
 def two_lines(squares):
@@ -264,8 +261,7 @@
     return jnp.where(line == 0, high, jnp.where(line == 1, squares - high, 0.0)).astype(BF)
 
 
-def project_send_kernel(order_ref, target_ref, moved_ref, text_ref, *refs):
-    weight_refs, (rows_ref, squares_ref, out_ref, text_buf, sem) = refs[:-5], refs[-5:]
+def mix_kernel(target_ref, moved_ref, text_ref, rows_ref, squares_ref, text_buf, sem):
     text_copy = pltpu.make_async_copy(text_ref, text_buf, sem)
     text_copy.start()
     span = text_ref.shape[0]
@@ -285,48 +281,58 @@
         rows_ref[columns] = mixed.astype(BF)
         squares += jnp.sum(mixed * mixed, axis=0, keepdims=True)
     squares_ref[...] = two_lines(squares)
+
+
+def mix(target, moved, text):
+    span, features = text.shape
+    return pl.pallas_call(
+        mix_kernel,
+        in_specs=[IN_VMEM, IN_VMEM, IN_HBM],
+        out_specs=[IN_VMEM] * 2,
+        out_shape=[
+            jax.ShapeDtypeStruct((features, span), BF),
+            jax.ShapeDtypeStruct((16, span), BF),
+        ],
+        scratch_shapes=[pltpu.VMEM((span, features), BF), pltpu.SemaphoreType.DMA(())],
+        compiler_params=pltpu.CompilerParams(vmem_limit_bytes=VMEM_LIMIT),
+    )(target, moved, in_hbm(text))
+
+
+def project_send_kernel(order_ref, rows_ref, squares_ref, *refs):
+    weight_refs, out_ref = refs[:-1], refs[-1]
     width = weight_refs[0].shape[2]
     for i in range(NY):
         put_head(i, order_ref, rows_ref, weight_refs, out_ref.at[i])
         out_ref[i, width:] = squares_ref[...]
 
 
-def project_send(order, target, moved, text, weights):
-    span, features = text.shape
+def project_send(order, rows, squares, weights):
+    span = rows.shape[1]
     width = weights[0].shape[2]
     return pl.pallas_call(
         project_send_kernel,
-        in_specs=[IN_SMEM, IN_VMEM, IN_VMEM, IN_HBM] + [IN_VMEM] * len(weights),
-        out_specs=[IN_VMEM] * 3,
-        out_shape=[
-            jax.ShapeDtypeStruct((features, span), BF),
-            jax.ShapeDtypeStruct((16, span), BF),
-            jax.ShapeDtypeStruct((NY, width + 16, span), BF),
-        ],
-        scratch_shapes=[pltpu.VMEM((span, features), BF), pltpu.SemaphoreType.DMA(())],
-        compiler_params=pltpu.CompilerParams(vmem_limit_bytes=VMEM_LIMIT),
-    )(order, target, moved, in_hbm(text), *weights)
-
-
-def project_keep_kernel(order_ref, rows_ref, squares_ref, got_ref, *refs):
-    weight_refs, out_refs = refs[:-NY], refs[-NY:]
-    width = weight_refs[0].shape[2]
+        in_specs=[IN_SMEM] + [IN_VMEM] * (2 + len(weights)),
+        out_specs=IN_VMEM,
+        out_shape=jax.ShapeDtypeStruct((NY, width + 16, span), BF),
+        compiler_params=pltpu.CompilerParams(vmem_limit_bytes=VMEM_LIMIT),
+    )(order, rows, squares, *weights)
+
+
+def pair_kernel(lines, own_ref, got_ref, *out_refs):
+    rows = own_ref.shape[1] - lines
     for i, out_ref in enumerate(out_refs):
-        put_head(i, order_ref, rows_ref, weight_refs, out_ref, got_ref)
-        squares = squares_ref[...].astype(F32) + got_ref[i, width:].astype(F32)
-        out_ref[width:] = two_lines(squares[0:1] + squares[1:2])
-
-
-def project_keep(order, rows, squares, got, weights):
-    features, span = rows.shape
-    width = weights[0].shape[2]
-    return pl.pallas_call(
-        project_keep_kernel,
-        in_specs=[IN_SMEM] + [IN_VMEM] * (3 + len(weights)),
-        out_specs=[IN_VMEM] * NY,
-        out_shape=[jax.ShapeDtypeStruct((width + 16, span), BF)] * NY,
-        compiler_params=pltpu.CompilerParams(vmem_limit_bytes=VMEM_LIMIT),
-    )(order, rows, squares, got, *weights)
+        total = own_ref[i].astype(F32) + got_ref[i].astype(F32)
+        out_ref[:rows] = total[:rows].astype(BF)
+        if lines:
+            out_ref[rows:] = two_lines(total[rows : rows + 1] + total[rows + 1 : rows + 2])
+
+
+def add_pair(lines, own, got):
+    return pl.pallas_call(
+        functools.partial(pair_kernel, lines),
+        out_shape=[jax.ShapeDtypeStruct(own.shape[1:], BF)] * NY,
+        compiler_params=pltpu.CompilerParams(vmem_limit_bytes=VMEM_LIMIT),
+    )(own, got)
 
 
 def finish_kernel(features, a, b, c, d, cos_ref, sin_ref, keys_ref, values_ref):
@@ -452,9 +458,11 @@
     turn = jnp.arange(2 * NY, dtype=jnp.int32) < NY
     own_heads = jnp.where(turn, (order + core) % NZ, order)
     other_heads = jnp.where(turn, (order + 1 - core) % NZ, order)
-    mixed, squares, away = project_send(other_heads, rows, moved, text, kv_all)
+    mixed, squares = mix(rows, moved, text)
+    away = project_send(other_heads, mixed, squares, kv_all)
     got = lax.ppermute(away, "tp", SWAP_CORE)
-    sums = project_keep(own_heads, mixed, squares, got, kv_all)
+    own = project_send(own_heads, mixed, squares, kv_all)
+    sums = add_pair(16, own, got)
     sums = [sums[0]] + [lax.ppermute(sums[d], "tp", shift_y(d)) for d in range(1, NY)]
 
     positions = (enc_index * span + jnp.arange(span, dtype=jnp.int32)).astype(F32)

time: 132 us -> 131 us (level)
    all_to_all x1, waiting for transfers between devices: 0.17 us -> 12 us  [body(): moved = lax.all_to_all(merged, 'enc', 0, 0, tiled=True)]
    ppermute x1, waiting for transfers between devices: 8.3 us -> 0.01 us  [body(): lax.ppermute(after[0], 'enc', shift_x(-1))]
    ppermute x1, waiting for transfers between devices: 3.48 us -> 0.01 us  [body(): lax.ppermute(before[1], 'enc', shift_x(1))]
    ppermute x2, waiting for transfers between devices: 2.37 us -> 0.81 us  [body(): got = lax.ppermute(away, 'tp', SWAP_CORE)]
    pallas_call x2 -> x4, Pallas kernels: 5.19 us -> 5.55 us  [the longest x2 3.85 us: project_send(): pl.pallas_call(project_send_kernel, in_specs=[IN_SMEM] + [IN_VMEM] * (2 +...]
  transfers between devices with their start and end apart: 27 -> 27, of which waited for: 20 -> 17; matrix products, arithmetic and copies ran while one was open for 3% -> 3% of each run, Pallas kernels for 7% -> 10%
where the time goes in v5:
time: 131 us; the launch traced here: 130 us
  waiting for transfers between devices  54.8 us (42%)
  starting transfers between devices  48.4 us (37%)
  Pallas kernels  20.5 us (16%)
  other arithmetic  3.84 us (3%)
  local copies, waits for them, and re-layouts  2 us (2%)
    all_to_all x1, waiting for transfers between devices, body(): moved = lax.all_to_all(merged, 'enc', 0, 0, tiled=True)  12 us
    ppermute x2, waiting for transfers between devices, body(): up.append(lax.ppermute(up[-1], 'enc', shift_z(-1)))  8.32 us
    ppermute x2, starting transfers between devices, body(): got = lax.ppermute(away, 'tp', SWAP_CORE)  7.7 us
    all_to_all x1, starting transfers between devices, body(): moved = lax.all_to_all(merged, 'enc', 0, 0, tiled=True)  6.87 us
    pallas_call x1, Pallas kernels, hidden_rows(): pl.pallas_call(functools.partial(hidden_kernel, slots), in_specs=[IN_HBM]...  6.66 us
    ppermute x1, starting transfers between devices, body(): up = [block, lax.ppermute(block, 'enc', shift_z(-1))]  6.48 us
    ppermute x2, waiting for transfers between devices, body(): after = [lax.ppermute(part, 'enc', shift_x(-1)) for part in kv_own]  5.64 us
    ppermute x3, waiting for transfers between devices, body(): lax.ppermute(sums[d], 'tp', shift_y(d))  5.53 us
  transfers between devices with their start and end apart: 27, of which 17 were waited for; matrix products, arithmetic and copies ran while one was open for 3% of the time, Pallas kernels for 10%

profile of v5, /device:TPU:1, one launch (start us, length us, event | category | flops | bytes accessed | tf_op | source)
XLA Modules:
  0.0 130.4 jit_solution(12134730988707594778)
XLA Ops:
  2.6 6.5 %collective-permute-start = (bf16[896,256]{1,0:T(8,128)(2,1)S(1)}, bf16[896,256]{1,0:T(8,128)(2,1)S(1)}, u32[]{:S(2)}, u32[]{:S(2)}) collective-permute-start(bf16[896,256]{1,0:T(8,128)(2,1)S(1)} %slice_dynamic-update-slice_fusion.refs_0_), channel_id=1, source_target_pairs={{0,224},{8,232},{16,240},{24,248},{32,0},{40,8},{48,16},{56,24},{6... | collective-permute-start | bytes 1376264 | tf_op jit(solution)/shard_map/ppermute | solution.py:394
  9.1 6.7 %shard_map.113 = bf16[256,640]{1,0:T(8,128)(2,1)} custom-call(bf16[256,5120]{1,0:T(8,128)(2,1)} %bitcast.11, f32[1280]{0:T(1024)} %gain_ref.1, f32[1280]{0:T(1024)} %bias_ref.1, bf16[5120,640]{1,0:T(8,128)(2,1)} %weight_ref.1), custom_call_target="tpu_custom_call" | custom-call | tf_op jit(solution)/shard_map/pallas_call | solution.py:106
  15.8 2.5 %collective-permute-done.refs_1_ = bf16[896,256]{1,0:T(8,128)(2,1)S(1)} collective-permute-done((bf16[896,256]{1,0:T(8,128)(2,1)S(1)}, bf16[896,256]{1,0:T(8,128)(2,1)S(1)}, u32[]{:S(2)}, u32[]{:S(2)}) %collective-permute-start) | collective-permute-done | bytes 458784 | tf_op jit(solution)/shard_map/ppermute | solution.py:394
  18.3 3.1 %collective-permute-done.1.refs_8_ = bf16[896,256]{1,0:T(8,128)(2,1)S(1)} collective-permute-done((bf16[896,256]{1,0:T(8,128)(2,1)S(1)}, bf16[896,256]{1,0:T(8,128)(2,1)S(1)}, u32[]{:S(2)}, u32[]{:S(2)}) %collective-permute-start.1) | collective-permute-done | bytes 458784 | tf_op jit(solution)/shard_map/ppermute | solution.py:395
  22.9 3.4 %all-to-all-start = ((bf16[8,32,640]{2,1,0:T(8,128)(2,1)}), bf16[8,32,640]{2,1,0:T(8,128)(2,1)S(1)}, u32[]{:S(2)}, u32[]{:S(2)}) async-start(bf16[8,32,640]{2,1,0:T(8,128)(2,1)} %bitcast.2), calls=%async_computation | async-start | bytes 655360 | tf_op jit(solution)/shard_map/all_to_all | solution.py:402
  26.3 5.3 %collective-permute-done.3.refs_2_ = bf16[896,256]{1,0:T(8,128)(2,1)S(1)} collective-permute-done((bf16[896,256]{1,0:T(8,128)(2,1)S(1)}, bf16[896,256]{1,0:T(8,128)(2,1)S(1)}, u32[]{:S(2)}, u32[]{:S(2)}) %collective-permute-start.3) | collective-permute-done | bytes 458784 | tf_op jit(solution)/shard_map/ppermute | solution.py:399
  34.4 3.9 %all-to-all-done = bf16[8,32,640]{2,1,0:T(8,128)(2,1)S(1)} async-done(((bf16[8,32,640]{2,1,0:T(8,128)(2,1)}), bf16[8,32,640]{2,1,0:T(8,128)(2,1)S(1)}, u32[]{:S(2)}, u32[]{:S(2)}) %all-to-all-start) | async-done | bytes 327712 | tf_op jit(solution)/shard_map/all_to_all | solution.py:402
  39.7 2.5 %collective-permute-start.7 = (bf16[256,640]{1,0:T(8,128)(2,1)S(1)}, bf16[256,640]{1,0:T(8,128)(2,1)S(1)}, u32[]{:S(2)}, u32[]{:S(2)}) collective-permute-start(bf16[256,640]{1,0:T(8,128)(2,1)S(1)} %bitcast.8), channel_id=1, source_target_pairs={{0,16},{8,24},{16,0},{24,8},{32,48},{40,56},{48,32},{56,40},{64,80... | collective-permute-start | bytes 983048 | tf_op jit(solution)/shard_map/ppermute | solution.py:403
  43.3 2.1 %collective-permute-done.2.b = bf16[256,640]{1,0:T(8,128)(2,1)S(1)} collective-permute-done((bf16[256,640]{1,0:T(8,128)(2,1)S(1)}, bf16[256,640]{1,0:T(8,128)(2,1)S(1)}, u32[]{:S(2)}, u32[]{:S(2)}) %collective-permute-start.2) | collective-permute-done | bytes 327712 | tf_op jit(solution)/shard_map/ppermute | solution.py:403
  45.4 3.0 %collective-permute-done.4.refs_3_ = bf16[896,256]{1,0:T(8,128)(2,1)S(1)} collective-permute-done((bf16[896,256]{1,0:T(8,128)(2,1)S(1)}, bf16[896,256]{1,0:T(8,128)(2,1)S(1)}, u32[]{:S(2)}, u32[]{:S(2)}) %collective-permute-start.4) | collective-permute-done | bytes 458784 | tf_op jit(solution)/shard_map/ppermute | solution.py:399
  54.4 2.8 %collective-permute-done.10.refs_5_ = bf16[448,256]{1,0:T(8,128)(2,1)} collective-permute-done((bf16[448,256]{1,0:T(8,128)(2,1)}, bf16[448,256]{1,0:T(8,128)(2,1)}, u32[]{:S(2)}, u32[]{:S(2)}) %collective-permute-start.10) | collective-permute-done | bytes 229408 | tf_op jit(solution)/shard_map/ppermute | solution.py:407
  57.2 4.6 %shard_map.115 = (bf16[4,512,256]{2,1,0:T(8,128)(2,1)S(1)}, bf16[8,128,256]{2,1,0:T(8,128)(2,1)S(1)}, bf16[8,128,256]{2,1,0:T(8,128)(2,1)S(1)}, bf16[4,640,256]{2,1,0:T(8,128)(2,1)S(1)}) custom-call(s32[9]{0:T(128)S(1)} %pad_add_fusion.1.plan_ref, bf16[512,640]{1,0:T(8,128)(2,1)S(1)} %shard_map.114.live_ref, bf16[896,256]{1,0:T(8,128)(2,1)} %copy-done, ...), custom_call_target="tpu_custom_call" | custom-call | tf_op jit(solution)/shard_map/pallas_call | solution.py:206
  61.8 5.6 %collective-permute-start.11 = (bf16[4,512,256]{2,1,0:T(8,128)(2,1)S(1)}, bf16[4,512,256]{2,1,0:T(8,128)(2,1)S(1)}, u32[]{:S(2)}, u32[]{:S(2)}) collective-permute-start(bf16[4,512,256]{2,1,0:T(8,128)(2,1)S(1)} %get-tuple-element.28), channel_id=1, source_target_pairs={{0,1},{1,0},{2,3},{3,2},{4,5},{5,4},{6,7},{7,6},{8,9},{9,8},{10,11... | collective-permute-start | bytes 3145736 | tf_op jit(solution)/shard_map/ppermute | solution.py:431
  71.5 2.7 %collective-permute-start.14 = (bf16[512,256]{1,0:T(8,128)(2,1)}, bf16[512,256]{1,0:T(8,128)(2,1)}, u32[]{:S(2)}, u32[]{:S(2)}) collective-permute-start(bf16[512,256]{1,0:T(8,128)(2,1)} %get-tuple-element.33), channel_id=1, source_target_pairs={{0,6},{1,7},{2,0},{3,1},{4,2},{5,3},{6,4},{7,5},{8,14},{9,15},{10,... | collective-permute-start | bytes 786440 | tf_op jit(solution)/shard_map/ppermute | solution.py:435
  75.3 5.6 %collective-permute-done.15.refs_2_ = bf16[8,128,256]{2,1,0:T(8,128)(2,1)S(1)} collective-permute-done((bf16[8,128,256]{2,1,0:T(8,128)(2,1)S(1)}, bf16[8,128,256]{2,1,0:T(8,128)(2,1)S(1)}, u32[]{:S(2)}, u32[]{:S(2)}) %collective-permute-start.15) | collective-permute-done | bytes 524320 | tf_op jit(solution)/shard_map/ppermute | solution.py:432
  81.0 2.5 %collective-permute-start.16 = (bf16[8,128,256]{2,1,0:T(8,128)(2,1)S(1)}, bf16[8,128,256]{2,1,0:T(8,128)(2,1)S(1)}, u32[]{:S(2)}, u32[]{:S(2)}) collective-permute-start(bf16[8,128,256]{2,1,0:T(8,128)(2,1)S(1)} %get-tuple-element.37.refs_1_), channel_id=1, source_target_pairs={{0,24},{8,0},{16,8},{24,16},{32,56},{40,32},{48,40},{56,48},{64,88... | collective-permute-start | bytes 1572872 | tf_op jit(solution)/shard_map/ppermute | solution.py:432
  86.8 3.1 %collective-permute-done.12 = bf16[512,256]{1,0:T(8,128)(2,1)} collective-permute-done((bf16[512,256]{1,0:T(8,128)(2,1)}, bf16[512,256]{1,0:T(8,128)(2,1)}, u32[]{:S(2)}, u32[]{:S(2)}) %collective-permute-start.12) | collective-permute-done | bytes 262176 | tf_op jit(solution)/shard_map/ppermute | solution.py:435
  89.9 1.9 %add_convert_fusion = bf16[512,256]{1,0:T(8,128)(2,1)} fusion(bf16[512,256]{1,0:T(8,128)(2,1)} %collective-permute-done.14, bf16[512,256]{1,0:T(8,128)(2,1)} %collective-permute-done.13, bf16[512,256]{1,0:T(8,128)(2,1)} %collective-permute-done.12, bf16[512,256]{1,0:T(8,128)(2,1)S(1)} %get-tuple-element.30), kind=kLoop, calls=%fused_computation | loop fusion | flops 1048576 | bytes 1310720 | tf_op jit(solution)/shard_map/convert_element_type | solution.py:443
  91.8 6.9 %all-to-all-start.1 = ((bf16[32,16,256]{2,1,0:T(8,128)(2,1)}), bf16[32,16,256]{2,1,0:T(8,128)(2,1)S(1)}, u32[]{:S(2)}, u32[]{:S(2)}) async-start(bf16[32,16,256]{2,1,0:T(8,128)(2,1)} %bitcast.12), calls=%async_computation.1 | async-start | bytes 524288 | tf_op jit(solution)/shard_map/all_to_all | solution.py:446
  99.0 12.0 %all-to-all-done.1.moved_ref = bf16[32,16,256]{2,1,0:T(8,128)(2,1)S(1)} async-done(((bf16[32,16,256]{2,1,0:T(8,128)(2,1)}), bf16[32,16,256]{2,1,0:T(8,128)(2,1)S(1)}, u32[]{:S(2)}, u32[]{:S(2)}) %all-to-all-start.1) | async-done | bytes 262176 | tf_op jit(solution)/shard_map/all_to_all | solution.py:446
  112.6 1.9 %shard_map.119 = bf16[4,272,256]{2,1,0:T(8,128)(2,1)S(1)} custom-call(s32[8]{0:T(128)S(1)} %get-tuple-element.44.order_ref, bf16[1024,256]{1,0:T(8,128)(2,1)S(1)} %get-tuple-element.34.rows_ref, bf16[16,256]{1,0:T(8,128)(2,1)S(1)} %get-tuple-element.35.squares_ref, bf16[8,128,256]{2,1,0:T(8,128)(2,1)S(1)} %get-tuple-element.36.refs_0_, ...), custom_call_target="tpu_custom_call" | custom-call | tf_op jit(solution)/shard_map/pallas_call | solution.py:312
  114.5 2.1 %collective-permute-start.21 = (bf16[4,272,256]{2,1,0:T(8,128)(2,1)S(1)}, bf16[4,272,256]{2,1,0:T(8,128)(2,1)S(1)}, u32[]{:S(2)}, u32[]{:S(2)}) collective-permute-start(bf16[4,272,256]{2,1,0:T(8,128)(2,1)S(1)} %shard_map.119), channel_id=1, source_target_pairs={{0,1},{1,0},{2,3},{3,2},{4,5},{5,4},{6,7},{7,6},{8,9},{9,8},{10,11... | collective-permute-start | bytes 1671176 | tf_op jit(solution)/shard_map/ppermute | solution.py:463
  120.1 2.7 %collective-permute-start.23 = (bf16[272,256]{1,0:T(8,128)(2,1)S(1)}, bf16[272,256]{1,0:T(8,128)(2,1)S(1)}, u32[]{:S(2)}, u32[]{:S(2)}) collective-permute-start(bf16[272,256]{1,0:T(8,128)(2,1)S(1)} %get-tuple-element.40), channel_id=1, source_target_pairs={{0,4},{1,5},{2,6},{3,7},{4,0},{5,1},{6,2},{7,3},{8,12},{9,13},{10,... | collective-permute-start | bytes 417800 | tf_op jit(solution)/shard_map/ppermute | solution.py:466
  125.5 4.1 %collective-permute-done.23.c = bf16[272,256]{1,0:T(8,128)(2,1)S(1)} collective-permute-done((bf16[272,256]{1,0:T(8,128)(2,1)S(1)}, bf16[272,256]{1,0:T(8,128)(2,1)S(1)}, u32[]{:S(2)}, u32[]{:S(2)}) %collective-permute-start.23) | collective-permute-done | bytes 139296 | tf_op jit(solution)/shard_map/ppermute | solution.py:466
  (80 shorter events, 32.0 us)
Async XLA Ops:
  2.6 15.7 %collective-permute-start = (bf16[896,256]{1,0:T(8,128)(2,1)S(1)}, bf16[896,256]{1,0:T(8,128)(2,1)S(1)}, u32[]{:S(2)}, u32[]{:S(2)}) collective-permute-start(bf16[896,256]{1,0:T(8,128)(2,1)S(1)} %slice_dynamic-update-slice_fusion.refs_0_), channel_id=1, source_target_pairs={{0,224},{8,232},{16,240},{24,248},{32,0},{40,8},{48,16},{56,24},{6... | collective-permute-start | bytes 1376264 | tf_op jit(solution)/shard_map/ppermute | solution.py:394
  9.1 12.3 %collective-permute-start.1 = (bf16[896,256]{1,0:T(8,128)(2,1)S(1)}, bf16[896,256]{1,0:T(8,128)(2,1)S(1)}, u32[]{:S(2)}, u32[]{:S(2)}) collective-permute-start(bf16[896,256]{1,0:T(8,128)(2,1)S(1)} %slice_dynamic-update-slice_fusion.refs_0_), channel_id=1, source_target_pairs={{0,32},{8,40},{16,48},{24,56},{32,64},{40,72},{48,80},{56,88},{64,... | collective-permute-start | bytes 1376264 | tf_op jit(solution)/shard_map/ppermute | solution.py:395
  21.4 10.3 %collective-permute-start.3 = (bf16[896,256]{1,0:T(8,128)(2,1)S(1)}, bf16[896,256]{1,0:T(8,128)(2,1)S(1)}, u32[]{:S(2)}, u32[]{:S(2)}) collective-permute-start(bf16[896,256]{1,0:T(8,128)(2,1)S(1)} %collective-permute-done.refs_1_), channel_id=1, source_target_pairs={{0,224},{8,232},{16,240},{24,248},{32,0},{40,8},{48,16},{56,24},{6... | collective-permute-start | bytes 1376264 | tf_op jit(solution)/shard_map/ppermute | solution.py:399
  21.8 12.6 %collective-permute-start.5 = (bf16[896,256]{1,0:T(8,128)(2,1)S(1)}, bf16[896,256]{1,0:T(8,128)(2,1)}, u32[]{:S(2)}, u32[]{:S(2)}) collective-permute-start(bf16[896,256]{1,0:T(8,128)(2,1)S(1)} %collective-permute-done.1.refs_8_), channel_id=1, source_target_pairs={{0,32},{8,40},{16,48},{24,56},{32,64},{40,72},{48,80},{56,88},{64,... | collective-permute-start | bytes 1376264 | tf_op jit(solution)/shard_map/ppermute | solution.py:400
  22.9 15.4 %all-to-all-start = ((bf16[8,32,640]{2,1,0:T(8,128)(2,1)}), bf16[8,32,640]{2,1,0:T(8,128)(2,1)S(1)}, u32[]{:S(2)}, u32[]{:S(2)}) async-start(bf16[8,32,640]{2,1,0:T(8,128)(2,1)} %bitcast.2), calls=%async_computation | async-start | bytes 655360 | tf_op jit(solution)/shard_map/all_to_all | solution.py:402
  31.7 16.7 %collective-permute-start.4 = (bf16[896,256]{1,0:T(8,128)(2,1)S(1)}, bf16[896,256]{1,0:T(8,128)(2,1)S(1)}, u32[]{:S(2)}, u32[]{:S(2)}) collective-permute-start(bf16[896,256]{1,0:T(8,128)(2,1)S(1)} %collective-permute-done.3.refs_2_), channel_id=1, source_target_pairs={{0,224},{8,232},{16,240},{24,248},{32,0},{40,8},{48,16},{56,24},{6... | collective-permute-start | bytes 1376264 | tf_op jit(solution)/shard_map/ppermute | solution.py:399
  34.4 14.7 %collective-permute-start.6 = (bf16[896,256]{1,0:T(8,128)(2,1)}, bf16[896,256]{1,0:T(8,128)(2,1)S(1)}, u32[]{:S(2)}, u32[]{:S(2)}) collective-permute-start(bf16[896,256]{1,0:T(8,128)(2,1)} %collective-permute-done.5.refs_7_), channel_id=1, source_target_pairs={{0,32},{8,40},{16,48},{24,56},{32,64},{40,72},{48,80},{56,88},{64,... | collective-permute-start | bytes 1376264 | tf_op jit(solution)/shard_map/ppermute | solution.py:400
  38.3 7.1 %collective-permute-start.2 = (bf16[256,640]{1,0:T(8,128)(2,1)S(1)}, bf16[256,640]{1,0:T(8,128)(2,1)S(1)}, u32[]{:S(2)}, u32[]{:S(2)}) collective-permute-start(bf16[256,640]{1,0:T(8,128)(2,1)S(1)} %bitcast.7), channel_id=1, source_target_pairs={{0,8},{8,16},{16,24},{24,0},{32,40},{40,48},{48,56},{56,32},{64,72... | collective-permute-start | bytes 983048 | tf_op jit(solution)/shard_map/ppermute | solution.py:403
  39.7 12.0 %collective-permute-start.7 = (bf16[256,640]{1,0:T(8,128)(2,1)S(1)}, bf16[256,640]{1,0:T(8,128)(2,1)S(1)}, u32[]{:S(2)}, u32[]{:S(2)}) collective-permute-start(bf16[256,640]{1,0:T(8,128)(2,1)S(1)} %bitcast.8), channel_id=1, source_target_pairs={{0,16},{8,24},{16,0},{24,8},{32,48},{40,56},{48,32},{56,40},{64,80... | collective-permute-start | bytes 983048 | tf_op jit(solution)/shard_map/ppermute | solution.py:403
  42.2 9.5 %collective-permute-start.8 = (bf16[256,640]{1,0:T(8,128)(2,1)S(1)}, bf16[256,640]{1,0:T(8,128)(2,1)S(1)}, u32[]{:S(2)}, u32[]{:S(2)}) collective-permute-start(bf16[256,640]{1,0:T(8,128)(2,1)S(1)} %bitcast.9), channel_id=1, source_target_pairs={{0,24},{8,0},{16,8},{24,16},{32,56},{40,32},{48,40},{56,48},{64,88... | collective-permute-start | bytes 983048 | tf_op jit(solution)/shard_map/ppermute | solution.py:403
  61.8 7.9 %collective-permute-start.11 = (bf16[4,512,256]{2,1,0:T(8,128)(2,1)S(1)}, bf16[4,512,256]{2,1,0:T(8,128)(2,1)S(1)}, u32[]{:S(2)}, u32[]{:S(2)}) collective-permute-start(bf16[4,512,256]{2,1,0:T(8,128)(2,1)S(1)} %get-tuple-element.28), channel_id=1, source_target_pairs={{0,1},{1,0},{2,3},{3,2},{4,5},{5,4},{6,7},{7,6},{8,9},{9,8},{10,11... | collective-permute-start | bytes 3145736 | tf_op jit(solution)/shard_map/ppermute | solution.py:431
  67.4 13.6 %collective-permute-start.15 = (bf16[8,128,256]{2,1,0:T(8,128)(2,1)S(1)}, bf16[8,128,256]{2,1,0:T(8,128)(2,1)S(1)}, u32[]{:S(2)}, u32[]{:S(2)}) collective-permute-start(bf16[8,128,256]{2,1,0:T(8,128)(2,1)S(1)} %get-tuple-element.36.refs_0_), channel_id=1, source_target_pairs={{0,24},{8,0},{16,8},{24,16},{32,56},{40,32},{48,40},{56,48},{64,88... | collective-permute-start | bytes 1572872 | tf_op jit(solution)/shard_map/ppermute | solution.py:432
  68.7 14.8 %collective-permute-start.18 = (bf16[8,128,256]{2,1,0:T(8,128)(2,1)S(1)}, bf16[8,128,256]{2,1,0:T(8,128)(2,1)S(1)}, u32[]{:S(2)}, u32[]{:S(2)}) collective-permute-start(bf16[8,128,256]{2,1,0:T(8,128)(2,1)S(1)} %get-tuple-element.37.refs_1_), channel_id=1, source_target_pairs={{0,8},{8,16},{16,24},{24,0},{32,40},{40,48},{48,56},{56,32},{64,72... | collective-permute-start | bytes 1572872 | tf_op jit(solution)/shard_map/ppermute | solution.py:433
  71.5 13.8 %collective-permute-start.14 = (bf16[512,256]{1,0:T(8,128)(2,1)}, bf16[512,256]{1,0:T(8,128)(2,1)}, u32[]{:S(2)}, u32[]{:S(2)}) collective-permute-start(bf16[512,256]{1,0:T(8,128)(2,1)} %get-tuple-element.33), channel_id=1, source_target_pairs={{0,6},{1,7},{2,0},{3,1},{4,2},{5,3},{6,4},{7,5},{8,14},{9,15},{10,... | collective-permute-start | bytes 786440 | tf_op jit(solution)/shard_map/ppermute | solution.py:435
  74.2 11.9 %collective-permute-start.13 = (bf16[512,256]{1,0:T(8,128)(2,1)}, bf16[512,256]{1,0:T(8,128)(2,1)}, u32[]{:S(2)}, u32[]{:S(2)}) collective-permute-start(bf16[512,256]{1,0:T(8,128)(2,1)} %get-tuple-element.32), channel_id=1, source_target_pairs={{0,4},{1,5},{2,6},{3,7},{4,0},{5,1},{6,2},{7,3},{8,12},{9,13},{10,... | collective-permute-start | bytes 786440 | tf_op jit(solution)/shard_map/ppermute | solution.py:435
  74.6 15.3 %collective-permute-start.12 = (bf16[512,256]{1,0:T(8,128)(2,1)}, bf16[512,256]{1,0:T(8,128)(2,1)}, u32[]{:S(2)}, u32[]{:S(2)}) collective-permute-start(bf16[512,256]{1,0:T(8,128)(2,1)} %get-tuple-element.31), channel_id=1, source_target_pairs={{0,2},{1,3},{2,4},{3,5},{4,6},{5,7},{6,0},{7,1},{8,10},{9,11},{10,... | collective-permute-start | bytes 786440 | tf_op jit(solution)/shard_map/ppermute | solution.py:435
  81.0 31.6 %collective-permute-start.16 = (bf16[8,128,256]{2,1,0:T(8,128)(2,1)S(1)}, bf16[8,128,256]{2,1,0:T(8,128)(2,1)S(1)}, u32[]{:S(2)}, u32[]{:S(2)}) collective-permute-start(bf16[8,128,256]{2,1,0:T(8,128)(2,1)S(1)} %get-tuple-element.37.refs_1_), channel_id=1, source_target_pairs={{0,24},{8,0},{16,8},{24,16},{32,56},{40,32},{48,40},{56,48},{64,88... | collective-permute-start | bytes 1572872 | tf_op jit(solution)/shard_map/ppermute | solution.py:432
  83.4 29.1 %collective-permute-start.20 = (bf16[8,128,256]{2,1,0:T(8,128)(2,1)S(1)}, bf16[8,128,256]{2,1,0:T(8,128)(2,1)S(1)}, u32[]{:S(2)}, u32[]{:S(2)}) collective-permute-start(bf16[8,128,256]{2,1,0:T(8,128)(2,1)S(1)} %get-tuple-element.36.refs_0_), channel_id=1, source_target_pairs={{0,8},{8,16},{16,24},{24,0},{32,40},{40,48},{48,56},{56,32},{64,72... | collective-permute-start | bytes 1572872 | tf_op jit(solution)/shard_map/ppermute | solution.py:433
  85.3 27.3 %collective-permute-start.17 = (bf16[8,128,256]{2,1,0:T(8,128)(2,1)S(1)}, bf16[8,128,256]{2,1,0:T(8,128)(2,1)}, u32[]{:S(2)}, u32[]{:S(2)}) collective-permute-start(bf16[8,128,256]{2,1,0:T(8,128)(2,1)S(1)} %collective-permute-done.15.refs_2_), channel_id=1, source_target_pairs={{0,24},{8,0},{16,8},{24,16},{32,56},{40,32},{48,40},{56,48},{64,88... | collective-permute-start | bytes 1572872 | tf_op jit(solution)/shard_map/ppermute | solution.py:437
  86.1 26.5 %collective-permute-start.19 = (bf16[8,128,256]{2,1,0:T(8,128)(2,1)S(1)}, bf16[8,128,256]{2,1,0:T(8,128)(2,1)}, u32[]{:S(2)}, u32[]{:S(2)}) collective-permute-start(bf16[8,128,256]{2,1,0:T(8,128)(2,1)S(1)} %collective-permute-done.18.refs_7_), channel_id=1, source_target_pairs={{0,8},{8,16},{16,24},{24,0},{32,40},{40,48},{48,56},{56,32},{64,72... | collective-permute-start | bytes 1572872 | tf_op jit(solution)/shard_map/ppermute | solution.py:438
  91.8 19.2 %all-to-all-start.1 = ((bf16[32,16,256]{2,1,0:T(8,128)(2,1)}), bf16[32,16,256]{2,1,0:T(8,128)(2,1)S(1)}, u32[]{:S(2)}, u32[]{:S(2)}) async-start(bf16[32,16,256]{2,1,0:T(8,128)(2,1)} %bitcast.12), calls=%async_computation.1 | async-start | bytes 524288 | tf_op jit(solution)/shard_map/all_to_all | solution.py:446
  118.8 6.7 %collective-permute-start.22 = (bf16[272,256]{1,0:T(8,128)(2,1)S(1)}, bf16[272,256]{1,0:T(8,128)(2,1)S(1)}, u32[]{:S(2)}, u32[]{:S(2)}) collective-permute-start(bf16[272,256]{1,0:T(8,128)(2,1)S(1)} %get-tuple-element.39), channel_id=1, source_target_pairs={{0,2},{1,3},{2,4},{3,5},{4,6},{5,7},{6,0},{7,1},{8,10},{9,11},{10,... | collective-permute-start | bytes 417800 | tf_op jit(solution)/shard_map/ppermute | solution.py:466
  120.1 9.5 %collective-permute-start.23 = (bf16[272,256]{1,0:T(8,128)(2,1)S(1)}, bf16[272,256]{1,0:T(8,128)(2,1)S(1)}, u32[]{:S(2)}, u32[]{:S(2)}) collective-permute-start(bf16[272,256]{1,0:T(8,128)(2,1)S(1)} %get-tuple-element.40), channel_id=1, source_target_pairs={{0,4},{1,5},{2,6},{3,7},{4,0},{5,1},{6,2},{7,3},{8,12},{9,13},{10,... | collective-permute-start | bytes 417800 | tf_op jit(solution)/shard_map/ppermute | solution.py:466
  122.8 6.8 %collective-permute-start.24 = (bf16[272,256]{1,0:T(8,128)(2,1)S(1)}, bf16[272,256]{1,0:T(8,128)(2,1)S(1)}, u32[]{:S(2)}, u32[]{:S(2)}) collective-permute-start(bf16[272,256]{1,0:T(8,128)(2,1)S(1)} %get-tuple-element.41), channel_id=1, source_target_pairs={{0,6},{1,7},{2,0},{3,1},{4,2},{5,3},{6,4},{7,5},{8,14},{9,15},{10,... | collective-permute-start | bytes 417800 | tf_op jit(solution)/shard_map/ppermute | solution.py:466
  (11 other events, 157.1 us)

commit v6 on v5

--- a/solution.py
+++ b/solution.py
@@ -14,6 +14,7 @@
 BF = jnp.bfloat16
 F32 = jnp.float32
 
+FAR_FIRST, FAR_LAST = (2, 1, 3), (3, 1, 2)
 GROUPS_Z = [[z * NX + x for z in range(NZ)] for x in range(NX)]
 
 
@@ -432,7 +433,7 @@
     after = [lax.ppermute(part, "enc", shift_x(-1)) for part in kv_own]
     before = [lax.ppermute(part, "enc", shift_x(1)) for part in kv_own]
     parts = keep_parts(live, got, kept)
-    others = [lax.ppermute(parts[d], "tp", shift_y(d)) for d in range(1, NY)]
+    others = [lax.ppermute(parts[d], "tp", shift_y(d)) for d in FAR_LAST]
     opposite = [
         lax.ppermute(after[0], "enc", shift_x(-1)),
         lax.ppermute(before[1], "enc", shift_x(1)),
@@ -463,7 +464,7 @@
     got = lax.ppermute(away, "tp", SWAP_CORE)
     own = project_send(own_heads, mixed, squares, kv_all)
     sums = add_pair(16, own, got)
-    sums = [sums[0]] + [lax.ppermute(sums[d], "tp", shift_y(d)) for d in range(1, NY)]
+    sums = [sums[0]] + [lax.ppermute(sums[d], "tp", shift_y(d)) for d in FAR_FIRST]
 
     positions = (enc_index * span + jnp.arange(span, dtype=jnp.int32)).astype(F32)
     cos, sin = rotary(positions, wide // 2)

time: 131 us -> 130 us (level)
  waiting for transfers between devices: 54.8 us -> 49.5 us
  starting transfers between devices: 48.4 us -> 53.1 us
    ppermute x3, waiting for transfers between devices: 4.95 us -> 1 us  [body(): others = [lax.ppermute(parts[d], 'tp', shift_y(d)) for d in FAR_LAST]]
    ppermute x1, starting transfers between devices: 0.82 us -> 2.67 us  [body(): lax.ppermute(after[0], 'enc', shift_x(-1))]
    ppermute x3, starting transfers between devices: 3.76 us -> 5.57 us  [body(): others = [lax.ppermute(parts[d], 'tp', shift_y(d)) for d in FAR_LAST]]
    ppermute x2, waiting for transfers between devices: 5.64 us -> 3.85 us  [body(): after = [lax.ppermute(part, 'enc', shift_x(-1)) for part in kv_own]]
    all_to_all x1, waiting for transfers between devices: 12 us -> 13.6 us  [body(): moved = lax.all_to_all(merged, 'enc', 0, 0, tiled=True)]
where the time goes in v6:
time: 130 us
  starting transfers between devices  53.1 us (41%)
  waiting for transfers between devices  49.5 us (38%)
  Pallas kernels  20.5 us (16%)
  other arithmetic  3.84 us (3%)
  local copies, waits for them, and re-layouts  2 us (2%)
    all_to_all x1, waiting for transfers between devices, body(): moved = lax.all_to_all(merged, 'enc', 0, 0, tiled=True)  13.6 us
    ppermute x2, waiting for transfers between devices, body(): up.append(lax.ppermute(up[-1], 'enc', shift_z(-1)))  8.32 us
    all_to_all x1, starting transfers between devices, body(): moved = lax.all_to_all(merged, 'enc', 0, 0, tiled=True)  8.03 us
    ppermute x2, starting transfers between devices, body(): got = lax.ppermute(away, 'tp', SWAP_CORE)  7.61 us
    pallas_call x1, Pallas kernels, hidden_rows(): pl.pallas_call(functools.partial(hidden_kernel, slots), in_specs=[IN_HBM]...  6.66 us
    ppermute x1, starting transfers between devices, body(): up = [block, lax.ppermute(block, 'enc', shift_z(-1))]  6.48 us
    ppermute x3, starting transfers between devices, body(): others = [lax.ppermute(parts[d], 'tp', shift_y(d)) for d in FAR_LAST]  5.57 us
    ppermute x3, starting transfers between devices, body(): lax.ppermute(sums[d], 'tp', shift_y(d))  5.57 us
  transfers between devices with their start and end apart: 27, of which 17 were waited for; matrix products, arithmetic and copies ran while one was open for 3% of the time, Pallas kernels for 10%

profile of v6, /device:TPU:1, one launch (start us, length us, event | category | flops | bytes accessed | tf_op | source)
XLA Modules:
  0.0 129.8 jit_solution(15021559546818959174)
XLA Ops:
  2.6 6.5 %collective-permute-start = (bf16[896,256]{1,0:T(8,128)(2,1)S(1)}, bf16[896,256]{1,0:T(8,128)(2,1)S(1)}, u32[]{:S(2)}, u32[]{:S(2)}) collective-permute-start(bf16[896,256]{1,0:T(8,128)(2,1)S(1)} %slice_dynamic-update-slice_fusion.refs_0_), channel_id=1, source_target_pairs={{0,224},{8,232},{16,240},{24,248},{32,0},{40,8},{48,16},{56,24},{6... | collective-permute-start | bytes 1376264 | tf_op jit(solution)/shard_map/ppermute | solution.py:395
  9.1 6.7 %shard_map.113 = bf16[256,640]{1,0:T(8,128)(2,1)} custom-call(bf16[256,5120]{1,0:T(8,128)(2,1)} %bitcast.11, f32[1280]{0:T(1024)} %gain_ref.1, f32[1280]{0:T(1024)} %bias_ref.1, bf16[5120,640]{1,0:T(8,128)(2,1)} %weight_ref.1), custom_call_target="tpu_custom_call" | custom-call | tf_op jit(solution)/shard_map/pallas_call | solution.py:107
  15.8 2.5 %collective-permute-done.refs_1_ = bf16[896,256]{1,0:T(8,128)(2,1)S(1)} collective-permute-done((bf16[896,256]{1,0:T(8,128)(2,1)S(1)}, bf16[896,256]{1,0:T(8,128)(2,1)S(1)}, u32[]{:S(2)}, u32[]{:S(2)}) %collective-permute-start) | collective-permute-done | bytes 458784 | tf_op jit(solution)/shard_map/ppermute | solution.py:395
  18.3 3.1 %collective-permute-done.1.refs_8_ = bf16[896,256]{1,0:T(8,128)(2,1)S(1)} collective-permute-done((bf16[896,256]{1,0:T(8,128)(2,1)S(1)}, bf16[896,256]{1,0:T(8,128)(2,1)S(1)}, u32[]{:S(2)}, u32[]{:S(2)}) %collective-permute-start.1) | collective-permute-done | bytes 458784 | tf_op jit(solution)/shard_map/ppermute | solution.py:396
  22.9 3.4 %all-to-all-start = ((bf16[8,32,640]{2,1,0:T(8,128)(2,1)}), bf16[8,32,640]{2,1,0:T(8,128)(2,1)S(1)}, u32[]{:S(2)}, u32[]{:S(2)}) async-start(bf16[8,32,640]{2,1,0:T(8,128)(2,1)} %bitcast.2), calls=%async_computation | async-start | bytes 655360 | tf_op jit(solution)/shard_map/all_to_all | solution.py:403
  26.3 5.3 %collective-permute-done.3.refs_2_ = bf16[896,256]{1,0:T(8,128)(2,1)S(1)} collective-permute-done((bf16[896,256]{1,0:T(8,128)(2,1)S(1)}, bf16[896,256]{1,0:T(8,128)(2,1)S(1)}, u32[]{:S(2)}, u32[]{:S(2)}) %collective-permute-start.3) | collective-permute-done | bytes 458784 | tf_op jit(solution)/shard_map/ppermute | solution.py:400
  34.4 3.9 %all-to-all-done = bf16[8,32,640]{2,1,0:T(8,128)(2,1)S(1)} async-done(((bf16[8,32,640]{2,1,0:T(8,128)(2,1)}), bf16[8,32,640]{2,1,0:T(8,128)(2,1)S(1)}, u32[]{:S(2)}, u32[]{:S(2)}) %all-to-all-start) | async-done | bytes 327712 | tf_op jit(solution)/shard_map/all_to_all | solution.py:403
  39.7 2.5 %collective-permute-start.7 = (bf16[256,640]{1,0:T(8,128)(2,1)S(1)}, bf16[256,640]{1,0:T(8,128)(2,1)S(1)}, u32[]{:S(2)}, u32[]{:S(2)}) collective-permute-start(bf16[256,640]{1,0:T(8,128)(2,1)S(1)} %bitcast.8), channel_id=1, source_target_pairs={{0,16},{8,24},{16,0},{24,8},{32,48},{40,56},{48,32},{56,40},{64,80... | collective-permute-start | bytes 983048 | tf_op jit(solution)/shard_map/ppermute | solution.py:404
  43.3 2.1 %collective-permute-done.2.b = bf16[256,640]{1,0:T(8,128)(2,1)S(1)} collective-permute-done((bf16[256,640]{1,0:T(8,128)(2,1)S(1)}, bf16[256,640]{1,0:T(8,128)(2,1)S(1)}, u32[]{:S(2)}, u32[]{:S(2)}) %collective-permute-start.2) | collective-permute-done | bytes 327712 | tf_op jit(solution)/shard_map/ppermute | solution.py:404
  45.4 3.0 %collective-permute-done.4.refs_3_ = bf16[896,256]{1,0:T(8,128)(2,1)S(1)} collective-permute-done((bf16[896,256]{1,0:T(8,128)(2,1)S(1)}, bf16[896,256]{1,0:T(8,128)(2,1)S(1)}, u32[]{:S(2)}, u32[]{:S(2)}) %collective-permute-start.4) | collective-permute-done | bytes 458784 | tf_op jit(solution)/shard_map/ppermute | solution.py:400
  54.4 2.8 %collective-permute-done.10.refs_5_ = bf16[448,256]{1,0:T(8,128)(2,1)} collective-permute-done((bf16[448,256]{1,0:T(8,128)(2,1)}, bf16[448,256]{1,0:T(8,128)(2,1)}, u32[]{:S(2)}, u32[]{:S(2)}) %collective-permute-start.10) | collective-permute-done | bytes 229408 | tf_op jit(solution)/shard_map/ppermute | solution.py:408
  57.2 4.6 %shard_map.115 = (bf16[4,512,256]{2,1,0:T(8,128)(2,1)S(1)}, bf16[8,128,256]{2,1,0:T(8,128)(2,1)S(1)}, bf16[8,128,256]{2,1,0:T(8,128)(2,1)S(1)}, bf16[4,640,256]{2,1,0:T(8,128)(2,1)S(1)}) custom-call(s32[9]{0:T(128)S(1)} %pad_add_fusion.1.plan_ref, bf16[512,640]{1,0:T(8,128)(2,1)S(1)} %shard_map.114.live_ref, bf16[896,256]{1,0:T(8,128)(2,1)} %copy-done, ...), custom_call_target="tpu_custom_call" | custom-call | tf_op jit(solution)/shard_map/pallas_call | solution.py:207
  61.8 5.6 %collective-permute-start.11 = (bf16[4,512,256]{2,1,0:T(8,128)(2,1)S(1)}, bf16[4,512,256]{2,1,0:T(8,128)(2,1)S(1)}, u32[]{:S(2)}, u32[]{:S(2)}) collective-permute-start(bf16[4,512,256]{2,1,0:T(8,128)(2,1)S(1)} %get-tuple-element.28), channel_id=1, source_target_pairs={{0,1},{1,0},{2,3},{3,2},{4,5},{5,4},{6,7},{7,6},{8,9},{9,8},{10,11... | collective-permute-start | bytes 3145736 | tf_op jit(solution)/shard_map/ppermute | solution.py:432
  71.5 2.9 %collective-permute-start.14 = (bf16[512,256]{1,0:T(8,128)(2,1)}, bf16[512,256]{1,0:T(8,128)(2,1)}, u32[]{:S(2)}, u32[]{:S(2)}) collective-permute-start(bf16[512,256]{1,0:T(8,128)(2,1)} %get-tuple-element.33), channel_id=1, source_target_pairs={{0,4},{1,5},{2,6},{3,7},{4,0},{5,1},{6,2},{7,3},{8,12},{9,13},{10,... | collective-permute-start | bytes 786440 | tf_op jit(solution)/shard_map/ppermute | solution.py:436
  74.8 2.3 %collective-permute-start.12 = (bf16[512,256]{1,0:T(8,128)(2,1)}, bf16[512,256]{1,0:T(8,128)(2,1)}, u32[]{:S(2)}, u32[]{:S(2)}) collective-permute-start(bf16[512,256]{1,0:T(8,128)(2,1)} %get-tuple-element.31), channel_id=1, source_target_pairs={{0,6},{1,7},{2,0},{3,1},{4,2},{5,3},{6,4},{7,5},{8,14},{9,15},{10,... | collective-permute-start | bytes 786440 | tf_op jit(solution)/shard_map/ppermute | solution.py:436
  77.1 3.8 %collective-permute-done.15.refs_2_ = bf16[8,128,256]{2,1,0:T(8,128)(2,1)S(1)} collective-permute-done((bf16[8,128,256]{2,1,0:T(8,128)(2,1)S(1)}, bf16[8,128,256]{2,1,0:T(8,128)(2,1)S(1)}, u32[]{:S(2)}, u32[]{:S(2)}) %collective-permute-start.15) | collective-permute-done | bytes 524320 | tf_op jit(solution)/shard_map/ppermute | solution.py:433
  81.0 2.5 %collective-permute-start.16 = (bf16[8,128,256]{2,1,0:T(8,128)(2,1)S(1)}, bf16[8,128,256]{2,1,0:T(8,128)(2,1)S(1)}, u32[]{:S(2)}, u32[]{:S(2)}) collective-permute-start(bf16[8,128,256]{2,1,0:T(8,128)(2,1)S(1)} %get-tuple-element.37.refs_1_), channel_id=1, source_target_pairs={{0,24},{8,0},{16,8},{24,16},{32,56},{40,32},{48,40},{56,48},{64,88... | collective-permute-start | bytes 1572872 | tf_op jit(solution)/shard_map/ppermute | solution.py:433
  83.5 2.7 %collective-permute-start.17 = (bf16[8,128,256]{2,1,0:T(8,128)(2,1)S(1)}, bf16[8,128,256]{2,1,0:T(8,128)(2,1)}, u32[]{:S(2)}, u32[]{:S(2)}) collective-permute-start(bf16[8,128,256]{2,1,0:T(8,128)(2,1)S(1)} %collective-permute-done.15.refs_2_), channel_id=1, source_target_pairs={{0,24},{8,0},{16,8},{24,16},{32,56},{40,32},{48,40},{56,48},{64,88... | collective-permute-start | bytes 1572872 | tf_op jit(solution)/shard_map/ppermute | solution.py:438
  89.1 8.0 %all-to-all-start.1 = ((bf16[32,16,256]{2,1,0:T(8,128)(2,1)}), bf16[32,16,256]{2,1,0:T(8,128)(2,1)S(1)}, u32[]{:S(2)}, u32[]{:S(2)}) async-start(bf16[32,16,256]{2,1,0:T(8,128)(2,1)} %bitcast.12), calls=%async_computation.1 | async-start | bytes 524288 | tf_op jit(solution)/shard_map/all_to_all | solution.py:447
  97.5 13.6 %all-to-all-done.1.moved_ref = bf16[32,16,256]{2,1,0:T(8,128)(2,1)S(1)} async-done(((bf16[32,16,256]{2,1,0:T(8,128)(2,1)}), bf16[32,16,256]{2,1,0:T(8,128)(2,1)S(1)}, u32[]{:S(2)}, u32[]{:S(2)}) %all-to-all-start.1) | async-done | bytes 262176 | tf_op jit(solution)/shard_map/all_to_all | solution.py:447
  114.6 2.0 %collective-permute-start.21 = (bf16[4,272,256]{2,1,0:T(8,128)(2,1)S(1)}, bf16[4,272,256]{2,1,0:T(8,128)(2,1)S(1)}, u32[]{:S(2)}, u32[]{:S(2)}) collective-permute-start(bf16[4,272,256]{2,1,0:T(8,128)(2,1)S(1)} %shard_map.119), channel_id=1, source_target_pairs={{0,1},{1,0},{2,3},{3,2},{4,5},{5,4},{6,7},{7,6},{8,9},{9,8},{10,11... | collective-permute-start | bytes 1671176 | tf_op jit(solution)/shard_map/ppermute | solution.py:464
  118.8 2.9 %collective-permute-start.22 = (bf16[272,256]{1,0:T(8,128)(2,1)S(1)}, bf16[272,256]{1,0:T(8,128)(2,1)S(1)}, u32[]{:S(2)}, u32[]{:S(2)}) collective-permute-start(bf16[272,256]{1,0:T(8,128)(2,1)S(1)} %get-tuple-element.39), channel_id=1, source_target_pairs={{0,4},{1,5},{2,6},{3,7},{4,0},{5,1},{6,2},{7,3},{8,12},{9,13},{10,... | collective-permute-start | bytes 417800 | tf_op jit(solution)/shard_map/ppermute | solution.py:467
  122.2 2.2 %collective-permute-start.24 = (bf16[272,256]{1,0:T(8,128)(2,1)S(1)}, bf16[272,256]{1,0:T(8,128)(2,1)S(1)}, u32[]{:S(2)}, u32[]{:S(2)}) collective-permute-start(bf16[272,256]{1,0:T(8,128)(2,1)S(1)} %get-tuple-element.41), channel_id=1, source_target_pairs={{0,6},{1,7},{2,0},{3,1},{4,2},{5,3},{6,4},{7,5},{8,14},{9,15},{10,... | collective-permute-start | bytes 417800 | tf_op jit(solution)/shard_map/ppermute | solution.py:467
  125.7 3.1 %collective-permute-done.23.c = bf16[272,256]{1,0:T(8,128)(2,1)S(1)} collective-permute-done((bf16[272,256]{1,0:T(8,128)(2,1)S(1)}, bf16[272,256]{1,0:T(8,128)(2,1)S(1)}, u32[]{:S(2)}, u32[]{:S(2)}) %collective-permute-start.23) | collective-permute-done | bytes 139296 | tf_op jit(solution)/shard_map/ppermute | solution.py:467
  (80 shorter events, 30.9 us)
Async XLA Ops:
  2.6 15.7 %collective-permute-start = (bf16[896,256]{1,0:T(8,128)(2,1)S(1)}, bf16[896,256]{1,0:T(8,128)(2,1)S(1)}, u32[]{:S(2)}, u32[]{:S(2)}) collective-permute-start(bf16[896,256]{1,0:T(8,128)(2,1)S(1)} %slice_dynamic-update-slice_fusion.refs_0_), channel_id=1, source_target_pairs={{0,224},{8,232},{16,240},{24,248},{32,0},{40,8},{48,16},{56,24},{6... | collective-permute-start | bytes 1376264 | tf_op jit(solution)/shard_map/ppermute | solution.py:395
  9.1 12.3 %collective-permute-start.1 = (bf16[896,256]{1,0:T(8,128)(2,1)S(1)}, bf16[896,256]{1,0:T(8,128)(2,1)S(1)}, u32[]{:S(2)}, u32[]{:S(2)}) collective-permute-start(bf16[896,256]{1,0:T(8,128)(2,1)S(1)} %slice_dynamic-update-slice_fusion.refs_0_), channel_id=1, source_target_pairs={{0,32},{8,40},{16,48},{24,56},{32,64},{40,72},{48,80},{56,88},{64,... | collective-permute-start | bytes 1376264 | tf_op jit(solution)/shard_map/ppermute | solution.py:396
  21.4 10.3 %collective-permute-start.3 = (bf16[896,256]{1,0:T(8,128)(2,1)S(1)}, bf16[896,256]{1,0:T(8,128)(2,1)S(1)}, u32[]{:S(2)}, u32[]{:S(2)}) collective-permute-start(bf16[896,256]{1,0:T(8,128)(2,1)S(1)} %collective-permute-done.refs_1_), channel_id=1, source_target_pairs={{0,224},{8,232},{16,240},{24,248},{32,0},{40,8},{48,16},{56,24},{6... | collective-permute-start | bytes 1376264 | tf_op jit(solution)/shard_map/ppermute | solution.py:400
  21.8 12.6 %collective-permute-start.5 = (bf16[896,256]{1,0:T(8,128)(2,1)S(1)}, bf16[896,256]{1,0:T(8,128)(2,1)}, u32[]{:S(2)}, u32[]{:S(2)}) collective-permute-start(bf16[896,256]{1,0:T(8,128)(2,1)S(1)} %collective-permute-done.1.refs_8_), channel_id=1, source_target_pairs={{0,32},{8,40},{16,48},{24,56},{32,64},{40,72},{48,80},{56,88},{64,... | collective-permute-start | bytes 1376264 | tf_op jit(solution)/shard_map/ppermute | solution.py:401
  22.9 15.4 %all-to-all-start = ((bf16[8,32,640]{2,1,0:T(8,128)(2,1)}), bf16[8,32,640]{2,1,0:T(8,128)(2,1)S(1)}, u32[]{:S(2)}, u32[]{:S(2)}) async-start(bf16[8,32,640]{2,1,0:T(8,128)(2,1)} %bitcast.2), calls=%async_computation | async-start | bytes 655360 | tf_op jit(solution)/shard_map/all_to_all | solution.py:403
  31.7 16.7 %collective-permute-start.4 = (bf16[896,256]{1,0:T(8,128)(2,1)S(1)}, bf16[896,256]{1,0:T(8,128)(2,1)S(1)}, u32[]{:S(2)}, u32[]{:S(2)}) collective-permute-start(bf16[896,256]{1,0:T(8,128)(2,1)S(1)} %collective-permute-done.3.refs_2_), channel_id=1, source_target_pairs={{0,224},{8,232},{16,240},{24,248},{32,0},{40,8},{48,16},{56,24},{6... | collective-permute-start | bytes 1376264 | tf_op jit(solution)/shard_map/ppermute | solution.py:400
  34.4 14.7 %collective-permute-start.6 = (bf16[896,256]{1,0:T(8,128)(2,1)}, bf16[896,256]{1,0:T(8,128)(2,1)S(1)}, u32[]{:S(2)}, u32[]{:S(2)}) collective-permute-start(bf16[896,256]{1,0:T(8,128)(2,1)} %collective-permute-done.5.refs_7_), channel_id=1, source_target_pairs={{0,32},{8,40},{16,48},{24,56},{32,64},{40,72},{48,80},{56,88},{64,... | collective-permute-start | bytes 1376264 | tf_op jit(solution)/shard_map/ppermute | solution.py:401
  38.3 7.1 %collective-permute-start.2 = (bf16[256,640]{1,0:T(8,128)(2,1)S(1)}, bf16[256,640]{1,0:T(8,128)(2,1)S(1)}, u32[]{:S(2)}, u32[]{:S(2)}) collective-permute-start(bf16[256,640]{1,0:T(8,128)(2,1)S(1)} %bitcast.7), channel_id=1, source_target_pairs={{0,8},{8,16},{16,24},{24,0},{32,40},{40,48},{48,56},{56,32},{64,72... | collective-permute-start | bytes 983048 | tf_op jit(solution)/shard_map/ppermute | solution.py:404
  39.7 12.0 %collective-permute-start.7 = (bf16[256,640]{1,0:T(8,128)(2,1)S(1)}, bf16[256,640]{1,0:T(8,128)(2,1)S(1)}, u32[]{:S(2)}, u32[]{:S(2)}) collective-permute-start(bf16[256,640]{1,0:T(8,128)(2,1)S(1)} %bitcast.8), channel_id=1, source_target_pairs={{0,16},{8,24},{16,0},{24,8},{32,48},{40,56},{48,32},{56,40},{64,80... | collective-permute-start | bytes 983048 | tf_op jit(solution)/shard_map/ppermute | solution.py:404
  42.2 9.5 %collective-permute-start.8 = (bf16[256,640]{1,0:T(8,128)(2,1)S(1)}, bf16[256,640]{1,0:T(8,128)(2,1)S(1)}, u32[]{:S(2)}, u32[]{:S(2)}) collective-permute-start(bf16[256,640]{1,0:T(8,128)(2,1)S(1)} %bitcast.9), channel_id=1, source_target_pairs={{0,24},{8,0},{16,8},{24,16},{32,56},{40,32},{48,40},{56,48},{64,88... | collective-permute-start | bytes 983048 | tf_op jit(solution)/shard_map/ppermute | solution.py:404
  61.8 7.9 %collective-permute-start.11 = (bf16[4,512,256]{2,1,0:T(8,128)(2,1)S(1)}, bf16[4,512,256]{2,1,0:T(8,128)(2,1)S(1)}, u32[]{:S(2)}, u32[]{:S(2)}) collective-permute-start(bf16[4,512,256]{2,1,0:T(8,128)(2,1)S(1)} %get-tuple-element.28), channel_id=1, source_target_pairs={{0,1},{1,0},{2,3},{3,2},{4,5},{5,4},{6,7},{7,6},{8,9},{9,8},{10,11... | collective-permute-start | bytes 3145736 | tf_op jit(solution)/shard_map/ppermute | solution.py:432
  67.4 13.6 %collective-permute-start.15 = (bf16[8,128,256]{2,1,0:T(8,128)(2,1)S(1)}, bf16[8,128,256]{2,1,0:T(8,128)(2,1)S(1)}, u32[]{:S(2)}, u32[]{:S(2)}) collective-permute-start(bf16[8,128,256]{2,1,0:T(8,128)(2,1)S(1)} %get-tuple-element.36.refs_0_), channel_id=1, source_target_pairs={{0,24},{8,0},{16,8},{24,16},{32,56},{40,32},{48,40},{56,48},{64,88... | collective-permute-start | bytes 1572872 | tf_op jit(solution)/shard_map/ppermute | solution.py:433
  68.7 14.8 %collective-permute-start.18 = (bf16[8,128,256]{2,1,0:T(8,128)(2,1)S(1)}, bf16[8,128,256]{2,1,0:T(8,128)(2,1)S(1)}, u32[]{:S(2)}, u32[]{:S(2)}) collective-permute-start(bf16[8,128,256]{2,1,0:T(8,128)(2,1)S(1)} %get-tuple-element.37.refs_1_), channel_id=1, source_target_pairs={{0,8},{8,16},{16,24},{24,0},{32,40},{40,48},{48,56},{56,32},{64,72... | collective-permute-start | bytes 1572872 | tf_op jit(solution)/shard_map/ppermute | solution.py:434
  71.5 12.0 %collective-permute-start.14 = (bf16[512,256]{1,0:T(8,128)(2,1)}, bf16[512,256]{1,0:T(8,128)(2,1)}, u32[]{:S(2)}, u32[]{:S(2)}) collective-permute-start(bf16[512,256]{1,0:T(8,128)(2,1)} %get-tuple-element.33), channel_id=1, source_target_pairs={{0,4},{1,5},{2,6},{3,7},{4,0},{5,1},{6,2},{7,3},{8,12},{9,13},{10,... | collective-permute-start | bytes 786440 | tf_op jit(solution)/shard_map/ppermute | solution.py:436
  74.4 12.8 %collective-permute-start.13 = (bf16[512,256]{1,0:T(8,128)(2,1)}, bf16[512,256]{1,0:T(8,128)(2,1)}, u32[]{:S(2)}, u32[]{:S(2)}) collective-permute-start(bf16[512,256]{1,0:T(8,128)(2,1)} %get-tuple-element.32), channel_id=1, source_target_pairs={{0,2},{1,3},{2,4},{3,5},{4,6},{5,7},{6,0},{7,1},{8,10},{9,11},{10,... | collective-permute-start | bytes 786440 | tf_op jit(solution)/shard_map/ppermute | solution.py:436
  74.8 12.4 %collective-permute-start.12 = (bf16[512,256]{1,0:T(8,128)(2,1)}, bf16[512,256]{1,0:T(8,128)(2,1)}, u32[]{:S(2)}, u32[]{:S(2)}) collective-permute-start(bf16[512,256]{1,0:T(8,128)(2,1)} %get-tuple-element.31), channel_id=1, source_target_pairs={{0,6},{1,7},{2,0},{3,1},{4,2},{5,3},{6,4},{7,5},{8,14},{9,15},{10,... | collective-permute-start | bytes 786440 | tf_op jit(solution)/shard_map/ppermute | solution.py:436
  81.0 31.7 %collective-permute-start.16 = (bf16[8,128,256]{2,1,0:T(8,128)(2,1)S(1)}, bf16[8,128,256]{2,1,0:T(8,128)(2,1)S(1)}, u32[]{:S(2)}, u32[]{:S(2)}) collective-permute-start(bf16[8,128,256]{2,1,0:T(8,128)(2,1)S(1)} %get-tuple-element.37.refs_1_), channel_id=1, source_target_pairs={{0,24},{8,0},{16,8},{24,16},{32,56},{40,32},{48,40},{56,48},{64,88... | collective-permute-start | bytes 1572872 | tf_op jit(solution)/shard_map/ppermute | solution.py:433
  83.4 29.2 %collective-permute-start.20 = (bf16[8,128,256]{2,1,0:T(8,128)(2,1)S(1)}, bf16[8,128,256]{2,1,0:T(8,128)(2,1)S(1)}, u32[]{:S(2)}, u32[]{:S(2)}) collective-permute-start(bf16[8,128,256]{2,1,0:T(8,128)(2,1)S(1)} %get-tuple-element.36.refs_0_), channel_id=1, source_target_pairs={{0,8},{8,16},{16,24},{24,0},{32,40},{40,48},{48,56},{56,32},{64,72... | collective-permute-start | bytes 1572872 | tf_op jit(solution)/shard_map/ppermute | solution.py:434
  83.5 29.2 %collective-permute-start.17 = (bf16[8,128,256]{2,1,0:T(8,128)(2,1)S(1)}, bf16[8,128,256]{2,1,0:T(8,128)(2,1)}, u32[]{:S(2)}, u32[]{:S(2)}) collective-permute-start(bf16[8,128,256]{2,1,0:T(8,128)(2,1)S(1)} %collective-permute-done.15.refs_2_), channel_id=1, source_target_pairs={{0,24},{8,0},{16,8},{24,16},{32,56},{40,32},{48,40},{56,48},{64,88... | collective-permute-start | bytes 1572872 | tf_op jit(solution)/shard_map/ppermute | solution.py:438
  87.1 25.6 %collective-permute-start.19 = (bf16[8,128,256]{2,1,0:T(8,128)(2,1)S(1)}, bf16[8,128,256]{2,1,0:T(8,128)(2,1)}, u32[]{:S(2)}, u32[]{:S(2)}) collective-permute-start(bf16[8,128,256]{2,1,0:T(8,128)(2,1)S(1)} %collective-permute-done.18.refs_7_), channel_id=1, source_target_pairs={{0,8},{8,16},{16,24},{24,0},{32,40},{40,48},{48,56},{56,32},{64,72... | collective-permute-start | bytes 1572872 | tf_op jit(solution)/shard_map/ppermute | solution.py:439
  89.1 22.0 %all-to-all-start.1 = ((bf16[32,16,256]{2,1,0:T(8,128)(2,1)}), bf16[32,16,256]{2,1,0:T(8,128)(2,1)S(1)}, u32[]{:S(2)}, u32[]{:S(2)}) async-start(bf16[32,16,256]{2,1,0:T(8,128)(2,1)} %bitcast.12), calls=%async_computation.1 | async-start | bytes 524288 | tf_op jit(solution)/shard_map/all_to_all | solution.py:447
  118.8 6.9 %collective-permute-start.22 = (bf16[272,256]{1,0:T(8,128)(2,1)S(1)}, bf16[272,256]{1,0:T(8,128)(2,1)S(1)}, u32[]{:S(2)}, u32[]{:S(2)}) collective-permute-start(bf16[272,256]{1,0:T(8,128)(2,1)S(1)} %get-tuple-element.39), channel_id=1, source_target_pairs={{0,4},{1,5},{2,6},{3,7},{4,0},{5,1},{6,2},{7,3},{8,12},{9,13},{10,... | collective-permute-start | bytes 417800 | tf_op jit(solution)/shard_map/ppermute | solution.py:467
  121.7 7.0 %collective-permute-start.23 = (bf16[272,256]{1,0:T(8,128)(2,1)S(1)}, bf16[272,256]{1,0:T(8,128)(2,1)S(1)}, u32[]{:S(2)}, u32[]{:S(2)}) collective-permute-start(bf16[272,256]{1,0:T(8,128)(2,1)S(1)} %get-tuple-element.40), channel_id=1, source_target_pairs={{0,2},{1,3},{2,4},{3,5},{4,6},{5,7},{6,0},{7,1},{8,10},{9,11},{10,... | collective-permute-start | bytes 417800 | tf_op jit(solution)/shard_map/ppermute | solution.py:467
  122.2 6.8 %collective-permute-start.24 = (bf16[272,256]{1,0:T(8,128)(2,1)S(1)}, bf16[272,256]{1,0:T(8,128)(2,1)S(1)}, u32[]{:S(2)}, u32[]{:S(2)}) collective-permute-start(bf16[272,256]{1,0:T(8,128)(2,1)S(1)} %get-tuple-element.41), channel_id=1, source_target_pairs={{0,6},{1,7},{2,0},{3,1},{4,2},{5,3},{6,4},{7,5},{8,14},{9,15},{10,... | collective-permute-start | bytes 417800 | tf_op jit(solution)/shard_map/ppermute | solution.py:467
  (11 other events, 158.8 us)

commit v7 on v6

--- a/solution.py
+++ b/solution.py
@@ -401,8 +401,9 @@
         down.append(lax.ppermute(down[-1], "enc", shift_z(1)))
 
     dealt = lax.all_to_all(hidden, "enc", 0, 0, axis_index_groups=GROUPS_Z, tiled=True)
-    pieces = [dealt] + [lax.ppermute(dealt, "enc", shift_x(d)) for d in range(1, NX)]
-    pieces[1], up[-1], down[-1] = lax.optimization_barrier((pieces[1], up[-1], down[-1]))
+    by_x = {d: lax.ppermute(dealt, "enc", shift_x(d)) for d in FAR_FIRST}
+    pieces = [dealt] + [by_x[d] for d in range(1, NX)]
+    pieces[2], up[-1], down[-1] = lax.optimization_barrier((pieces[2], up[-1], down[-1]))
     far = [
         lax.ppermute(up[-1][:middle], "enc", shift_z(-1)),
         lax.ppermute(down[-1][middle:], "enc", shift_z(1)),

time: 130 us -> 131 us (level)
  starting transfers between devices: 53.1 us -> 57 us
  waiting for transfers between devices: 49.5 us -> 46.7 us
    ppermute x2, starting transfers between devices: 3.76 us -> 5.96 us  [body(): after = [lax.ppermute(part, 'enc', shift_x(-1)) for part in kv_own]]
  transfers between devices with their start and end apart: 27 -> 27, of which waited for: 17 -> 15; matrix products, arithmetic and copies ran while one was open for 3% -> 3% of each run, Pallas kernels for 10% -> 10%
where the time goes in v7:
time: 131 us
  starting transfers between devices  57 us (44%)
  waiting for transfers between devices  46.7 us (36%)
  Pallas kernels  20.5 us (16%)
  other arithmetic  3.84 us (3%)
  local copies, waits for them, and re-layouts  2 us (2%)
    all_to_all x1, waiting for transfers between devices, body(): moved = lax.all_to_all(merged, 'enc', 0, 0, tiled=True)  13.3 us
    all_to_all x1, starting transfers between devices, body(): moved = lax.all_to_all(merged, 'enc', 0, 0, tiled=True)  8.3 us
    ppermute x2, waiting for transfers between devices, body(): up.append(lax.ppermute(up[-1], 'enc', shift_z(-1)))  7.94 us
    ppermute x2, starting transfers between devices, body(): got = lax.ppermute(away, 'tp', SWAP_CORE)  7.6 us
    pallas_call x1, Pallas kernels, hidden_rows(): pl.pallas_call(functools.partial(hidden_kernel, slots), in_specs=[IN_HBM]...  6.66 us
    ppermute x1, starting transfers between devices, body(): up = [block, lax.ppermute(block, 'enc', shift_z(-1))]  6.48 us
    ppermute x2, starting transfers between devices, body(): after = [lax.ppermute(part, 'enc', shift_x(-1)) for part in kv_own]  5.96 us
    ppermute x3, starting transfers between devices, body(): others = [lax.ppermute(parts[d], 'tp', shift_y(d)) for d in FAR_LAST]  5.59 us
  transfers between devices with their start and end apart: 27, of which 15 were waited for; matrix products, arithmetic and copies ran while one was open for 3% of the time, Pallas kernels for 10%

profile of v7, /device:TPU:1, one launch (start us, length us, event | category | flops | bytes accessed | tf_op | source)
XLA Modules:
  0.0 130.9 jit_solution(2279115975751456486)
XLA Ops:
  2.6 6.5 %collective-permute-start = (bf16[896,256]{1,0:T(8,128)(2,1)S(1)}, bf16[896,256]{1,0:T(8,128)(2,1)S(1)}, u32[]{:S(2)}, u32[]{:S(2)}) collective-permute-start(bf16[896,256]{1,0:T(8,128)(2,1)S(1)} %slice_dynamic-update-slice_fusion.refs_0_), channel_id=1, source_target_pairs={{0,224},{8,232},{16,240},{24,248},{32,0},{40,8},{48,16},{56,24},{6... | collective-permute-start | bytes 1376264 | tf_op jit(solution)/shard_map/ppermute | solution.py:395
  9.1 6.7 %shard_map.113 = bf16[256,640]{1,0:T(8,128)(2,1)} custom-call(bf16[256,5120]{1,0:T(8,128)(2,1)} %bitcast.11, f32[1280]{0:T(1024)} %gain_ref.1, f32[1280]{0:T(1024)} %bias_ref.1, bf16[5120,640]{1,0:T(8,128)(2,1)} %weight_ref.1), custom_call_target="tpu_custom_call" | custom-call | tf_op jit(solution)/shard_map/pallas_call | solution.py:107
  15.8 2.5 %collective-permute-done.refs_1_ = bf16[896,256]{1,0:T(8,128)(2,1)S(1)} collective-permute-done((bf16[896,256]{1,0:T(8,128)(2,1)S(1)}, bf16[896,256]{1,0:T(8,128)(2,1)S(1)}, u32[]{:S(2)}, u32[]{:S(2)}) %collective-permute-start) | collective-permute-done | bytes 458784 | tf_op jit(solution)/shard_map/ppermute | solution.py:395
  18.3 3.1 %collective-permute-done.1.refs_8_ = bf16[896,256]{1,0:T(8,128)(2,1)S(1)} collective-permute-done((bf16[896,256]{1,0:T(8,128)(2,1)S(1)}, bf16[896,256]{1,0:T(8,128)(2,1)S(1)}, u32[]{:S(2)}, u32[]{:S(2)}) %collective-permute-start.1) | collective-permute-done | bytes 458784 | tf_op jit(solution)/shard_map/ppermute | solution.py:396
  22.9 3.4 %all-to-all-start = ((bf16[8,32,640]{2,1,0:T(8,128)(2,1)}), bf16[8,32,640]{2,1,0:T(8,128)(2,1)S(1)}, u32[]{:S(2)}, u32[]{:S(2)}) async-start(bf16[8,32,640]{2,1,0:T(8,128)(2,1)} %bitcast.2), calls=%async_computation | async-start | bytes 655360 | tf_op jit(solution)/shard_map/all_to_all | solution.py:403
  26.3 5.3 %collective-permute-done.4.refs_2_ = bf16[896,256]{1,0:T(8,128)(2,1)S(1)} collective-permute-done((bf16[896,256]{1,0:T(8,128)(2,1)S(1)}, bf16[896,256]{1,0:T(8,128)(2,1)S(1)}, u32[]{:S(2)}, u32[]{:S(2)}) %collective-permute-start.4) | collective-permute-done | bytes 458784 | tf_op jit(solution)/shard_map/ppermute | solution.py:400
  34.4 3.9 %all-to-all-done = bf16[8,32,640]{2,1,0:T(8,128)(2,1)S(1)} async-done(((bf16[8,32,640]{2,1,0:T(8,128)(2,1)}), bf16[8,32,640]{2,1,0:T(8,128)(2,1)S(1)}, u32[]{:S(2)}, u32[]{:S(2)}) %all-to-all-start) | async-done | bytes 327712 | tf_op jit(solution)/shard_map/all_to_all | solution.py:403
  38.3 2.7 %collective-permute-start.3 = (bf16[256,640]{1,0:T(8,128)(2,1)S(1)}, bf16[256,640]{1,0:T(8,128)(2,1)S(1)}, u32[]{:S(2)}, u32[]{:S(2)}) collective-permute-start(bf16[256,640]{1,0:T(8,128)(2,1)S(1)} %bitcast.7), channel_id=1, source_target_pairs={{0,16},{8,24},{16,0},{24,8},{32,48},{40,56},{48,32},{56,40},{64,80... | collective-permute-start | bytes 983048 | tf_op jit(solution)/shard_map/ppermute | solution.py:404
  41.6 2.4 %collective-permute-start.8 = (bf16[256,640]{1,0:T(8,128)(2,1)S(1)}, bf16[256,640]{1,0:T(8,128)(2,1)S(1)}, u32[]{:S(2)}, u32[]{:S(2)}) collective-permute-start(bf16[256,640]{1,0:T(8,128)(2,1)S(1)} %bitcast.9), channel_id=1, source_target_pairs={{0,24},{8,0},{16,8},{24,16},{32,56},{40,32},{48,40},{56,48},{64,88... | collective-permute-start | bytes 983048 | tf_op jit(solution)/shard_map/ppermute | solution.py:404
  45.8 2.6 %collective-permute-done.5.refs_3_ = bf16[896,256]{1,0:T(8,128)(2,1)S(1)} collective-permute-done((bf16[896,256]{1,0:T(8,128)(2,1)S(1)}, bf16[896,256]{1,0:T(8,128)(2,1)S(1)}, u32[]{:S(2)}, u32[]{:S(2)}) %collective-permute-start.5) | collective-permute-done | bytes 458784 | tf_op jit(solution)/shard_map/ppermute | solution.py:400
  54.4 2.8 %collective-permute-done.10.refs_5_ = bf16[448,256]{1,0:T(8,128)(2,1)} collective-permute-done((bf16[448,256]{1,0:T(8,128)(2,1)}, bf16[448,256]{1,0:T(8,128)(2,1)}, u32[]{:S(2)}, u32[]{:S(2)}) %collective-permute-start.10) | collective-permute-done | bytes 229408 | tf_op jit(solution)/shard_map/ppermute | solution.py:409
  57.2 4.6 %shard_map.115 = (bf16[4,512,256]{2,1,0:T(8,128)(2,1)S(1)}, bf16[8,128,256]{2,1,0:T(8,128)(2,1)S(1)}, bf16[8,128,256]{2,1,0:T(8,128)(2,1)S(1)}, bf16[4,640,256]{2,1,0:T(8,128)(2,1)S(1)}) custom-call(s32[9]{0:T(128)S(1)} %pad_add_fusion.1.plan_ref, bf16[512,640]{1,0:T(8,128)(2,1)S(1)} %shard_map.114.live_ref, bf16[896,256]{1,0:T(8,128)(2,1)} %copy-done, ...), custom_call_target="tpu_custom_call" | custom-call | tf_op jit(solution)/shard_map/pallas_call | solution.py:207
  61.8 5.5 %collective-permute-start.11 = (bf16[4,512,256]{2,1,0:T(8,128)(2,1)S(1)}, bf16[4,512,256]{2,1,0:T(8,128)(2,1)S(1)}, u32[]{:S(2)}, u32[]{:S(2)}) collective-permute-start(bf16[4,512,256]{2,1,0:T(8,128)(2,1)S(1)} %get-tuple-element.28), channel_id=1, source_target_pairs={{0,1},{1,0},{2,3},{3,2},{4,5},{5,4},{6,7},{7,6},{8,9},{9,8},{10,11... | collective-permute-start | bytes 3145736 | tf_op jit(solution)/shard_map/ppermute | solution.py:433
  67.3 2.4 %collective-permute-start.15 = (bf16[8,128,256]{2,1,0:T(8,128)(2,1)S(1)}, bf16[8,128,256]{2,1,0:T(8,128)(2,1)S(1)}, u32[]{:S(2)}, u32[]{:S(2)}) collective-permute-start(bf16[8,128,256]{2,1,0:T(8,128)(2,1)S(1)} %get-tuple-element.36.refs_0_), channel_id=1, source_target_pairs={{0,24},{8,0},{16,8},{24,16},{32,56},{40,32},{48,40},{56,48},{64,88... | collective-permute-start | bytes 1572872 | tf_op jit(solution)/shard_map/ppermute | solution.py:434
  71.6 2.9 %collective-permute-start.14 = (bf16[512,256]{1,0:T(8,128)(2,1)}, bf16[512,256]{1,0:T(8,128)(2,1)}, u32[]{:S(2)}, u32[]{:S(2)}) collective-permute-start(bf16[512,256]{1,0:T(8,128)(2,1)} %get-tuple-element.33), channel_id=1, source_target_pairs={{0,4},{1,5},{2,6},{3,7},{4,0},{5,1},{6,2},{7,3},{8,12},{9,13},{10,... | collective-permute-start | bytes 786440 | tf_op jit(solution)/shard_map/ppermute | solution.py:437
  74.9 2.3 %collective-permute-start.12 = (bf16[512,256]{1,0:T(8,128)(2,1)}, bf16[512,256]{1,0:T(8,128)(2,1)}, u32[]{:S(2)}, u32[]{:S(2)}) collective-permute-start(bf16[512,256]{1,0:T(8,128)(2,1)} %get-tuple-element.31), channel_id=1, source_target_pairs={{0,6},{1,7},{2,0},{3,1},{4,2},{5,3},{6,4},{7,5},{8,14},{9,15},{10,... | collective-permute-start | bytes 786440 | tf_op jit(solution)/shard_map/ppermute | solution.py:437
  77.3 3.8 %collective-permute-done.15.refs_2_ = bf16[8,128,256]{2,1,0:T(8,128)(2,1)S(1)} collective-permute-done((bf16[8,128,256]{2,1,0:T(8,128)(2,1)S(1)}, bf16[8,128,256]{2,1,0:T(8,128)(2,1)S(1)}, u32[]{:S(2)}, u32[]{:S(2)}) %collective-permute-start.15) | collective-permute-done | bytes 524320 | tf_op jit(solution)/shard_map/ppermute | solution.py:434
  81.1 3.5 %collective-permute-start.16 = (bf16[8,128,256]{2,1,0:T(8,128)(2,1)S(1)}, bf16[8,128,256]{2,1,0:T(8,128)(2,1)S(1)}, u32[]{:S(2)}, u32[]{:S(2)}) collective-permute-start(bf16[8,128,256]{2,1,0:T(8,128)(2,1)S(1)} %get-tuple-element.37.refs_1_), channel_id=1, source_target_pairs={{0,24},{8,0},{16,8},{24,16},{32,56},{40,32},{48,40},{56,48},{64,88... | collective-permute-start | bytes 1572872 | tf_op jit(solution)/shard_map/ppermute | solution.py:434
  84.6 2.7 %collective-permute-start.17 = (bf16[8,128,256]{2,1,0:T(8,128)(2,1)S(1)}, bf16[8,128,256]{2,1,0:T(8,128)(2,1)}, u32[]{:S(2)}, u32[]{:S(2)}) collective-permute-start(bf16[8,128,256]{2,1,0:T(8,128)(2,1)S(1)} %collective-permute-done.15.refs_2_), channel_id=1, source_target_pairs={{0,24},{8,0},{16,8},{24,16},{32,56},{40,32},{48,40},{56,48},{64,88... | collective-permute-start | bytes 1572872 | tf_op jit(solution)/shard_map/ppermute | solution.py:439
  90.3 8.3 %all-to-all-start.1 = ((bf16[32,16,256]{2,1,0:T(8,128)(2,1)}), bf16[32,16,256]{2,1,0:T(8,128)(2,1)S(1)}, u32[]{:S(2)}, u32[]{:S(2)}) async-start(bf16[32,16,256]{2,1,0:T(8,128)(2,1)} %bitcast.12), calls=%async_computation.1 | async-start | bytes 524288 | tf_op jit(solution)/shard_map/all_to_all | solution.py:448
  99.0 13.3 %all-to-all-done.1.moved_ref = bf16[32,16,256]{2,1,0:T(8,128)(2,1)S(1)} async-done(((bf16[32,16,256]{2,1,0:T(8,128)(2,1)}), bf16[32,16,256]{2,1,0:T(8,128)(2,1)S(1)}, u32[]{:S(2)}, u32[]{:S(2)}) %all-to-all-start.1) | async-done | bytes 262176 | tf_op jit(solution)/shard_map/all_to_all | solution.py:448
  119.9 2.9 %collective-permute-start.22 = (bf16[272,256]{1,0:T(8,128)(2,1)S(1)}, bf16[272,256]{1,0:T(8,128)(2,1)S(1)}, u32[]{:S(2)}, u32[]{:S(2)}) collective-permute-start(bf16[272,256]{1,0:T(8,128)(2,1)S(1)} %get-tuple-element.39), channel_id=1, source_target_pairs={{0,4},{1,5},{2,6},{3,7},{4,0},{5,1},{6,2},{7,3},{8,12},{9,13},{10,... | collective-permute-start | bytes 417800 | tf_op jit(solution)/shard_map/ppermute | solution.py:468
  123.3 2.2 %collective-permute-start.24 = (bf16[272,256]{1,0:T(8,128)(2,1)S(1)}, bf16[272,256]{1,0:T(8,128)(2,1)S(1)}, u32[]{:S(2)}, u32[]{:S(2)}) collective-permute-start(bf16[272,256]{1,0:T(8,128)(2,1)S(1)} %get-tuple-element.41), channel_id=1, source_target_pairs={{0,6},{1,7},{2,0},{3,1},{4,2},{5,3},{6,4},{7,5},{8,14},{9,15},{10,... | collective-permute-start | bytes 417800 | tf_op jit(solution)/shard_map/ppermute | solution.py:468
  126.8 3.1 %collective-permute-done.23.c = bf16[272,256]{1,0:T(8,128)(2,1)S(1)} collective-permute-done((bf16[272,256]{1,0:T(8,128)(2,1)S(1)}, bf16[272,256]{1,0:T(8,128)(2,1)S(1)}, u32[]{:S(2)}, u32[]{:S(2)}) %collective-permute-start.23) | collective-permute-done | bytes 139296 | tf_op jit(solution)/shard_map/ppermute | solution.py:468
  (80 shorter events, 30.7 us)
Async XLA Ops:
  2.6 15.7 %collective-permute-start = (bf16[896,256]{1,0:T(8,128)(2,1)S(1)}, bf16[896,256]{1,0:T(8,128)(2,1)S(1)}, u32[]{:S(2)}, u32[]{:S(2)}) collective-permute-start(bf16[896,256]{1,0:T(8,128)(2,1)S(1)} %slice_dynamic-update-slice_fusion.refs_0_), channel_id=1, source_target_pairs={{0,224},{8,232},{16,240},{24,248},{32,0},{40,8},{48,16},{56,24},{6... | collective-permute-start | bytes 1376264 | tf_op jit(solution)/shard_map/ppermute | solution.py:395
  9.1 12.3 %collective-permute-start.1 = (bf16[896,256]{1,0:T(8,128)(2,1)S(1)}, bf16[896,256]{1,0:T(8,128)(2,1)S(1)}, u32[]{:S(2)}, u32[]{:S(2)}) collective-permute-start(bf16[896,256]{1,0:T(8,128)(2,1)S(1)} %slice_dynamic-update-slice_fusion.refs_0_), channel_id=1, source_target_pairs={{0,32},{8,40},{16,48},{24,56},{32,64},{40,72},{48,80},{56,88},{64,... | collective-permute-start | bytes 1376264 | tf_op jit(solution)/shard_map/ppermute | solution.py:396
  21.4 10.3 %collective-permute-start.4 = (bf16[896,256]{1,0:T(8,128)(2,1)S(1)}, bf16[896,256]{1,0:T(8,128)(2,1)S(1)}, u32[]{:S(2)}, u32[]{:S(2)}) collective-permute-start(bf16[896,256]{1,0:T(8,128)(2,1)S(1)} %collective-permute-done.refs_1_), channel_id=1, source_target_pairs={{0,224},{8,232},{16,240},{24,248},{32,0},{40,8},{48,16},{56,24},{6... | collective-permute-start | bytes 1376264 | tf_op jit(solution)/shard_map/ppermute | solution.py:400
  21.8 12.6 %collective-permute-start.6 = (bf16[896,256]{1,0:T(8,128)(2,1)S(1)}, bf16[896,256]{1,0:T(8,128)(2,1)}, u32[]{:S(2)}, u32[]{:S(2)}) collective-permute-start(bf16[896,256]{1,0:T(8,128)(2,1)S(1)} %collective-permute-done.1.refs_8_), channel_id=1, source_target_pairs={{0,32},{8,40},{16,48},{24,56},{32,64},{40,72},{48,80},{56,88},{64,... | collective-permute-start | bytes 1376264 | tf_op jit(solution)/shard_map/ppermute | solution.py:401
  22.9 15.4 %all-to-all-start = ((bf16[8,32,640]{2,1,0:T(8,128)(2,1)}), bf16[8,32,640]{2,1,0:T(8,128)(2,1)S(1)}, u32[]{:S(2)}, u32[]{:S(2)}) async-start(bf16[8,32,640]{2,1,0:T(8,128)(2,1)} %bitcast.2), calls=%async_computation | async-start | bytes 655360 | tf_op jit(solution)/shard_map/all_to_all | solution.py:403
  31.7 16.7 %collective-permute-start.5 = (bf16[896,256]{1,0:T(8,128)(2,1)S(1)}, bf16[896,256]{1,0:T(8,128)(2,1)S(1)}, u32[]{:S(2)}, u32[]{:S(2)}) collective-permute-start(bf16[896,256]{1,0:T(8,128)(2,1)S(1)} %collective-permute-done.4.refs_2_), channel_id=1, source_target_pairs={{0,224},{8,232},{16,240},{24,248},{32,0},{40,8},{48,16},{56,24},{6... | collective-permute-start | bytes 1376264 | tf_op jit(solution)/shard_map/ppermute | solution.py:400
  34.4 14.7 %collective-permute-start.7 = (bf16[896,256]{1,0:T(8,128)(2,1)}, bf16[896,256]{1,0:T(8,128)(2,1)S(1)}, u32[]{:S(2)}, u32[]{:S(2)}) collective-permute-start(bf16[896,256]{1,0:T(8,128)(2,1)} %collective-permute-done.6.refs_7_), channel_id=1, source_target_pairs={{0,32},{8,40},{16,48},{24,56},{32,64},{40,72},{48,80},{56,88},{64,... | collective-permute-start | bytes 1376264 | tf_op jit(solution)/shard_map/ppermute | solution.py:401
  38.3 7.5 %collective-permute-start.3 = (bf16[256,640]{1,0:T(8,128)(2,1)S(1)}, bf16[256,640]{1,0:T(8,128)(2,1)S(1)}, u32[]{:S(2)}, u32[]{:S(2)}) collective-permute-start(bf16[256,640]{1,0:T(8,128)(2,1)S(1)} %bitcast.7), channel_id=1, source_target_pairs={{0,16},{8,24},{16,0},{24,8},{32,48},{40,56},{48,32},{56,40},{64,80... | collective-permute-start | bytes 983048 | tf_op jit(solution)/shard_map/ppermute | solution.py:404
  41.2 10.5 %collective-permute-start.2 = (bf16[256,640]{1,0:T(8,128)(2,1)S(1)}, bf16[256,640]{1,0:T(8,128)(2,1)S(1)}, u32[]{:S(2)}, u32[]{:S(2)}) collective-permute-start(bf16[256,640]{1,0:T(8,128)(2,1)S(1)} %bitcast.8), channel_id=1, source_target_pairs={{0,8},{8,16},{16,24},{24,0},{32,40},{40,48},{48,56},{56,32},{64,72... | collective-permute-start | bytes 983048 | tf_op jit(solution)/shard_map/ppermute | solution.py:404
  41.6 10.1 %collective-permute-start.8 = (bf16[256,640]{1,0:T(8,128)(2,1)S(1)}, bf16[256,640]{1,0:T(8,128)(2,1)S(1)}, u32[]{:S(2)}, u32[]{:S(2)}) collective-permute-start(bf16[256,640]{1,0:T(8,128)(2,1)S(1)} %bitcast.9), channel_id=1, source_target_pairs={{0,24},{8,0},{16,8},{24,16},{32,56},{40,32},{48,40},{56,48},{64,88... | collective-permute-start | bytes 983048 | tf_op jit(solution)/shard_map/ppermute | solution.py:404
  61.8 8.0 %collective-permute-start.11 = (bf16[4,512,256]{2,1,0:T(8,128)(2,1)S(1)}, bf16[4,512,256]{2,1,0:T(8,128)(2,1)S(1)}, u32[]{:S(2)}, u32[]{:S(2)}) collective-permute-start(bf16[4,512,256]{2,1,0:T(8,128)(2,1)S(1)} %get-tuple-element.28), channel_id=1, source_target_pairs={{0,1},{1,0},{2,3},{3,2},{4,5},{5,4},{6,7},{7,6},{8,9},{9,8},{10,11... | collective-permute-start | bytes 3145736 | tf_op jit(solution)/shard_map/ppermute | solution.py:433
  67.3 13.7 %collective-permute-start.15 = (bf16[8,128,256]{2,1,0:T(8,128)(2,1)S(1)}, bf16[8,128,256]{2,1,0:T(8,128)(2,1)S(1)}, u32[]{:S(2)}, u32[]{:S(2)}) collective-permute-start(bf16[8,128,256]{2,1,0:T(8,128)(2,1)S(1)} %get-tuple-element.36.refs_0_), channel_id=1, source_target_pairs={{0,24},{8,0},{16,8},{24,16},{32,56},{40,32},{48,40},{56,48},{64,88... | collective-permute-start | bytes 1572872 | tf_op jit(solution)/shard_map/ppermute | solution.py:434
  69.8 14.8 %collective-permute-start.18 = (bf16[8,128,256]{2,1,0:T(8,128)(2,1)S(1)}, bf16[8,128,256]{2,1,0:T(8,128)(2,1)S(1)}, u32[]{:S(2)}, u32[]{:S(2)}) collective-permute-start(bf16[8,128,256]{2,1,0:T(8,128)(2,1)S(1)} %get-tuple-element.37.refs_1_), channel_id=1, source_target_pairs={{0,8},{8,16},{16,24},{24,0},{32,40},{40,48},{48,56},{56,32},{64,72... | collective-permute-start | bytes 1572872 | tf_op jit(solution)/shard_map/ppermute | solution.py:435
  71.6 13.0 %collective-permute-start.14 = (bf16[512,256]{1,0:T(8,128)(2,1)}, bf16[512,256]{1,0:T(8,128)(2,1)}, u32[]{:S(2)}, u32[]{:S(2)}) collective-permute-start(bf16[512,256]{1,0:T(8,128)(2,1)} %get-tuple-element.33), channel_id=1, source_target_pairs={{0,4},{1,5},{2,6},{3,7},{4,0},{5,1},{6,2},{7,3},{8,12},{9,13},{10,... | collective-permute-start | bytes 786440 | tf_op jit(solution)/shard_map/ppermute | solution.py:437
  74.5 12.8 %collective-permute-start.13 = (bf16[512,256]{1,0:T(8,128)(2,1)}, bf16[512,256]{1,0:T(8,128)(2,1)}, u32[]{:S(2)}, u32[]{:S(2)}) collective-permute-start(bf16[512,256]{1,0:T(8,128)(2,1)} %get-tuple-element.32), channel_id=1, source_target_pairs={{0,2},{1,3},{2,4},{3,5},{4,6},{5,7},{6,0},{7,1},{8,10},{9,11},{10,... | collective-permute-start | bytes 786440 | tf_op jit(solution)/shard_map/ppermute | solution.py:437
  74.9 13.5 %collective-permute-start.12 = (bf16[512,256]{1,0:T(8,128)(2,1)}, bf16[512,256]{1,0:T(8,128)(2,1)}, u32[]{:S(2)}, u32[]{:S(2)}) collective-permute-start(bf16[512,256]{1,0:T(8,128)(2,1)} %get-tuple-element.31), channel_id=1, source_target_pairs={{0,6},{1,7},{2,0},{3,1},{4,2},{5,3},{6,4},{7,5},{8,14},{9,15},{10,... | collective-permute-start | bytes 786440 | tf_op jit(solution)/shard_map/ppermute | solution.py:437
  81.1 32.7 %collective-permute-start.16 = (bf16[8,128,256]{2,1,0:T(8,128)(2,1)S(1)}, bf16[8,128,256]{2,1,0:T(8,128)(2,1)S(1)}, u32[]{:S(2)}, u32[]{:S(2)}) collective-permute-start(bf16[8,128,256]{2,1,0:T(8,128)(2,1)S(1)} %get-tuple-element.37.refs_1_), channel_id=1, source_target_pairs={{0,24},{8,0},{16,8},{24,16},{32,56},{40,32},{48,40},{56,48},{64,88... | collective-permute-start | bytes 1572872 | tf_op jit(solution)/shard_map/ppermute | solution.py:434
  84.6 29.2 %collective-permute-start.20 = (bf16[8,128,256]{2,1,0:T(8,128)(2,1)S(1)}, bf16[8,128,256]{2,1,0:T(8,128)(2,1)S(1)}, u32[]{:S(2)}, u32[]{:S(2)}) collective-permute-start(bf16[8,128,256]{2,1,0:T(8,128)(2,1)S(1)} %get-tuple-element.36.refs_0_), channel_id=1, source_target_pairs={{0,8},{8,16},{16,24},{24,0},{32,40},{40,48},{48,56},{56,32},{64,72... | collective-permute-start | bytes 1572872 | tf_op jit(solution)/shard_map/ppermute | solution.py:435
  84.6 29.2 %collective-permute-start.17 = (bf16[8,128,256]{2,1,0:T(8,128)(2,1)S(1)}, bf16[8,128,256]{2,1,0:T(8,128)(2,1)}, u32[]{:S(2)}, u32[]{:S(2)}) collective-permute-start(bf16[8,128,256]{2,1,0:T(8,128)(2,1)S(1)} %collective-permute-done.15.refs_2_), channel_id=1, source_target_pairs={{0,24},{8,0},{16,8},{24,16},{32,56},{40,32},{48,40},{56,48},{64,88... | collective-permute-start | bytes 1572872 | tf_op jit(solution)/shard_map/ppermute | solution.py:439
  87.3 26.6 %collective-permute-start.19 = (bf16[8,128,256]{2,1,0:T(8,128)(2,1)S(1)}, bf16[8,128,256]{2,1,0:T(8,128)(2,1)}, u32[]{:S(2)}, u32[]{:S(2)}) collective-permute-start(bf16[8,128,256]{2,1,0:T(8,128)(2,1)S(1)} %collective-permute-done.18.refs_7_), channel_id=1, source_target_pairs={{0,8},{8,16},{16,24},{24,0},{32,40},{40,48},{48,56},{56,32},{64,72... | collective-permute-start | bytes 1572872 | tf_op jit(solution)/shard_map/ppermute | solution.py:440
  90.3 21.9 %all-to-all-start.1 = ((bf16[32,16,256]{2,1,0:T(8,128)(2,1)}), bf16[32,16,256]{2,1,0:T(8,128)(2,1)S(1)}, u32[]{:S(2)}, u32[]{:S(2)}) async-start(bf16[32,16,256]{2,1,0:T(8,128)(2,1)} %bitcast.12), calls=%async_computation.1 | async-start | bytes 524288 | tf_op jit(solution)/shard_map/all_to_all | solution.py:448
  119.9 6.9 %collective-permute-start.22 = (bf16[272,256]{1,0:T(8,128)(2,1)S(1)}, bf16[272,256]{1,0:T(8,128)(2,1)S(1)}, u32[]{:S(2)}, u32[]{:S(2)}) collective-permute-start(bf16[272,256]{1,0:T(8,128)(2,1)S(1)} %get-tuple-element.39), channel_id=1, source_target_pairs={{0,4},{1,5},{2,6},{3,7},{4,0},{5,1},{6,2},{7,3},{8,12},{9,13},{10,... | collective-permute-start | bytes 417800 | tf_op jit(solution)/shard_map/ppermute | solution.py:468
  122.8 7.1 %collective-permute-start.23 = (bf16[272,256]{1,0:T(8,128)(2,1)S(1)}, bf16[272,256]{1,0:T(8,128)(2,1)S(1)}, u32[]{:S(2)}, u32[]{:S(2)}) collective-permute-start(bf16[272,256]{1,0:T(8,128)(2,1)S(1)} %get-tuple-element.40), channel_id=1, source_target_pairs={{0,2},{1,3},{2,4},{3,5},{4,6},{5,7},{6,0},{7,1},{8,10},{9,11},{10,... | collective-permute-start | bytes 417800 | tf_op jit(solution)/shard_map/ppermute | solution.py:468
  123.3 6.8 %collective-permute-start.24 = (bf16[272,256]{1,0:T(8,128)(2,1)S(1)}, bf16[272,256]{1,0:T(8,128)(2,1)S(1)}, u32[]{:S(2)}, u32[]{:S(2)}) collective-permute-start(bf16[272,256]{1,0:T(8,128)(2,1)S(1)} %get-tuple-element.41), channel_id=1, source_target_pairs={{0,6},{1,7},{2,0},{3,1},{4,2},{5,3},{6,4},{7,5},{8,14},{9,15},{10,... | collective-permute-start | bytes 417800 | tf_op jit(solution)/shard_map/ppermute | solution.py:468
  (11 other events, 162.0 us)
